TPU v7x, 32 devices: a whole 2x2x4 slice. The times are simulated.
32 devices in a mesh: section: 2 (over y), seq: 4 (over x, core), fsdp: 4 (over z).
Axes of the slice: x: 2, y: 2, z: 4, core: 2. Of those that a mesh axis runs over, the one named last changes fastest.
Arguments:
- section_ends: bfloat16 [2, 2, 4, 1024, 1536], P('section', None, 'fsdp', 'seq'), may hold values from -6 to 6
- norm_gain: bfloat16 [2, 1536], P('section', 'fsdp'), may hold values from 0.5 to 1.5
- in_weight: bfloat16 [2, 1536, 6448], P('section', 'fsdp'), may hold values from -0.15625 to 0.15625
- conv_weight: bfloat16 [2, 4, 3328], P('section', None, 'fsdp'), may hold values from -3 to 3
- conv_bias: bfloat16 [2, 3328], P('section', 'fsdp'), may hold values from -3 to 3
- step_bias: bfloat16 [2, 48], P('section', 'fsdp'), may hold values from -5 to -2
- log_decay: bfloat16 [2, 48], P('section', 'fsdp'), may hold values from -8 to 0
- skip_gain: bfloat16 [2, 48], P('section', 'fsdp'), may hold values from 0.5 to 2
- gate_gain: bfloat16 [2, 3072], P('section', 'fsdp'), may hold values from 0.5 to 1.5
- out_weight: bfloat16 [2, 3072, 1536], P('section', 'fsdp'), may hold values from -0.109375 to 0.109375
Outputs:
- section_results: float32 [2, 2, 4, 1024, 1536], P('section', None, 'fsdp', 'seq')
- grad_norm_gain: float32 [2, 1536], P('section', 'fsdp')
- grad_in_weight: float32 [2, 1536, 6448], P('section', 'fsdp')
- grad_conv_weight: float32 [2, 4, 3328], P('section', None, 'fsdp')
- grad_conv_bias: float32 [2, 3328], P('section', 'fsdp')
- grad_step_bias: float32 [2, 48], P('section', 'fsdp')
- grad_log_decay: float32 [2, 48], P('section', 'fsdp')
- grad_skip_gain: float32 [2, 48], P('section', 'fsdp')
- grad_gate_gain: float32 [2, 3072], P('section', 'fsdp')
- grad_out_weight: float32 [2, 3072, 1536], P('section', 'fsdp')
All inputs are finite; a program needn't handle non-finite values.
Results may differ from a plain program's by a relative error of at most 0.038.
Values may be sent and summed in bfloat16 or wider, within the bound.
A program may use at most 384 MiB of HBM per device.

v0:
```python
import jax
import jax.numpy as jnp
from jax import lax
from jax.sharding import PartitionSpec as P

SPAN = 256


epsilon = 1e-05
highest = lax.Precision.HIGHEST


def shifted(value, axis, steps):
    count = lax.axis_size(axis)
    leading, last = (max(0, -steps), min(count, count - steps))
    return lax.ppermute(value, axis, [(source, source + steps) for source in range(leading, last)])


def rms_scale(value):
    return value * lax.rsqrt(jnp.mean(value * value, axis=-1, keepdims=True) + epsilon)


def pre_norm(hidden, norm_gain):
    return rms_scale(hidden) * norm_gain


def post_norm(result, gate_part, gate_gain):
    return rms_scale(result * jax.nn.silu(gate_part)) * gate_gain


def conv_part(padded, conv_weight, conv_bias):
    length = padded.shape[0] - (conv_weight.shape[0] - 1)
    running = conv_bias + conv_weight[0] * padded[0:length]
    for offset in range(1, conv_weight.shape[0]):
        running = running + conv_weight[offset] * padded[offset : offset + length]
    return jax.nn.silu(running)


def decays(scores, b_rows, dt_raw, step_bias, log_decay):
    blocks, block_len = (scores.shape[0], scores.shape[1])
    dt_value = jax.nn.softplus(dt_raw + step_bias)
    log_rate = -dt_value * jnp.exp(log_decay)
    dt_value = jnp.transpose(dt_value.reshape(blocks, block_len, -1), (0, 2, 1))
    log_rate = jnp.transpose(log_rate.reshape(blocks, block_len, -1), (0, 2, 1))
    triangle = jnp.tril(jnp.ones((block_len, block_len), jnp.float32))
    cumulative = jnp.einsum("chj,ij->chi", log_rate, triangle, precision=highest)
    inside = triangle > 0.5
    spread = cumulative[:, :, :, None] - cumulative[:, :, None, :]
    fading_inner = jnp.where(inside, jnp.exp(jnp.where(inside, spread, 0.0)), 0.0)
    mixing = scores[:, None, :, :] * fading_inner * dt_value[:, :, None, :]
    tail = jnp.exp(cumulative[:, :, -1:] - cumulative) * dt_value
    weighted = b_rows[:, None, :, :] * tail[:, :, :, None]
    return (mixing, weighted, jnp.exp(cumulative), jnp.exp(cumulative[:, :, -1]))


def carry_states(local_part, fading):

    def advance(carried, inputs):
        block_part, fade_now = inputs
        return (fade_now[:, None, None] * carried + block_part, carried)

    initial = jnp.zeros(local_part.shape[1:], local_part.dtype)
    finished, entering = lax.scan(advance, initial, (local_part, fading))
    return entering


def split_rows(heads_x, shared, heads_dt):
    length = heads_x.shape[0]
    blocks = length // SPAN
    heads_here = heads_dt.shape[1]
    state_size = shared.shape[1] // 2
    head_rows = heads_x.reshape(blocks, SPAN, heads_here, -1)
    b_rows = shared[:, :state_size].reshape(blocks, SPAN, state_size)
    c_rows = shared[:, state_size:].reshape(blocks, SPAN, state_size)
    return (head_rows, b_rows, c_rows)


def mixer_forward(heads_x, shared, heads_dt, bias_here, decay_here, skip_here):
    head_rows, b_rows, c_rows = split_rows(heads_x, shared, heads_dt)
    scores = jnp.einsum("cin,cjn->cij", c_rows, b_rows, preferred_element_type=jnp.float32)
    mixing, weighted, growth, fading = decays(
        scores, b_rows.astype(jnp.float32), heads_dt.astype(jnp.float32), bias_here, decay_here
    )
    mixing_low = mixing.astype(jnp.bfloat16)
    weighted_low = weighted.astype(jnp.bfloat16)
    within = jnp.einsum(
        "chij,cjhp->cihp", mixing_low, head_rows, preferred_element_type=jnp.float32
    )
    local_part = jnp.einsum(
        "cjhp,chjn->chpn", head_rows, weighted_low, preferred_element_type=jnp.float32
    )
    entering = carry_states(local_part, fading).astype(jnp.bfloat16)
    reach_part = jnp.einsum("cin,chpn->cihp", c_rows, entering, preferred_element_type=jnp.float32)
    growth_rows = jnp.transpose(growth, (0, 2, 1))[:, :, :, None]
    result = within + growth_rows * reach_part + skip_here[:, None] * head_rows.astype(jnp.float32)
    return result.reshape(heads_x.shape[0], -1)


def mixer_backward(heads_x, shared, heads_dt, bias_here, decay_here, skip_here, grad_result):
    head_rows, b_rows, c_rows = split_rows(heads_x, shared, heads_dt)
    length = heads_x.shape[0]
    scores = jnp.einsum("cin,cjn->cij", c_rows, b_rows, preferred_element_type=jnp.float32)
    built, decay_pull = jax.vjp(
        decays,
        scores,
        b_rows.astype(jnp.float32),
        heads_dt.astype(jnp.float32),
        bias_here,
        decay_here,
    )
    mixing, weighted, growth, fading = built
    mixing_low = mixing.astype(jnp.bfloat16)
    weighted_low = weighted.astype(jnp.bfloat16)
    local_part = jnp.einsum(
        "cjhp,chjn->chpn", head_rows, weighted_low, preferred_element_type=jnp.float32
    )
    entering, carry_pull = jax.vjp(carry_states, local_part, fading)
    entering_low = entering.astype(jnp.bfloat16)
    reach_part = jnp.einsum(
        "cin,chpn->cihp", c_rows, entering_low, preferred_element_type=jnp.float32
    )
    grad_rows = grad_result.reshape(head_rows.shape)
    grad_float = grad_rows.astype(jnp.float32)
    growth_rows = jnp.transpose(growth, (0, 2, 1))[:, :, :, None]
    grad_skip = jnp.sum(grad_float * head_rows.astype(jnp.float32), axis=(0, 1, 3))
    grad_mixing = jnp.einsum(
        "cihp,cjhp->chij", grad_rows, head_rows, preferred_element_type=jnp.float32
    )
    grad_inputs = jnp.einsum(
        "chij,cihp->cjhp", mixing_low, grad_rows, preferred_element_type=jnp.float32
    )
    grad_inputs = grad_inputs + skip_here[:, None] * grad_float
    grad_reach = (grad_float * growth_rows).astype(jnp.bfloat16)
    grad_growth = jnp.transpose(jnp.sum(grad_float * reach_part, axis=3), (0, 2, 1))
    grad_entering = jnp.einsum(
        "cihp,cin->chpn", grad_reach, c_rows, preferred_element_type=jnp.float32
    )
    grad_c = jnp.einsum(
        "cihp,chpn->cin", grad_reach, entering_low, preferred_element_type=jnp.float32
    )
    grad_local, grad_fading = carry_pull(grad_entering)
    grad_local_low = grad_local.astype(jnp.bfloat16)
    grad_weighted = jnp.einsum(
        "cjhp,chpn->chjn", head_rows, grad_local_low, preferred_element_type=jnp.float32
    )
    grad_inputs = grad_inputs + jnp.einsum(
        "chjn,chpn->cjhp", weighted_low, grad_local_low, preferred_element_type=jnp.float32
    )
    grad_scores, grad_b, grad_dt, grad_bias, grad_decay = decay_pull(
        (grad_mixing, grad_weighted, grad_growth, grad_fading)
    )
    grad_scores_low = grad_scores.astype(jnp.bfloat16)
    grad_c = grad_c + jnp.einsum(
        "cij,cjn->cin", grad_scores_low, b_rows, preferred_element_type=jnp.float32
    )
    grad_b = grad_b + jnp.einsum(
        "cij,cin->cjn", grad_scores_low, c_rows, preferred_element_type=jnp.float32
    )
    grad_shared = jnp.concatenate([grad_b.reshape(length, -1), grad_c.reshape(length, -1)], 1)
    return (grad_inputs.reshape(length, -1), grad_dt, grad_shared, grad_bias, grad_decay, grad_skip)


def head_params(weights, offset, heads_here):
    return tuple(
        (
            lax.dynamic_slice_in_dim(member.astype(jnp.float32), offset, heads_here, 0)
            for member in (weights[4], weights[5], weights[6])
        )
    )


def layer_forward(hidden, weights):
    (
        norm_gain,
        in_weight,
        conv_weight,
        conv_bias,
        step_bias,
        log_decay,
        skip_gain,
        gate_gain,
        out_weight,
    ) = weights
    inner_width = gate_gain.shape[0]
    channels = conv_bias.shape[0]
    reach_rows = conv_weight.shape[0] - 1
    normed = pre_norm(hidden, norm_gain.astype(jnp.float32)).astype(jnp.bfloat16)
    projected = jnp.dot(normed, in_weight, preferred_element_type=jnp.float32).astype(jnp.bfloat16)
    before = projected[:, inner_width : inner_width + channels]
    halo_rows = shifted(before[before.shape[0] - reach_rows :], "seq", 1)
    padded = jnp.concatenate([halo_rows, before], 0).astype(jnp.float32)
    mixed_in = conv_part(
        padded, conv_weight.astype(jnp.float32), conv_bias.astype(jnp.float32)
    ).astype(jnp.bfloat16)
    heads_x, heads_dt = (
        lax.all_to_all(mixed_in[:, :inner_width], "seq", split_axis=1, concat_axis=0, tiled=True),
        lax.all_to_all(
            projected[:, inner_width + channels :], "seq", split_axis=1, concat_axis=0, tiled=True
        ),
    )
    shared = lax.all_gather(mixed_in[:, inner_width:], "seq", axis=0, tiled=True)
    heads_here = heads_dt.shape[1]
    offset = lax.axis_index("seq") * heads_here
    bias_here, decay_here, skip_here = head_params(weights, offset, heads_here)
    result_heads = mixer_forward(heads_x, shared, heads_dt, bias_here, decay_here, skip_here)
    result = lax.all_to_all(
        result_heads.astype(jnp.bfloat16), "seq", split_axis=0, concat_axis=1, tiled=True
    )
    normed_out = post_norm(
        result.astype(jnp.float32),
        projected[:, :inner_width].astype(jnp.float32),
        gate_gain.astype(jnp.float32),
    ).astype(jnp.bfloat16)
    branch = jnp.dot(normed_out, out_weight, preferred_element_type=jnp.float32)
    return (hidden + branch, (hidden, projected, halo_rows, heads_x, heads_dt, shared, result))


def place_heads(values, offset, heads_all):
    return lax.dynamic_update_slice_in_dim(jnp.zeros((heads_all,), jnp.float32), values, offset, 0)


def layer_backward(grad_next, saved, weights):
    (
        norm_gain,
        in_weight,
        conv_weight,
        conv_bias,
        step_bias,
        log_decay,
        skip_gain,
        gate_gain,
        out_weight,
    ) = weights
    hidden, projected, halo_rows, heads_x, heads_dt, shared, result = saved
    inner_width = gate_gain.shape[0]
    channels = conv_bias.shape[0]
    reach_rows = conv_weight.shape[0] - 1
    heads_all = step_bias.shape[0]
    grad_low = grad_next.astype(jnp.bfloat16)
    normed_float, post_pull = jax.vjp(
        post_norm,
        result.astype(jnp.float32),
        projected[:, :inner_width].astype(jnp.float32),
        gate_gain.astype(jnp.float32),
    )
    normed_out = normed_float.astype(jnp.bfloat16)
    grad_output = jnp.einsum("ti,td->id", normed_out, grad_low, preferred_element_type=jnp.float32)
    grad_normed_out = jnp.einsum(
        "td,id->ti", grad_low, out_weight, preferred_element_type=jnp.float32
    )
    grad_result, grad_gate, grad_gain = post_pull(grad_normed_out)
    grad_heads = lax.all_to_all(
        grad_result.astype(jnp.bfloat16), "seq", split_axis=1, concat_axis=0, tiled=True
    )
    heads_here = heads_dt.shape[1]
    offset = lax.axis_index("seq") * heads_here
    bias_here, decay_here, skip_here = head_params(weights, offset, heads_here)
    grad_inputs, grad_dt, grad_shared, grad_bias, grad_decay, grad_skip = mixer_backward(
        heads_x, shared, heads_dt, bias_here, decay_here, skip_here, grad_heads
    )
    token_inputs, token_dt = (
        lax.all_to_all(
            grad_inputs.astype(jnp.bfloat16), "seq", split_axis=0, concat_axis=1, tiled=True
        ),
        lax.all_to_all(
            grad_dt.astype(jnp.bfloat16), "seq", split_axis=0, concat_axis=1, tiled=True
        ),
    )
    token_shared = lax.psum_scatter(
        grad_shared.astype(jnp.bfloat16), "seq", scatter_dimension=0, tiled=True
    )
    grad_mixed = jnp.concatenate([token_inputs, token_shared], 1).astype(jnp.float32)
    before = projected[:, inner_width : inner_width + channels]
    padded = jnp.concatenate([halo_rows, before], 0).astype(jnp.float32)
    unused_value, conv_pull = jax.vjp(
        conv_part, padded, conv_weight.astype(jnp.float32), conv_bias.astype(jnp.float32)
    )
    grad_padded, grad_kernel, grad_shift = conv_pull(grad_mixed)
    spilled = shifted(grad_padded[:reach_rows].astype(jnp.bfloat16), "seq", -1).astype(jnp.float32)
    grad_before = grad_padded[reach_rows:]
    cut_point = grad_before.shape[0] - reach_rows
    grad_before = jnp.concatenate([grad_before[:cut_point], grad_before[cut_point:] + spilled], 0)
    grad_projected = jnp.concatenate(
        [grad_gate, grad_before, token_dt.astype(jnp.float32)], 1
    ).astype(jnp.bfloat16)
    normed_float, pre_pull = jax.vjp(pre_norm, hidden, norm_gain.astype(jnp.float32))
    normed = normed_float.astype(jnp.bfloat16)
    grad_input = jnp.einsum("td,tk->dk", normed, grad_projected, preferred_element_type=jnp.float32)
    grad_normed = jnp.einsum(
        "tk,dk->td", grad_projected, in_weight, preferred_element_type=jnp.float32
    )
    grad_hidden, grad_norm = pre_pull(grad_normed)
    grads = (
        grad_norm,
        grad_input,
        grad_kernel,
        grad_shift,
        place_heads(grad_bias, offset, heads_all),
        place_heads(grad_decay, offset, heads_all),
        place_heads(grad_skip, offset, heads_all),
        grad_gain,
        grad_output,
    )
    return (grad_next + grad_hidden, grads)


def join_items(*items):
    return jnp.stack(items)


def per_device(
    section_ends,
    norm_gain,
    in_weight,
    conv_weight,
    conv_bias,
    step_bias,
    log_decay,
    skip_gain,
    gate_gain,
    out_weight,
):
    section_index = lax.axis_index("section")
    batches = section_ends.shape[1]
    local_ends = section_ends[0, :, 0]
    gathered = (
        lax.all_gather(norm_gain, "fsdp", axis=1, tiled=True),
        lax.all_gather(in_weight, "fsdp", axis=1, tiled=True),
        lax.all_gather(conv_weight, "fsdp", axis=2, tiled=True),
        lax.all_gather(conv_bias, "fsdp", axis=1, tiled=True),
        lax.all_gather(step_bias, "fsdp", axis=1, tiled=True),
        lax.all_gather(log_decay, "fsdp", axis=1, tiled=True),
        lax.all_gather(skip_gain, "fsdp", axis=1, tiled=True),
        lax.all_gather(gate_gain, "fsdp", axis=1, tiled=True),
        lax.all_gather(out_weight, "fsdp", axis=1, tiled=True),
    )
    forward_weights = tuple((member[0] for member in gathered))
    incoming = jnp.zeros(local_ends.shape[1:], jnp.float32)
    saved_list = []
    outputs = []
    for moment in range(batches + 1):
        supplied = local_ends[min(moment, batches - 1)].astype(jnp.float32)
        hidden = jnp.where(section_index == 0, supplied, incoming)
        produced, saved = layer_forward(hidden, forward_weights)
        saved_list.append(saved)
        if moment > 0:
            outputs.append(produced)
        if moment < batches:
            incoming = shifted(produced.astype(jnp.bfloat16), "section", 1).astype(jnp.float32)
    stacked = jax.tree.map(join_items, *saved_list)
    regathered = (
        lax.all_gather(norm_gain, "fsdp", axis=1, tiled=True),
        lax.all_gather(in_weight, "fsdp", axis=1, tiled=True),
        lax.all_gather(conv_weight, "fsdp", axis=2, tiled=True),
        lax.all_gather(conv_bias, "fsdp", axis=1, tiled=True),
        lax.all_gather(step_bias, "fsdp", axis=1, tiled=True),
        lax.all_gather(log_decay, "fsdp", axis=1, tiled=True),
        lax.all_gather(skip_gain, "fsdp", axis=1, tiled=True),
        lax.all_gather(gate_gain, "fsdp", axis=1, tiled=True),
        lax.all_gather(out_weight, "fsdp", axis=1, tiled=True),
    )
    backward_weights = tuple((member[0] for member in regathered))
    totals = tuple((jnp.zeros(member.shape, jnp.float32) for member in backward_weights))
    received = jnp.zeros(local_ends.shape[1:], jnp.float32)
    grads_in = []
    for moment in range(batches + 1):
        chosen = moment - 1 + section_index
        validity = ((chosen >= 0) & (chosen < batches)).astype(jnp.float32)
        position = jnp.clip(moment - 1 + 2 * section_index, 0, batches)
        saved = tuple((lax.dynamic_index_in_dim(member, position, 0, False) for member in stacked))
        supplied = local_ends[min(moment, batches - 1)].astype(jnp.float32)
        grad_next = jnp.where(section_index == 1, supplied, received)
        grad_hidden, grads = layer_backward(grad_next, saved, backward_weights)
        totals = tuple((running + validity * member for running, member in zip(totals, grads)))
        if moment > 0:
            grads_in.append(grad_hidden)
        if moment < batches:
            received = shifted(grad_hidden.astype(jnp.bfloat16), "section", -1).astype(jnp.float32)
    pieces = [
        jnp.where(section_index == 0, grads_in[number], outputs[number])
        for number in range(batches)
    ]
    section_results = jnp.stack(pieces)[None, :, None]
    shares = (
        lax.psum_scatter(
            totals[0].astype(jnp.bfloat16), "fsdp", scatter_dimension=0, tiled=True
        ).astype(jnp.float32),
        lax.psum_scatter(
            totals[1].astype(jnp.bfloat16), "fsdp", scatter_dimension=0, tiled=True
        ).astype(jnp.float32),
        lax.psum_scatter(
            totals[2].astype(jnp.bfloat16), "fsdp", scatter_dimension=1, tiled=True
        ).astype(jnp.float32),
        lax.psum_scatter(
            totals[3].astype(jnp.bfloat16), "fsdp", scatter_dimension=0, tiled=True
        ).astype(jnp.float32),
        lax.psum_scatter(
            totals[4].astype(jnp.bfloat16), "fsdp", scatter_dimension=0, tiled=True
        ).astype(jnp.float32),
        lax.psum_scatter(
            totals[5].astype(jnp.bfloat16), "fsdp", scatter_dimension=0, tiled=True
        ).astype(jnp.float32),
        lax.psum_scatter(
            totals[6].astype(jnp.bfloat16), "fsdp", scatter_dimension=0, tiled=True
        ).astype(jnp.float32),
        lax.psum_scatter(
            totals[7].astype(jnp.bfloat16), "fsdp", scatter_dimension=0, tiled=True
        ).astype(jnp.float32),
        lax.psum_scatter(
            totals[8].astype(jnp.bfloat16), "fsdp", scatter_dimension=0, tiled=True
        ).astype(jnp.float32),
    )
    summed = (
        lax.psum(shares[0].astype(jnp.bfloat16), "seq").astype(jnp.float32),
        lax.psum(shares[1].astype(jnp.bfloat16), "seq").astype(jnp.float32),
        lax.psum(shares[2].astype(jnp.bfloat16), "seq").astype(jnp.float32),
        lax.psum(shares[3].astype(jnp.bfloat16), "seq").astype(jnp.float32),
        lax.psum(shares[4].astype(jnp.bfloat16), "seq").astype(jnp.float32),
        lax.psum(shares[5].astype(jnp.bfloat16), "seq").astype(jnp.float32),
        lax.psum(shares[6].astype(jnp.bfloat16), "seq").astype(jnp.float32),
        lax.psum(shares[7].astype(jnp.bfloat16), "seq").astype(jnp.float32),
        lax.psum(shares[8].astype(jnp.bfloat16), "seq").astype(jnp.float32),
    )
    return (
        section_results,
        summed[0][None],
        summed[1][None],
        summed[2][None],
        summed[3][None],
        summed[4][None],
        summed[5][None],
        summed[6][None],
        summed[7][None],
        summed[8][None],
    )


def solution(mesh):
    return jax.shard_map(
        per_device,
        mesh=mesh,
        in_specs=(
            P("section", None, "fsdp", "seq", None),
            P("section", "fsdp"),
            P("section", "fsdp", None),
            P("section", None, "fsdp"),
            P("section", "fsdp"),
            P("section", "fsdp"),
            P("section", "fsdp"),
            P("section", "fsdp"),
            P("section", "fsdp"),
            P("section", "fsdp", None),
        ),
        out_specs=(
            P("section", None, "fsdp", "seq", None),
            P("section", "fsdp"),
            P("section", "fsdp", None),
            P("section", None, "fsdp"),
            P("section", "fsdp"),
            P("section", "fsdp"),
            P("section", "fsdp"),
            P("section", "fsdp"),
            P("section", "fsdp"),
            P("section", "fsdp", None),
        ),
        check_vma=False,
    )
```

profile of v0, /device:TPU:19, one launch (start us, length us, event | category | flops | bytes accessed | tf_op | source)
XLA Modules:
  0.0 2158.2 jit_solution(15016888893507221359)
XLA Ops:
  19.8 59.1 %all_gather.46 = bf16[1,4,3328]{1,0,2:T(2,128)(2,1)S(1)} all-gather(bf16[1,4,832]{1,0,2:T(2,128)(2,1)S(1)} %copy.540), channel_id=1, replica_groups=mesh['section'=2,'seq'=4,'fsdp'=4] {'fsdp'}, dimensions={2}, use_global_device_ids=true | all-gather | bytes 33280 | tf_op jit(solution)/shard_map/all_gather | solution.py:329
  80.7 24.7 %all_gather.47 = bf16[1,1536]{1,0:T(2,128)(2,1)S(1)} all-gather(bf16[1,384]{1,0:T(2,128)(2,1)S(1)} %copy-done.253), channel_id=1, replica_groups=mesh['section'=2,'seq'=4,'fsdp'=4] {'fsdp'}, dimensions={1}, use_global_device_ids=true | all-gather | bytes 3840 | tf_op jit(solution)/shard_map/all_gather | solution.py:327
  107.4 69.3 %slice_reduce_fusion.3 = (f32[3328]{0:T(1024)S(1)}, f32[3328]{0:T(1024)S(1)}, f32[3328]{0:T(1024)S(1)}, f32[3328]{0:T(1024)S(1)}) fusion(f32[1,4,3328]{1,0,2:T(1,128)S(1)} %convert_element_type.635), kind=kLoop, calls=%fused_computation.402 | loop fusion | bytes 106496 | tf_op jit(solution)/shard_map/slice | solution.py:33
  176.7 195.8 %all-gather.3.cloned.1.call-done = bf16[1,1536,6448]{1,2,0:T(8,128)(2,1)} async-done(((bf16[1,384,6448]{1,2,0:T(8,128)(2,1)}), bf16[1,1536,6448]{1,2,0:T(8,128)(2,1)}) %all-gather.3.cloned.1.call-update) | async-done | bytes 19808272 | tf_op jit(solution)/shard_map/all_gather | solution.py:328
  372.5 9.9 fusion.42
  401.2 21.7 %all_gather.49 = bf16[1024,256]{1,0:T(8,128)(2,1)S(1)} all-gather(bf16[256,256]{1,0:T(8,128)(2,1)S(1)} %slice-done.5), channel_id=1, replica_groups=mesh['section'=2,'seq'=4,'fsdp'=4] {'seq'}, dimensions={0}, use_global_device_ids=true | all-gather | bytes 655360 | tf_op jit(solution)/shard_map/all_gather | solution.py:201
  450.6 11.0 all_gather.53
  474.2 64.9 %all-gather.5.cloned.1.call-done = bf16[1,3072,1536]{2,1,0:T(8,128)(2,1)} async-done(((bf16[1,768,1536]{2,1,0:T(8,128)(2,1)}), bf16[1,3072,1536]{2,1,0:T(8,128)(2,1)}) %all-gather.5.cloned.1.call-update) | async-done | bytes 9437200 | tf_op jit(solution)/shard_map/all_gather | solution.py:335
  539.1 8.1 fusion.207
  550.6 16.0 collective-permute-done.1
  568.0 9.9 fusion.45
  601.6 21.2 all_gather.55
  676.3 8.2 fusion.543
  706.6 9.9 fusion.48
  735.4 8.1 pad_maximum_fusion
  776.3 22.5 %all_gather.56 = bf16[1024,256]{1,0:T(8,128)(2,1)S(1)} all-gather(bf16[256,256]{1,0:T(8,128)(2,1)S(1)} %slice-done.7), channel_id=1, replica_groups=mesh['section'=2,'seq'=4,'fsdp'=4] {'seq'}, dimensions={0}, use_global_device_ids=true | all-gather | bytes 655360 | tf_op jit(solution)/shard_map/all_gather | solution.py:201
  815.2 16.4 while.143
  886.7 9.8 multiply_reduce_fusion.26
  909.4 21.3 while.144
  952.6 22.2 %while.145 = (s32[]{:T(128)}, f32[12,64,128]{2,1,0:T(8,128)}, bf16[4,12,64,128]{3,2,1,0:T(8,128)(2,1)}, f32[4,12]{1,0:T(4,128)}, f32[4,12,64,128]{3,2,1,0:T(8,12...) while((s32[]{:T(128)}, f32[12,64,128]{2,1,0:T(8,128)}, ...), condition=%wide.region_17.19_spmd.clone, body=%wide.region_15.18_spmd.clone.sunk | while | flops 589816 | bytes 2163124 | solution.py:63
  983.3 11.9 fusion.52
  996.8 7.7 fusion.143
  1057.4 14.4 multiply_reduce_fusion.38
  1079.1 16.3 collective-permute-done.6
  1137.7 7.9 while.147
  1153.0 11.8 fusion.54
  1166.4 7.6 fusion.154
  1194.8 8.5 all-to-all-done.13
  1227.0 13.4 multiply_reduce_fusion.37
  1250.5 14.4 collective-permute-done.8
  1265.0 8.9 multiply_reduce_fusion.24
  1284.5 20.8 fusion.294
  1326.4 11.8 fusion.56
  1339.8 7.6 fusion.165
  1365.4 9.7 all-to-all-done.16
  1397.6 20.4 fusion.295
  1421.1 32.8 %add_convert_fusion = bf16[1536,6448]{0,1:T(8,128)(2,1)} fusion(f32[1536,6448]{0,1:T(8,128)} %fusion.295, f32[1536,6448]{0,1:T(8,128)} %fusion.294, f32[]{:T(128)S(6)} %convert_element_type.768, f32[]{:T(128)S(6)} %convert_element_type.767, f32[]{:T(128)S(6)} %convert_element_type.766, f32[3,256,1536]{2,1,0:T(8,128)} %copy-done.2, s32[]{:T(128)S(6)} %min.12, ...), kind=kOutput, calls=%fused_computation.45 | convolution fusion | flops 5144723456 | bytes 103963664 | tf_op jit(solution)/shard_map/td,tk->dk/dot_general | solution.py:288
  1453.9 24.5 %copy.650 = bf16[1536,6448]{1,0:T(8,128)(2,1)} copy(bf16[1536,6448]{0,1:T(8,128)(2,1)} %add_convert_fusion) | data formatting | bytes 39616512
  1480.3 11.4 fusion.228
  1491.8 11.9 fusion.229
  1503.7 19.1 add_convert_fusion.1
  1543.3 268.7 %reduce-scatter.19.cloned.1.call-done = bf16[384,6448]{1,0:T(8,128)(2,1)} async-done(((bf16[1536,6448]{1,0:T(8,128)(2,1)}), bf16[384,6448]{1,0:T(8,128)(2,1)}) %reduce-scatter.19.cloned.1.call-update) | async-done | bytes 4952080
  1819.5 157.6 %reduce-scatter.17.cloned.1.call-done = bf16[768,1536]{1,0:T(8,128)(2,1)} async-done(((bf16[3072,1536]{1,0:T(8,128)(2,1)}), bf16[768,1536]{1,0:T(8,128)(2,1)}) %reduce-scatter.17.cloned.1.call-update) | async-done | bytes 2359312 | tf_op jit(solution)/shard_map/reduce_scatter | solution.py:409
  1978.7 14.3 multiply_reduce_fusion.36
  1992.9 14.0 all-reduce.40
  2007.4 11.1 fusion.225
  2021.5 14.0 all-reduce.42
  2039.4 102.9 %all-reduce.46.cloned.1.call-done = (bf16[1,384,6448]{1,2,0:T(8,128)(2,1)}, bf16[1,768,1536]{2,1,0:T(8,128)(2,1)}) async-done(((bf16[1,384,6448]{1,2,0:T(8,128)(2,1)}, bf16[1,768,1536]{2,1,0:T(8,128)(2,1)}), (bf16[1,384,6448]{1,2,0:T(8,128)(2,1)}, bf16[1,768,1536]{2,1,0:T(8,128)(2,1)})) %all-reduce.46.cloned.1.call-update) | async-done | bytes 7311376 | tf_op jit(solution)/shard_map/psum | solution.py:415
  (1154 shorter events, 722.5 us)
Async XLA Ops:
  7.2 365.3 %all-gather.3.cloned.1.call-start = ((), (), s32[]{:S(2)}) async-start(), calls=%async_computation.24 | async-start | bytes 24760320 | tf_op jit(solution)/shard_map/all_gather | solution.py:328
  8.0 531.2 %all-gather.5.cloned.1.call-start = ((), (), s32[]{:S(2)}) async-start(), calls=%async_computation.25 | async-start | bytes 11796480 | tf_op jit(solution)/shard_map/all_gather | solution.py:335
  19.0 366.6 %copy-start.232 = (f32[48]{0:T(128)}, f32[48]{0:T(128)S(1)}, u32[]{:S(2)}) copy-start(f32[48]{0:T(128)S(1)} %convert_element_type.808) | copy-start | bytes 580
  105.4 601.1 %copy-start.74 = (f32[1536]{0:T(1024)}, f32[1536]{0:T(1024)S(1)}, u32[]{:S(2)}) copy-start(f32[1536]{0:T(1024)S(1)} %convert_reduce_fusion) | copy-start | bytes 18436
  105.5 532.0 %copy-start.207 = (pred[256,256]{1,0:T(8,128)(4,1)}, pred[256,256]{1,0:T(8,128)(4,1)S(1)}, u32[]{:S(2)}) copy-start(pred[256,256]{1,0:T(8,128)(4,1)S(1)} %select_compare_fusion) | copy-start | bytes 196612
  105.7 280.2 %copy-start.7 = (bf16[4,12,64,128]{3,2,1,0:T(8,128)(2,1)}, bf16[4,12,64,128]{3,2,1,0:T(8,128)(2,1)S(1)}, u32[]{:S(2)}) copy-start(bf16[4,12,64,128]{3,2,1,0:T(8,128)(2,1)S(1)} %fusion.535) | copy-start | bytes 2359300
  176.7 414.8 %copy-start.87 = (f32[3328]{0:T(1024)}, f32[3328]{0:T(1024)S(1)}, u32[]{:S(2)}) copy-start(f32[3328]{0:T(1024)S(1)} %get-tuple-element.953) | copy-start | bytes 39940
  176.7 414.8 %copy-start.92 = (f32[3328]{0:T(1024)}, f32[3328]{0:T(1024)S(1)}, u32[]{:S(2)}) copy-start(f32[3328]{0:T(1024)S(1)} %get-tuple-element.954) | copy-start | bytes 39940
  384.2 7.5 collective-permute-start
  385.7 215.1 %copy-start.227 = (f32[12]{0:T(128)}, f32[12]{0:T(128)S(1)}, u32[]{:S(2)}) copy-start(f32[12]{0:T(128)S(1)} %dynamic-slice_exponential_fusion) | copy-start | bytes 148
  385.8 373.6 %copy-start.218 = (f32[12]{0:T(128)}, f32[12]{0:T(128)S(1)}, u32[]{:S(2)}) copy-start(f32[12]{0:T(128)S(1)} %dynamic-slice.7) | copy-start | bytes 148
  385.9 205.7 %copy-start.116 = (f32[3328]{0:T(1024)}, f32[3328]{0:T(1024)S(1)}, u32[]{:S(2)}) copy-start(f32[3328]{0:T(1024)S(1)} %add.847) | copy-start | bytes 39940
  386.6 10.3 all-to-all-start.1
  396.9 28.2 %all-to-all-start = ((bf16[256,4,768]{2,0,1:T(8,128)(2,1)}), bf16[256,4,768]{2,0,1:T(8,128)(2,1)S(1)}, u32[]{:S(2)}, u32[]{:S(2)}) async-start(bf16[256,4,768]{2,0,1:T(8,128)(2,1)} %bitcast.977), calls=%async_computation | async-start | bytes 3145728 | tf_op jit(solution)/shard_map/all_to_all | solution.py:196
  445.6 23.1 %all-to-all-start.2 = ((bf16[4,256,768]{2,1,0:T(8,128)(2,1)}), bf16[4,256,768]{2,1,0:T(8,128)(2,1)S(1)}, u32[]{:S(2)}, u32[]{:S(2)}) async-start(bf16[4,256,768]{2,1,0:T(8,128)(2,1)} %copy.545), calls=%async_computation.2 | async-start | bytes 3145728 | tf_op jit(solution)/shard_map/all_to_all | solution.py:206
  461.6 214.6 %copy-start.137 = (f32[1,3072]{1,0:T(1,128)}, f32[1,3072]{1,0:T(1,128)S(1)}, u32[]{:S(2)}) copy-start(f32[1,3072]{1,0:T(1,128)S(1)} %mul.2092) | copy-start | bytes 36868
  547.2 19.3 collective-permute-start.1
  579.6 10.1 collective-permute-start.2
  584.5 12.0 all-to-all-start.4
  596.5 28.6 %all-to-all-start.3 = ((bf16[256,4,768]{2,0,1:T(8,128)(2,1)}), bf16[256,4,768]{2,0,1:T(8,128)(2,1)}, u32[]{:S(2)}, u32[]{:S(2)}) async-start(bf16[256,4,768]{2,0,1:T(8,128)(2,1)} %bitcast.978), calls=%async_computation.3 | async-start | bytes 3145728 | tf_op jit(solution)/shard_map/all_to_all | solution.py:196
  646.7 24.7 %all-to-all-start.5 = ((bf16[4,256,768]{2,1,0:T(8,128)(2,1)}), bf16[4,256,768]{2,1,0:T(8,128)(2,1)}, u32[]{:S(2)}, u32[]{:S(2)}) async-start(bf16[4,256,768]{2,1,0:T(8,128)(2,1)} %copy.552), calls=%async_computation.5 | async-start | bytes 3145728 | tf_op jit(solution)/shard_map/all_to_all | solution.py:206
  684.5 20.7 collective-permute-start.3
  725.1 39.7 %collective-permute-start.4 = (bf16[3,3328]{1,0:T(4,128)(2,1)}, bf16[3,3328]{1,0:T(4,128)(2,1)}, u32[]{:S(2)}, u32[]{:S(2)}) collective-permute-start(bf16[3,3328]{1,0:T(4,128)(2,1)} %slice.408), channel_id=1, source_target_pairs={{0,4},{4,8},{8,12},{1,5},{5,9},{9,13},{2,6},{6,10},{10,14},{3,7},{... | collective-permute-start | bytes 59912 | tf_op jit(solution)/shard_map/ppermute | solution.py:16
  728.0 28.4 %all-to-all-start.7 = ((bf16[256,4,12]{0,2,1:T(8,128)(2,1)}), bf16[256,4,12]{0,2,1:T(8,128)(2,1)}, u32[]{:S(2)}, u32[]{:S(2)}) async-start(bf16[256,4,12]{0,2,1:T(8,128)(2,1)} %all_to_all.221), calls=%async_computation.7 | async-start | bytes 65536 | tf_op jit(solution)/shard_map/all_to_all | solution.py:197
  771.8 36.5 %all-to-all-start.6 = ((bf16[256,4,768]{2,0,1:T(8,128)(2,1)}), bf16[256,4,768]{2,0,1:T(8,128)(2,1)}, u32[]{:S(2)}, u32[]{:S(2)}) async-start(bf16[256,4,768]{2,0,1:T(8,128)(2,1)} %bitcast.853), calls=%async_computation.6 | async-start | bytes 3145728 | tf_op jit(solution)/shard_map/all_to_all | solution.py:196
  841.7 31.4 %all-to-all-start.8 = ((bf16[4,256,768]{2,1,0:T(8,128)(2,1)}), bf16[4,256,768]{2,1,0:T(8,128)(2,1)}, u32[]{:S(2)}, u32[]{:S(2)}) async-start(bf16[4,256,768]{2,1,0:T(8,128)(2,1)} %copy.559), calls=%async_computation.8 | async-start | bytes 3145728 | tf_op jit(solution)/shard_map/all_to_all | solution.py:206
  902.7 41.5 %all-to-all-start.9 = ((bf16[256,4,768]{2,0,1:T(8,128)(2,1)}), bf16[256,4,768]{2,0,1:T(8,128)(2,1)}, u32[]{:S(2)}, u32[]{:S(2)}) async-start(bf16[256,4,768]{2,0,1:T(8,128)(2,1)} %bitcast.976), calls=%async_computation.9 | async-start | bytes 3145728 | tf_op jit(solution)/shard_map/all_to_all | solution.py:252
  907.0 134.2 %reduce-scatter.11.cloned.1.call-start = ((), (), s32[]{:S(2)}) async-start(), calls=%async_computation.26 | async-start | bytes 655360 | tf_op jit(solution)/shard_map/reduce_scatter | solution.py:269
  1007.1 25.6 %all-to-all-start.10 = ((bf16[4,256,768]{2,1,0:T(8,128)(2,1)}), bf16[4,256,768]{2,1,0:T(8,128)(2,1)}, u32[]{:S(2)}, u32[]{:S(2)}) async-start(bf16[4,256,768]{2,1,0:T(8,128)(2,1)} %copy.573), calls=%async_computation.10 | async-start | bytes 3145728 | tf_op jit(solution)/shard_map/all_to_all | solution.py:262
  1032.7 22.2 %all-to-all-start.11 = ((bf16[4,256,12]{1,2,0:T(8,128)(2,1)}), bf16[4,256,12]{1,2,0:T(8,128)(2,1)}, u32[]{:S(2)}, u32[]{:S(2)}) async-start(bf16[4,256,12]{1,2,0:T(8,128)(2,1)} %copy.583), calls=%async_computation.12 | async-start | bytes 65536 | tf_op jit(solution)/shard_map/all_to_all | solution.py:265
  1051.8 4.4 collective-permute-start.5
  1073.9 21.5 collective-permute-start.6
  1076.0 109.0 %copy-start.186 = (f32[4,12]{1,0:T(4,128)}, f32[4,12]{1,0:T(4,128)S(1)}, u32[]{:S(2)}) copy-start(f32[4,12]{1,0:T(4,128)S(1)} %slice_reduce_fusion.5) | copy-start | bytes 580
  1107.9 22.3 %all-to-all-start.12 = ((bf16[256,4,768]{2,0,1:T(8,128)(2,1)}), bf16[256,4,768]{2,0,1:T(8,128)(2,1)}, u32[]{:S(2)}, u32[]{:S(2)}) async-start(bf16[256,4,768]{2,0,1:T(8,128)(2,1)} %bitcast.851), calls=%async_computation.13 | async-start | bytes 3145728 | tf_op jit(solution)/shard_map/all_to_all | solution.py:252
  1112.4 99.0 %reduce-scatter.13.cloned.1.call-start = ((), (), s32[]{:S(2)}) async-start(), calls=%async_computation.27 | async-start | bytes 655360 | tf_op jit(solution)/shard_map/reduce_scatter | solution.py:269
  1176.7 26.7 %all-to-all-start.13 = ((bf16[4,256,768]{2,1,0:T(8,128)(2,1)}), bf16[4,256,768]{2,1,0:T(8,128)(2,1)}, u32[]{:S(2)}, u32[]{:S(2)}) async-start(bf16[4,256,768]{2,1,0:T(8,128)(2,1)} %copy.594), calls=%async_computation.14 | async-start | bytes 3145728 | tf_op jit(solution)/shard_map/all_to_all | solution.py:262
  1203.3 21.2 all-to-all-start.14
  1222.1 3.8 collective-permute-start.7
  1244.0 21.0 collective-permute-start.8
  1280.0 25.9 %all-to-all-start.15 = ((bf16[256,4,768]{2,0,1:T(8,128)(2,1)}), bf16[256,4,768]{2,0,1:T(8,128)(2,1)}, u32[]{:S(2)}, u32[]{:S(2)}) async-start(bf16[256,4,768]{2,0,1:T(8,128)(2,1)} %bitcast.979), calls=%async_computation.17 | async-start | bytes 3145728 | tf_op jit(solution)/shard_map/all_to_all | solution.py:252
  1284.4 99.5 %reduce-scatter.15.cloned.1.call-start = ((), (), s32[]{:S(2)}) async-start(), calls=%async_computation.28 | async-start | bytes 655360 | tf_op jit(solution)/shard_map/reduce_scatter | solution.py:269
  1350.0 25.2 %all-to-all-start.16 = ((bf16[4,256,768]{2,1,0:T(8,128)(2,1)}), bf16[4,256,768]{2,1,0:T(8,128)(2,1)}, u32[]{:S(2)}, u32[]{:S(2)}) async-start(bf16[4,256,768]{2,1,0:T(8,128)(2,1)} %copy.615), calls=%async_computation.18 | async-start | bytes 3145728 | tf_op jit(solution)/shard_map/all_to_all | solution.py:262
  1375.1 42.8 %all-to-all-start.17 = ((bf16[4,256,12]{1,2,0:T(8,128)(2,1)}), bf16[4,256,12]{1,2,0:T(8,128)(2,1)}, u32[]{:S(2)}, u32[]{:S(2)}) async-start(bf16[4,256,12]{1,2,0:T(8,128)(2,1)} %copy.625), calls=%async_computation.20 | async-start | bytes 65536 | tf_op jit(solution)/shard_map/all_to_all | solution.py:265
  1381.1 430.8 %reduce-scatter.19.cloned.1.call-start = ((), (), s32[]{:S(2)}) async-start(), calls=%async_computation.30 | async-start | bytes 25067520
  1394.7 25.2 %collective-permute-start.9 = (bf16[3,3328]{1,0:T(4,128)(2,1)S(1)}, bf16[3,3328]{1,0:T(4,128)(2,1)}, u32[]{:S(2)}, u32[]{:S(2)}) collective-permute-start(bf16[3,3328]{1,0:T(4,128)(2,1)S(1)} %slice.455), channel_id=1, source_target_pairs={{4,0},{8,4},{12,8},{5,1},{9,5},{13,9},{6,2},{10,6},{14,10},{7,3},{... | collective-permute-start | bytes 59912 | tf_op jit(solution)/shard_map/ppermute | solution.py:16
  1478.4 498.8 %reduce-scatter.17.cloned.1.call-start = ((), (), s32[]{:S(2)}) async-start(), calls=%async_computation.29 | async-start | bytes 11796480 | tf_op jit(solution)/shard_map/reduce_scatter | solution.py:409
  1522.8 497.7 %reduce-scatter.21.cloned.1.call-start = ((), (), s32[]{:S(2)}) async-start(), calls=%async_computation.31 | async-start | bytes 1064960
  1543.2 599.1 %all-reduce.46.cloned.1.call-start = ((), (), s32[]{:S(2)}) async-start(), calls=%async_computation.32 | async-start | bytes 14622720 | tf_op jit(solution)/shard_map/psum | solution.py:415
  (268 other events, 2203.8 us)
Sparse Core Ops, SparseCore 0:
  9.7 362.8 all-gather.2
  374.1 164.9 all-gather.4
  996.9 24.7 reduce-scatter.10
  1166.5 21.7 reduce-scatter.12
  1339.9 24.2 reduce-scatter.14
  1478.5 333.4 reduce-scatter.18
  1815.0 162.1 reduce-scatter.16
  1979.6 22.9 reduce-scatter.20
  2005.0 137.2 all-reduce.45
where the time goes:
time: 2170 us; the launch traced here: 2160 us
  waiting for transfers between devices  888 us (41%)
  matrix products  400 us (18%)
  local copies, waits for them, and re-layouts  315 us (15%)
  other arithmetic  219 us (10%)
  blocking collectives  195 us (9%)
  starting transfers between devices  117 us (5%)
  between operations  21.8 us (1%)
    unnamed x11, waiting for transfers between devices  270 us
    all_gather x1, waiting for transfers between devices, per_device(): lax.all_gather(in_weight, 'fsdp', axis=1, tiled=True)  196 us
    reduce_scatter x1, waiting for transfers between devices, per_device(): lax.psum_scatter(totals[8].astype(jnp.bfloat16), 'fsdp', scatter_dimensio...  158 us
    psum x1, waiting for transfers between devices, per_device(): lax.psum(shares[1].astype(jnp.bfloat16), 'seq').astype(jnp.float32)  103 us
    dot_general x3, matrix products, layer_backward(): jnp.einsum('td,tk->dk', normed, grad_projected, preferred_element_type=jn...  74 us
    slice x1, local copies, waits for them, and re-layouts, conv_part(): running = conv_bias + conv_weight[0] * padded[0:length]  69.3 us
    unnamed x582, local copies, waits for them, and re-layouts  65.7 us
    all_gather x3, blocking collectives, layer_forward(): lax.all_gather(mixed_in[:, inner_width:], 'seq', axis=0, tiled=True)  65.3 us
  transfers between devices with their start and end apart: 37, of which 15 were waited for; matrix products, arithmetic and copies ran while one was open for 24% of the time, Pallas kernels for 0%

commit v1 on v0

v1 whole, which is shorter than its diff:
```python
import functools

import jax
import jax.numpy as jnp
import numpy as np
from jax import lax
from jax.experimental import pallas as pl
from jax.experimental.pallas import tpu as pltpu
from jax.sharding import PartitionSpec as P

SPAN = 256
HEAD = 64
STATE = 128
EPS = 1e-05
F32 = jnp.float32
BF16 = jnp.bfloat16


def dot(a, b, ca, cb):
    return lax.dot_general(a, b, (((ca,), (cb,)), ((), ())), preferred_element_type=F32)


def split3(v):
    hi = v.astype(BF16)
    rest = v - hi.astype(F32)
    mid = rest.astype(BF16)
    low = (rest - mid.astype(F32)).astype(BF16)
    return hi, mid, low


def sigmoid(v):
    return 1.0 / (1.0 + jnp.exp(-v))


def running_conv(pad_ref, vec_ref, taps):
    run = vec_ref[taps : taps + 1, :] + vec_ref[0:1, :] * pad_ref[pl.ds(8 - taps + 1, SPAN), :]
    for k in range(1, taps):
        run = run + vec_ref[k : k + 1, :] * pad_ref[pl.ds(8 - taps + 1 + k, SPAN), :]
    return run


def step_sizes(dt_raw, vec_ref, tri):
    x = dt_raw + vec_ref[6:7, :STATE]
    e = jnp.exp(-jnp.abs(x))
    dt = jnp.maximum(x, 0.0) + jnp.log1p(e)
    decay = jnp.exp(vec_ref[7:8, :STATE])
    rate = -dt * decay
    hi, mid, low = split3(rate)
    packed = dot(tri, jnp.concatenate([hi, mid, low], 1), 1, 0)
    cum = packed[:, :STATE] + packed[:, STATE : 2 * STATE] + packed[:, 2 * STATE :]
    return x, e, dt, decay, rate, cum


def expand(v, spread3):
    return dot(jnp.concatenate(split3(v), 1), spread3, 1, 0)


def per_head(v, gather3):
    return dot(jnp.concatenate(split3(v), 1), gather3, 1, 0)


def fading(cum, cum_t, dt_t, h, inside):
    spread = cum[:, h : h + 1] - cum_t[h : h + 1, :]
    return jnp.exp(jnp.where(inside, spread, -1e30)) * dt_t[h : h + 1, :]


def inside_mask():
    rows = lax.broadcasted_iota(jnp.int32, (SPAN, SPAN), 0)
    cols = lax.broadcasted_iota(jnp.int32, (SPAN, SPAN), 1)
    return cols <= rows


def forward_kernel(
    heads, blocks, taps,
    full_ref, wgx_ref, ws_ref, wo_ref, vec_ref, tri_ref, spread_ref,
    part_ref, ss_ref, pgx_ref, ps_ref, res_ref, ent_ref,
    pad_ref, state_ref, within_ref,
):
    cw = heads * HEAD
    first = lax.rem(pl.program_id(0), blocks) == 0

    @pl.when(first)
    def _():
        pad_ref[pl.ds(SPAN, 8), :] = jnp.zeros((8, pad_ref.shape[1]), F32)
        state_ref[...] = jnp.zeros_like(state_ref)

    x = full_ref[...]
    pgx = dot(x, wgx_ref[...], 1, 0).astype(BF16)
    ps = dot(x, ws_ref[...], 1, 0).astype(BF16)
    pgx_ref[...] = pgx
    ps_ref[...] = ps
    pad_ref[pl.ds(0, 8), :] = pad_ref[pl.ds(SPAN, 8), :]
    pad_ref[pl.ds(8, SPAN), :cw] = pgx[:, cw:].astype(F32)
    pad_ref[pl.ds(8, SPAN), cw:] = ps[:, : 2 * STATE].astype(F32)
    run = running_conv(pad_ref, vec_ref, taps)
    mixed = (run * sigmoid(run)).astype(BF16)
    xs, b, c = mixed[:, :cw], mixed[:, cw : cw + STATE], mixed[:, cw + STATE :]
    _, _, dt, _, _, cum = step_sizes(ps[:, 2 * STATE :].astype(F32), vec_ref, tri_ref[...])
    cum_t, dt_t = cum.T, dt.T
    inside = inside_mask()
    scores = dot(c, b, 1, 1)
    for h in range(heads):
        mixing = (scores * fading(cum, cum_t, dt_t, h, inside)).astype(BF16)
        within_ref[:, h * HEAD : (h + 1) * HEAD] = dot(mixing, xs[:, h * HEAD : (h + 1) * HEAD], 1, 0)
    tail = jnp.exp(cum[SPAN - 1 : SPAN, :] - cum) * dt
    growth = jnp.exp(cum)
    both = expand(jnp.concatenate([tail, growth], 0), spread_ref[...])
    tail_e, growth_e = both[:SPAN], both[SPAN:]
    xs_f = xs.astype(F32)
    state = state_ref[...]
    state_low = state.astype(BF16)
    ent_ref[0] = state_low
    reach = dot(c, state_low, 1, 0)
    state_ref[...] = growth_e[SPAN - 1 : SPAN, :] * state + dot(b, (xs_f * tail_e).astype(BF16), 0, 0)
    result = (within_ref[...] + growth_e * reach + vec_ref[8:9, :cw] * xs_f).astype(BF16)
    res_ref[...] = result
    gate = pgx[:, :cw].astype(F32)
    g = result.astype(F32) * (gate * sigmoid(gate))
    ss = jnp.sum(g * g, axis=1, keepdims=True)
    ss_ref[0] = jnp.broadcast_to(ss, (SPAN, STATE)).T[:8, :]
    part_ref[...] = dot((g * vec_ref[5:6, :cw]).astype(BF16), wo_ref[...], 1, 0).astype(BF16)


def backward_kernel(
    heads, blocks, taps,
    gb_ref, sc_ref, pgx_ref, ps_ref, hgx_ref, hs_ref, res_ref, ent_ref,
    wgx_ref, ws_ref, wo_ref, vec_ref, tri_ref, spread_ref, gather_ref,
    pg_ref, gpgx_ref, gps_ref, no_ref, small_ref,
    pad_ref, next_ref, ge_ref, within_ref, gxm_ref,
):
    cw = heads * HEAD
    step = pl.program_id(0)
    place = lax.rem(step, blocks)

    @pl.when(step == 0)
    def _():
        small_ref[...] = jnp.zeros_like(small_ref)

    @pl.when(place == 0)
    def _():
        next_ref[pl.ds(0, 8), :] = jnp.zeros((8, next_ref.shape[1]), F32)
        ge_ref[...] = jnp.zeros_like(ge_ref)

    pgx, ps = pgx_ref[...], ps_ref[...]
    keep = jnp.where(place == blocks - 1, 0.0, 1.0)
    pad_ref[pl.ds(0, 8), :cw] = hgx_ref[8:, cw:].astype(F32) * keep
    pad_ref[pl.ds(0, 8), cw:] = hs_ref[8:, : 2 * STATE].astype(F32) * keep
    pad_ref[pl.ds(8, SPAN), :cw] = pgx[:, cw:].astype(F32)
    pad_ref[pl.ds(8, SPAN), cw:] = ps[:, : 2 * STATE].astype(F32)
    run = running_conv(pad_ref, vec_ref, taps)
    sig = sigmoid(run)
    mixed = (run * sig).astype(BF16)
    slope = sig * (1.0 + run * (1.0 - sig))
    xs, b, c = mixed[:, :cw], mixed[:, cw : cw + STATE], mixed[:, cw + STATE :]
    xs_f = xs.astype(F32)
    tri = tri_ref[...]
    x, e, dt, decay, rate, cum = step_sizes(ps[:, 2 * STATE :].astype(F32), vec_ref, tri)
    cum_t, dt_t = cum.T, dt.T
    tail = jnp.exp(cum[SPAN - 1 : SPAN, :] - cum) * dt
    growth = jnp.exp(cum)
    both = expand(jnp.concatenate([tail, growth], 0), spread_ref[...])
    tail_e, growth_e = both[:SPAN], both[SPAN:]

    gb = gb_ref[...]
    gu = dot(gb, wo_ref[...], 1, 1)
    columns = jnp.concatenate([sc_ref[0]] * (STATE // 8), 0).T
    r, pull = columns[:, 0:1], columns[:, 1:2]
    gain = vec_ref[5:6, :cw]
    gate = pgx[:, :cw].astype(F32)
    sg = sigmoid(gate)
    sl = gate * sg
    res = res_ref[...].astype(F32)
    g = res * sl
    rg = r * g
    no_ref[...] = (rg * gain).astype(BF16)
    dg = r * (gu * gain) - pull * g
    gr = (dg * sl).astype(BF16)
    gr_f = gr.astype(F32)
    ggate = dg * res * (sg + sl * (1.0 - sg))

    ent = ent_ref[0]
    ge = ge_ref[...]
    gl = ge.astype(BF16)
    reach = dot(c, ent, 1, 0)
    pulled = tail_e * dot(b, gl, 1, 0)
    gq = (growth_e * gr_f).astype(BF16)
    grad_c = dot(gq, ent, 1, 1)
    grad_b = dot((xs_f * tail_e).astype(BF16), gl, 1, 1)
    fade = growth_e[SPAN - 1 : SPAN, :]
    ge_ref[...] = fade * ge + dot(c, gq, 0, 0)
    grad_fade = fade * jnp.sum(ge * ent.astype(F32), axis=0, keepdims=True)
    inside = inside_mask()
    scores = dot(c, b, 1, 1)
    gs = jnp.zeros((SPAN, SPAN), F32)
    for h in range(heads):
        cols = slice(h * HEAD, (h + 1) * HEAD)
        fade_in = fading(cum, cum_t, dt_t, h, inside)
        mixing = (scores * fade_in).astype(BF16)
        gs = gs + dot(gr[:, cols], xs[:, cols], 1, 1) * fade_in
        within_ref[:, cols] = dot(mixing, xs[:, cols], 1, 0)
        gxm_ref[:, cols] = dot(mixing, gr[:, cols], 0, 0)
    gs = gs.astype(BF16)
    grad_c = grad_c + dot(gs, b, 1, 0)
    grad_b = grad_b + dot(gs, c, 0, 0)
    gxm = gxm_ref[...]
    grad_x = vec_ref[8:9, :cw] * gr_f + pulled + gxm

    gather = gather_ref[...]
    tall = jnp.concatenate([gr_f * (within_ref[...] + growth_e * reach), xs_f * gxm, xs_f * pulled], 0)
    sums = per_head(tall, gather)
    s1, s2, s3 = sums[:SPAN], sums[SPAN : 2 * SPAN], sums[2 * SPAN :]
    thin = jnp.concatenate(
        [jnp.sum(gr_f * xs_f, axis=0, keepdims=True), grad_fade, jnp.zeros((6, cw), F32)], 0
    )
    thin = per_head(thin, gather)
    hi, mid, low = split3(s1 - s2 - s3)
    packed = dot(tri, jnp.concatenate([hi, mid, low], 1), 0, 0)
    grad_rate = packed[:, :STATE] + packed[:, STATE : 2 * STATE] + packed[:, 2 * STATE :]
    grad_rate = grad_rate + (jnp.sum(s3, axis=0, keepdims=True) + thin[1:2, :])
    denominator = 1.0 + e
    slope_x = jnp.where(x >= 0, 1.0, e) / denominator
    ratio = jnp.where(x < -20.0, 1.0, slope_x / jnp.maximum(dt, 1e-12))
    grad_raw = (s2 + s3) * ratio - decay * grad_rate * slope_x
    small_ref[6:7, :STATE] += jnp.sum(grad_raw, axis=0, keepdims=True)
    small_ref[7:8, :STATE] += jnp.sum(grad_rate * rate, axis=0, keepdims=True)
    small_ref[8:9, :STATE] += thin[0:1, :]
    small_ref[5:6, :cw] += jnp.sum(gu * rg, axis=0, keepdims=True)

    grun = jnp.concatenate([grad_x, grad_b, grad_c], 1) * slope
    next_ref[pl.ds(SPAN, 8), :] = next_ref[pl.ds(0, 8), :]
    next_ref[pl.ds(0, SPAN), :] = grun
    small_ref[taps : taps + 1, :] += jnp.sum(grun, axis=0, keepdims=True)
    gbefore = jnp.zeros_like(grun)
    for k in range(taps):
        small_ref[k : k + 1, :] += jnp.sum(
            grun * pad_ref[pl.ds(8 - taps + 1 + k, SPAN), :], axis=0, keepdims=True
        )
        gbefore = gbefore + vec_ref[k : k + 1, :] * next_ref[pl.ds(taps - 1 - k, SPAN), :]
    gpgx = jnp.concatenate([ggate, gbefore[:, :cw]], 1).astype(BF16)
    gps = jnp.concatenate([gbefore[:, cw:], grad_raw], 1).astype(BF16)
    gpgx_ref[...] = gpgx
    gps_ref[...] = gps
    pg_ref[...] = (dot(gpgx, wgx_ref[...], 1, 1) + dot(gps, ws_ref[...], 1, 1)).astype(BF16)


def tables(heads):
    cw = heads * HEAD
    tri = np.tril(np.ones((SPAN, SPAN), np.float32))
    one = (np.arange(cw)[None, :] // HEAD == np.arange(STATE)[:, None]).astype(np.float32)
    spread3 = np.concatenate([one] * 3, 0)
    gather3 = np.concatenate([one.T] * 3, 0)
    return jnp.asarray(tri, BF16), jnp.asarray(spread3, BF16), jnp.asarray(gather3, BF16)


def whole(a):
    return pl.BlockSpec(memory_space=pltpu.VMEM)


def layer_forward(full, wgx, ws, wo, vec, taps, sequences):
    tokens, width = full.shape
    cw = wo.shape[0]
    heads = cw // HEAD
    steps = tokens // SPAN
    blocks = steps // sequences
    tri, spread3, _ = tables(heads)
    rows = lambda w: pl.BlockSpec((SPAN, w), lambda t: (t, 0))
    chans = cw + 2 * STATE
    return pl.pallas_call(
        functools.partial(forward_kernel, heads, blocks, taps),
        grid=(steps,),
        in_specs=[rows(width)] + [whole(a) for a in (wgx, ws, wo, vec, tri, spread3)],
        out_specs=[
            rows(width),
            pl.BlockSpec((1, 8, SPAN), lambda t: (t, 0, 0)),
            rows(2 * cw),
            rows(3 * STATE),
            rows(cw),
            pl.BlockSpec((1, STATE, cw), lambda t: (t, 0, 0)),
        ],
        out_shape=[
            jax.ShapeDtypeStruct((tokens, width), BF16),
            jax.ShapeDtypeStruct((steps, 8, SPAN), F32),
            jax.ShapeDtypeStruct((tokens, 2 * cw), BF16),
            jax.ShapeDtypeStruct((tokens, 3 * STATE), BF16),
            jax.ShapeDtypeStruct((tokens, cw), BF16),
            jax.ShapeDtypeStruct((steps, STATE, cw), BF16),
        ],
        scratch_shapes=[
            pltpu.VMEM((SPAN + 8, chans), F32),
            pltpu.VMEM((STATE, cw), F32),
            pltpu.VMEM((SPAN, cw), F32),
        ],
        compiler_params=pltpu.CompilerParams(vmem_limit_bytes=48 << 20),
        cost_estimate=pl.CostEstimate(
            flops=2 * tokens * width * (3 * cw + 3 * STATE) + 2 * tokens * cw * 700,
            bytes_accessed=4 * tokens * width + 2 * width * (3 * cw + 3 * STATE) + 8 * tokens * cw,
            transcendentals=tokens * SPAN * heads,
        ),
        name="layer_forward",
    )(full, wgx, ws, wo, vec, tri, spread3)


def layer_backward(gb, sc, pgx, ps, res, ent, wgx, ws, wo, vec, taps, sequences):
    tokens, width = gb.shape
    cw = wo.shape[0]
    heads = cw // HEAD
    steps = tokens // SPAN
    blocks = steps // sequences
    tri, spread3, gather3 = tables(heads)
    chans = cw + 2 * STATE

    def at(t):
        return t - lax.rem(t, blocks) + (blocks - 1 - lax.rem(t, blocks))

    rows = lambda w: pl.BlockSpec((SPAN, w), lambda t: (at(t), 0))
    edge = lambda w: pl.BlockSpec((16, w), lambda t: (jnp.maximum(at(t) * (SPAN // 16) - 1, 0), 0))
    return pl.pallas_call(
        functools.partial(backward_kernel, heads, blocks, taps),
        grid=(steps,),
        in_specs=[
            rows(width),
            pl.BlockSpec((1, 8, SPAN), lambda t: (at(t), 0, 0)),
            rows(2 * cw),
            rows(3 * STATE),
            edge(2 * cw),
            edge(3 * STATE),
            rows(cw),
            pl.BlockSpec((1, STATE, cw), lambda t: (at(t), 0, 0)),
        ]
        + [whole(a) for a in (wgx, ws, wo, vec, tri, spread3, gather3)],
        out_specs=[
            rows(width),
            rows(2 * cw),
            rows(3 * STATE),
            rows(cw),
            pl.BlockSpec((16, chans), lambda t: (0, 0)),
        ],
        out_shape=[
            jax.ShapeDtypeStruct((tokens, width), BF16),
            jax.ShapeDtypeStruct((tokens, 2 * cw), BF16),
            jax.ShapeDtypeStruct((tokens, 3 * STATE), BF16),
            jax.ShapeDtypeStruct((tokens, cw), BF16),
            jax.ShapeDtypeStruct((16, chans), F32),
        ],
        scratch_shapes=[
            pltpu.VMEM((SPAN + 8, chans), F32),
            pltpu.VMEM((SPAN + 8, chans), F32),
            pltpu.VMEM((STATE, cw), F32),
            pltpu.VMEM((SPAN, cw), F32),
            pltpu.VMEM((SPAN, cw), F32),
        ],
        compiler_params=pltpu.CompilerParams(vmem_limit_bytes=48 << 20),
        cost_estimate=pl.CostEstimate(
            flops=2 * tokens * width * (3 * cw + 3 * STATE) + 2 * tokens * cw * 2000,
            bytes_accessed=4 * tokens * width + 2 * width * (3 * cw + 3 * STATE) + 8 * tokens * cw,
            transcendentals=tokens * SPAN * heads,
        ),
        name="layer_backward",
    )(gb, sc, pgx, ps, pgx, ps, res, ent, wgx, ws, wo, vec, tri, spread3, gather3)


def swapped(value, axis):
    count = lax.axis_size(axis)
    return lax.ppermute(value, axis, [(i, count - 1 - i) for i in range(count)])


PLANE = ("section", "seq")
EVERY = ("section", "seq", "fsdp")


def per_device(
    section_ends, norm_gain, in_weight, conv_weight, conv_bias, step_bias, log_decay, skip_gain, gate_gain, out_weight
):
    sec, seq, dep = lax.axis_index("section"), lax.axis_index("seq"), lax.axis_index("fsdp")
    layers, ranks, depth = lax.axis_size("section"), lax.axis_size("seq"), lax.axis_size("fsdp")
    group = layers * ranks
    here = sec * ranks + seq
    there = (layers - 1 - sec) * ranks + seq
    low_layer = sec == 0
    width = in_weight.shape[1] * depth
    inner = gate_gain.shape[1] * depth
    chans = conv_bias.shape[1] * depth
    heads_all = step_bias.shape[1] * depth
    taps = conv_weight.shape[1]
    cw = inner // group
    heads = cw // HEAD
    shared = 2 * STATE

    ends = section_ends[0, :, 0]
    sent = jnp.where(low_layer, ends[1], ends[0])
    got = swapped(sent, "section")
    hidden = jnp.where(low_layer, ends[0], got).astype(F32)
    cot = jnp.where(low_layer, got, ends[1]).astype(F32)
    local = hidden.shape[0]

    flat = [norm_gain, conv_weight, conv_bias, step_bias, log_decay, skip_gain, gate_gain]
    sizes = [v.size for v in flat]
    packed = jnp.concatenate([v.reshape(-1) for v in flat])
    packed = lax.all_gather(packed, ("section", "fsdp")).reshape(layers, depth, -1).astype(F32)

    def member(layer, number):
        begin = sum(sizes[:number])
        return packed[layer, :, begin : begin + sizes[number]]

    def head_columns(v, begin, count):
        return lax.dynamic_slice_in_dim(v, begin, count, v.ndim - 1)

    def vectors(layer):
        kernel = jnp.transpose(member(layer, 1).reshape(depth, taps, -1), (1, 0, 2)).reshape(taps, chans)
        rows = jnp.concatenate([kernel, member(layer, 2).reshape(1, chans)], 0)
        rows = jnp.concatenate([head_columns(rows, here * cw, cw), rows[:, inner:]], 1)
        total = cw + shared

        def padded(v):
            return jnp.pad(v[None], ((0, 0), (0, total - v.shape[0])))

        gain = head_columns(member(layer, 6).reshape(-1), here * cw, cw)
        by_head = [head_columns(member(layer, n).reshape(-1), here * heads, heads) for n in (3, 4, 5)]
        return jnp.concatenate(
            [rows, jnp.zeros((5 - taps - 1, total), F32), padded(gain), padded(by_head[0]), padded(by_head[1]),
             padded(jnp.repeat(by_head[2], HEAD)), jnp.zeros((7, total), F32)], 0)

    gains = [member(layer, 0).reshape(1, -1) for layer in range(layers)]
    vecs = [vectors(layer) for layer in range(layers)]

    def own_columns(rank):
        return jnp.concatenate(
            [head_columns(in_weight[0], rank * cw, cw), head_columns(in_weight[0], inner + rank * cw, cw)], 1
        )

    out_rows = out_weight.shape[1]

    def own_rows(rank):
        start = rank * cw - dep * out_rows
        inside = (start >= 0) & (start < out_rows)
        block = lax.dynamic_slice_in_dim(out_weight[0], jnp.clip(start, 0, out_rows - cw), cw, 0)
        return jnp.where(inside, block, jnp.zeros_like(block))

    mine, theirs = own_columns(here), swapped(own_columns(there), "section")
    mine_o, theirs_o = own_rows(here), swapped(own_rows(there), "section")
    piece = in_weight.shape[1] // ranks
    thin = lax.dynamic_slice(in_weight[0], (seq * piece, inner + chans - shared), (piece, shared + heads_all))
    thin = lax.all_gather(thin, ("section", "fsdp", "seq"), axis=0, tiled=True).reshape(layers, width, -1)
    weights = []
    for layer in range(layers):
        own = low_layer if layer == 0 else ~low_layer
        wgx = lax.all_gather(jnp.where(own, mine, theirs), "fsdp", axis=0, tiled=True)
        wo = lax.psum(jnp.where(own, mine_o, theirs_o), "fsdp")
        steps_w = head_columns(thin[layer, :, shared:], here * heads, heads)
        ws = jnp.concatenate([thin[layer, :, :shared], steps_w, jnp.zeros((width, STATE - heads), BF16)], 1)
        weights.append((wgx, ws, wo))

    def spread_rows(v):
        return lax.all_gather(v, PLANE, axis=0, tiled=True)

    def collect_rows(v):
        return lax.psum_scatter(v, PLANE, scatter_dimension=0, tiled=True).astype(F32)

    saved = []
    for layer in range(layers):
        wgx, ws, wo = weights[layer]
        rs = lax.rsqrt(jnp.mean(hidden * hidden, axis=-1, keepdims=True) + EPS)
        full = spread_rows((hidden * rs * gains[layer]).astype(BF16))
        part, ss, pgx, ps, res, ent = layer_forward(full, wgx, ws, wo, vecs[layer], taps, layers)
        raw = collect_rows(part)
        ss = lax.psum_scatter(ss[:, 0, :].reshape(-1), PLANE, scatter_dimension=0, tiled=True)[:, None]
        r = lax.rsqrt(ss / inner + EPS)
        saved.append((hidden, rs, full, pgx, ps, res, ent, raw, r))
        hidden = hidden + r * raw
        if layer + 1 < layers:
            hidden = hidden.astype(BF16).astype(F32)
    output = hidden

    grad = cot
    big, small = [None] * layers, [None] * layers
    for layer in reversed(range(layers)):
        wgx, ws, wo = weights[layer]
        before, rs, full, pgx, ps, res, ent, raw, r = saved[layer]
        low = grad.astype(BF16)
        pull = r * r * r * jnp.sum(low.astype(F32) * raw, axis=-1, keepdims=True) / inner
        sc = jnp.concatenate([r.T, pull.T, jnp.zeros((6, local), F32)], 0)
        gb = spread_rows(low)
        sc = lax.all_gather(sc, PLANE).reshape(-1, 8, local)
        if local != SPAN:
            sc = jnp.transpose(sc.reshape(-1, 8, local // SPAN, SPAN), (0, 2, 1, 3)).reshape(-1, 8, SPAN)
        pg, gpgx, gps, no, tiny = layer_backward(
            gb, sc, pgx, ps, res, ent, wgx, ws, wo, vecs[layer], taps, layers
        )
        g_gx = dot(full, gpgx, 0, 0).astype(BF16)
        g_s = dot(full, gps, 0, 0).astype(BF16)
        g_o = dot(no, gb, 0, 0).astype(BF16)
        gn = collect_rows(pg)
        unit = before * rs
        g_gain = jnp.sum(gn * unit, axis=0)
        gn = gn * gains[layer]
        grad = grad + rs * (gn - unit * jnp.mean(gn * unit, axis=-1, keepdims=True))
        if layer > 0:
            grad = grad.astype(BF16).astype(F32)

        def placed(v, count, begin):
            return lax.dynamic_update_slice(jnp.zeros((count,), F32), v, (begin,))

        conv = lax.dynamic_update_slice(jnp.zeros((taps + 1, chans), F32), tiny[: taps + 1, :cw], (0, here * cw))
        conv = conv + jnp.pad(tiny[: taps + 1, cw:], ((0, 0), (inner, 0)))
        small[layer] = jnp.concatenate(
            [g_gain, conv.reshape(-1), placed(tiny[5, :cw], inner, here * cw)]
            + [placed(tiny[n, :heads], heads_all, here * heads) for n in (6, 7, 8)]
        )
        g_gx = lax.psum_scatter(g_gx, "fsdp", scatter_dimension=0, tiled=True)
        steps_g = lax.dynamic_update_slice(jnp.zeros((width, heads_all), BF16), g_s[:, shared : shared + heads], (0, here * heads))
        g_s = jnp.concatenate([g_s[:, :shared], steps_g], 1)
        g_s = lax.psum_scatter(g_s, "fsdp", scatter_dimension=0, tiled=True)
        g_o = lax.psum(g_o, "fsdp")
        big[layer] = (g_gx, g_s, g_o)

    sent = jnp.where(low_layer, output, grad).astype(BF16)
    got = swapped(sent, "section").astype(F32)
    first = jnp.where(low_layer, grad, got)
    second = jnp.where(low_layer, got, output)
    section_results = jnp.stack([first, second])[None, :, None]

    def own_layer(values):
        own = jnp.where(low_layer, values[0], values[1])
        other = jnp.where(low_layer, values[1], values[0])
        return own, other

    own, other = own_layer([b[0] for b in big])
    other = swapped(other, "section")
    pair = jnp.stack([jnp.where(low_layer, own, other), jnp.where(low_layer, other, own)])
    gx = lax.all_gather(pair, "seq")
    gx = jnp.transpose(gx, (3, 1, 0, 2, 4)) if False else gx
    rows = gx.shape[2]
    gx = gx.reshape(ranks, layers, rows, 2, cw)
    gx = jnp.transpose(gx, (2, 3, 1, 0, 4)).reshape(rows, 2 * inner)
    s_all = lax.psum(jnp.stack([b[1] for b in big]), PLANE)
    s_own, _ = own_layer([s_all[0], s_all[1]])
    grad_in = jnp.concatenate([gx.astype(F32), s_own.astype(F32)], 1)[None]

    own, other = own_layer([b[2] for b in big])
    other = swapped(other, "section")
    pair = jnp.stack([jnp.where(low_layer, own, other), jnp.where(low_layer, other, own)])
    spread = jnp.zeros((out_rows, width), BF16)
    for s in range(layers):
        start = (s * ranks + seq) * cw - dep * out_rows
        inside = (start >= 0) & (start < out_rows)
        block = jnp.where(inside, pair[s], jnp.zeros_like(pair[s]))
        spread = spread + lax.dynamic_update_slice(jnp.zeros_like(spread), block, (jnp.clip(start, 0, out_rows - cw), 0))
    grad_out = lax.psum(spread, "seq").astype(F32)[None]

    tiny = lax.psum(jnp.stack(small), EVERY)
    tiny = jnp.where(low_layer, tiny[0], tiny[1])
    cuts = np.cumsum([0, width, taps * chans, chans, inner, heads_all, heads_all, heads_all])
    parts = [tiny[cuts[i] : cuts[i + 1]] for i in range(7)]

    def share(v):
        count = v.shape[-1] // depth
        return lax.dynamic_slice_in_dim(v, dep * count, count, v.ndim - 1)[None]

    return (
        section_results,
        share(parts[0]),
        grad_in,
        share(parts[1].reshape(taps, chans)),
        share(parts[2]),
        share(parts[4]),
        share(parts[5]),
        share(parts[6]),
        share(parts[3]),
        grad_out,
    )


def solution(mesh):
    weight = P("section", "fsdp")
    matrix = P("section", "fsdp", None)
    ends = P("section", None, "fsdp", "seq", None)
    kernel = P("section", None, "fsdp")
    return jax.shard_map(
        per_device,
        mesh=mesh,
        in_specs=(ends, weight, matrix, kernel, weight, weight, weight, weight, weight, matrix),
        out_specs=(ends, weight, matrix, kernel, weight, weight, weight, weight, weight, matrix),
        check_vma=False,
    )
```

time: 2170 us -> 1270 us (0.59)
  matrix products: 400 us -> 41.6 us
  local copies, waits for them, and re-layouts: 315 us -> 85 us
  Pallas kernels: 0 us -> 166 us
  other arithmetic: 219 us -> 59 us
  blocking collectives: 195 us -> 42.6 us
  starting transfers between devices: 117 us -> 10.2 us
  waiting for transfers between devices: 888 us -> 838 us
    dot_general x72 -> x6, matrix products: 400 us -> 41.6 us  [dot(): lax.dot_general(a, b, (((ca,), (cb,)), ((), ())), preferred_element_type=...]
    psum x1 -> x5, waiting for transfers between devices: 103 us -> 304 us  [the longest x1 122 us: per_device(): wo = lax.psum(jnp.where(own, mine_o, theirs_o), 'fsdp')]
    unnamed x11 -> x25, waiting for transfers between devices: 270 us -> 71.4 us
    pallas_call x0 -> x4, Pallas kernels: none -> 166 us  [the longest x2 110 us: layer_backward(): pl.pallas_call(functools.partial(backward_kernel, heads, blocks, taps), g...]
    all_gather x6 -> x2, blocking collectives: 160 us -> 19.1 us  [per_device(): sc = lax.all_gather(sc, PLANE).reshape(-1, 8, local)]
    reduce_scatter x4 -> x6, waiting for transfers between devices: 158 us -> 294 us  [the longest x4 218 us: collect_rows(): lax.psum_scatter(v, PLANE, scatter_dimension=0, tiled=True).astype(F32)]
    all_gather x2 -> x8, waiting for transfers between devices: 261 us -> 129 us  [the longest x4 98.6 us: spread_rows(): return lax.all_gather(v, PLANE, axis=0, tiled=True)]
    all_to_all x18 -> x0, starting transfers between devices: 93.4 us -> none  [the longest x3 17.6 us: layer_forward(): lax.all_to_all(projected[:, inner_width + channels:], 'seq', split_axis=1...]
  transfers between devices with their start and end apart: 37 -> 28, of which waited for: 15 -> 19; matrix products, arithmetic and copies ran while one was open for 24% -> 9% of each run, Pallas kernels for 0% -> 0%
where the time goes in v1:
time: 1270 us; the launch traced here: 1260 us
  waiting for transfers between devices  838 us (66%)
  Pallas kernels  166 us (13%)
  local copies, waits for them, and re-layouts  85 us (7%)
  other arithmetic  59 us (5%)
  blocking collectives  42.6 us (3%)
  matrix products  41.6 us (3%)
  between operations  18.5 us (1%)
    reduce_scatter x4, waiting for transfers between devices, collect_rows(): lax.psum_scatter(v, PLANE, scatter_dimension=0, tiled=True).astype(F32)  218 us
    psum x1, waiting for transfers between devices, per_device(): wo = lax.psum(jnp.where(own, mine_o, theirs_o), 'fsdp')  122 us
    psum x1, waiting for transfers between devices, per_device(): tiny = lax.psum(jnp.stack(small), EVERY)  116 us
    pallas_call x2, Pallas kernels, layer_backward(): pl.pallas_call(functools.partial(backward_kernel, heads, blocks, taps), g...  110 us
    all_gather x4, waiting for transfers between devices, spread_rows(): return lax.all_gather(v, PLANE, axis=0, tiled=True)  98.6 us
    reduce_scatter x2, waiting for transfers between devices, per_device(): g_gx = lax.psum_scatter(g_gx, 'fsdp', scatter_dimension=0, tiled=True)  75.6 us
    unnamed x25, waiting for transfers between devices  71.4 us
    psum x1, waiting for transfers between devices, per_device(): g_o = lax.psum(g_o, 'fsdp')  59.6 us
  transfers between devices with their start and end apart: 28, of which 19 were waited for; matrix products, arithmetic and copies ran while one was open for 9% of the time, Pallas kernels for 0%

profile of v1, /device:TPU:19, one launch (start us, length us, event | category | flops | bytes accessed | tf_op | source)
XLA Modules:
  0.0 1260.5 jit_solution(3916662465272029035)
XLA Ops:
  21.0 26.7 %collective-permute-done.2 = bf16[384,1536]{1,0:T(8,128)(2,1)} collective-permute-done((bf16[384,1536]{1,0:T(8,128)(2,1)S(1)}, bf16[384,1536]{1,0:T(8,128)(2,1)}, u32[]{:S(2)}, u32[]{:S(2)}) %collective-permute-start.2) | collective-permute-done | bytes 1179680 | tf_op jit(solution)/shard_map/ppermute | solution.py:364
  47.7 3.3 bitcast_select_fusion
  55.1 12.9 %collective-permute-done.1 = bf16[384,768]{1,0:T(8,128)(2,1)S(1)} collective-permute-done((bf16[384,768]{1,0:T(8,128)(2,1)S(1)}, bf16[384,768]{1,0:T(8,128)(2,1)S(1)}, u32[]{:S(2)}, u32[]{:S(2)}) %collective-permute-start.1) | collective-permute-done | bytes 589856 | tf_op jit(solution)/shard_map/ppermute | solution.py:364
  69.5 2.4 collective-permute-start
  71.9 13.9 %all-reduce.28.cloned.1.call-done = bf16[42784]{0:T(1024)(128)(2,1)} async-done(((bf16[42784]{0:T(1024)(128)(2,1)}), bf16[42784]{0:T(1024)(128)(2,1)}) %all-reduce.28.cloned.1.call-update) | async-done | bytes 85584
  93.8 122.4 %all-reduce.32.cloned.1.call-done = (bf16[384,1536]{1,0:T(8,128)(2,1)}, bf16[384,1536]{1,0:T(8,128)(2,1)}) async-done(((bf16[384,1536]{1,0:T(8,128)(2,1)}, bf16[384,1536]{1,0:T(8,128)(2,1)}), (bf16[384,1536]{1,0:T(8,128)(2,1)}, bf16[384,1536]{1,0:T(8,128)(2,1)})) %all-reduce.32.cloned.1.call-update) | async-done | bytes 2359312 | tf_op jit(solution)/shard_map/psum | solution.py:448
  217.5 28.0 %layer_forward.2 = (bf16[2048,1536]{1,0:T(8,128)(2,1)}, f32[8,8,256]{2,1,0:T(8,128)S(1)}, bf16[2048,768]{1,0:T(8,128)(2,1)}, bf16[2048,384]{1,0:T(8,128)(2,1)S(1...) custom-call(bf16[2048,1536]{1,0:T(8,128)(2,1)} %all-gather.14.cloned.1.call-done.full_ref, ...), custom_call_target="tpu_custom_call" | custom-call | flops 10764681216 | bytes 23592960 | tf_op jit(solution)/shard_map/layer_forward/pallas_call | solution.py:268
  249.7 12.0 all-reduce.11
  261.8 47.3 %reduce-scatter.13.cloned.1.call-done = bf16[256,1536]{1,0:T(8,128)(2,1)} async-done(((bf16[2048,1536]{1,0:T(8,128)(2,1)}), bf16[256,1536]{1,0:T(8,128)(2,1)}) %reduce-scatter.13.cloned.1.call-update) | async-done | bytes 786448 | tf_op jit(solution)/shard_map/reduce_scatter | solution.py:457
  314.3 45.0 %all-gather.20.cloned.1.call-done.full_ref = bf16[2048,1536]{1,0:T(8,128)(2,1)} async-done(((bf16[256,1536]{1,0:T(8,128)(2,1)}), bf16[2048,1536]{1,0:T(8,128)(2,1)}) %all-gather.20.cloned.1.call-update) | async-done | bytes 6291472 | tf_op jit(solution)/shard_map/all_gather | solution.py:454
  360.6 28.0 %layer_forward.3 = (bf16[2048,1536]{1,0:T(8,128)(2,1)}, f32[8,8,256]{2,1,0:T(8,128)S(1)}, bf16[2048,768]{1,0:T(8,128)(2,1)}, bf16[2048,384]{1,0:T(8,128)(2,1)S(1...) custom-call(bf16[2048,1536]{1,0:T(8,128)(2,1)} %all-gather.20.cloned.1.call-done.full_ref, ...), custom_call_target="tpu_custom_call" | custom-call | flops 10764681216 | bytes 23592960 | tf_op jit(solution)/shard_map/layer_forward/pallas_call | solution.py:268
  390.8 61.4 %reduce-scatter.15.cloned.1.call-done = bf16[256,1536]{1,0:T(8,128)(2,1)} async-done(((bf16[2048,1536]{1,0:T(8,128)(2,1)}), bf16[256,1536]{1,0:T(8,128)(2,1)}) %reduce-scatter.15.cloned.1.call-update) | async-done | bytes 786448 | tf_op jit(solution)/shard_map/reduce_scatter | solution.py:457
  452.2 2.8 fusion.14
  455.2 11.5 all-reduce.12
  467.4 10.1 all-gather.2
  477.6 23.6 %all-gather.18.cloned.1.call-done.gb_ref = bf16[2048,1536]{1,0:T(8,128)(2,1)} async-done(((bf16[256,1536]{1,0:T(8,128)(2,1)}), bf16[2048,1536]{1,0:T(8,128)(2,1)}) %all-gather.18.cloned.1.call-update) | async-done | bytes 6291472 | tf_op jit(solution)/shard_map/all_gather | solution.py:454
  503.6 54.8 %layer_backward.2 = (bf16[2048,1536]{1,0:T(8,128)(2,1)}, bf16[2048,768]{1,0:T(8,128)(2,1)}, bf16[2048,384]{1,0:T(8,128)(2,1)S(1)}, bf16[2048,384]{1,0:T(8,128)(2,1)}, f32[16,640]{1,0:T(8,128)S(1)}) custom-call(bf16[2048,1536]{1,0:T(8,128)(2,1)} %all-gather.18.cloned.1.call-done.gb_ref, f32[8,8,256]{2,1,0:T(8,128)S(1)} %bitcast.110, ...), custom_call_target="tpu_custom_call" | custom-call | flops 12809404416 | bytes 23592960 | tf_op jit(solution)/shard_map/layer_backward/pallas_call | solution.py:317
  559.7 61.0 %reduce-scatter.17.cloned.1.call-done = bf16[256,1536]{1,0:T(8,128)(2,1)} async-done(((bf16[2048,1536]{1,0:T(8,128)(2,1)}), bf16[256,1536]{1,0:T(8,128)(2,1)}) %reduce-scatter.17.cloned.1.call-update) | async-done | bytes 786448 | tf_op jit(solution)/shard_map/reduce_scatter | solution.py:457
  622.6 3.0 fusion.15
  625.8 7.0 convolution_convert_fusion.2
  633.0 8.9 all-gather.3
  641.9 30.0 %all-gather.24.cloned.1.call-done.gb_ref = bf16[2048,1536]{1,0:T(8,128)(2,1)} async-done(((bf16[256,1536]{1,0:T(8,128)(2,1)}), bf16[2048,1536]{1,0:T(8,128)(2,1)}) %all-gather.24.cloned.1.call-update) | async-done | bytes 6291472 | tf_op jit(solution)/shard_map/all_gather | solution.py:454
  673.0 54.9 %layer_backward.3 = (bf16[2048,1536]{1,0:T(8,128)(2,1)}, bf16[2048,768]{1,0:T(8,128)(2,1)}, bf16[2048,384]{1,0:T(8,128)(2,1)S(1)}, bf16[2048,384]{1,0:T(8,128)(2,1)}, f32[16,640]{1,0:T(8,128)S(1)}) custom-call(bf16[2048,1536]{1,0:T(8,128)(2,1)} %all-gather.24.cloned.1.call-done.gb_ref, f32[8,8,256]{2,1,0:T(8,128)S(1)} %bitcast.109, ...), custom_call_target="tpu_custom_call" | custom-call | flops 12809404416 | bytes 23592960 | tf_op jit(solution)/shard_map/layer_backward/pallas_call | solution.py:317
  729.1 5.1 convolution_convert_fusion.3
  735.6 5.4 convolution_convert_fusion.4
  743.1 5.4 convolution_convert_fusion.5
  750.5 9.4 convolution_convert_fusion
  760.0 9.3 convolution_convert_fusion.1
  769.3 59.6 %all-reduce.30.cloned.1.call-done = (bf16[384,1536]{1,0:T(8,128)(2,1)}, bf16[384,1536]{1,0:T(8,128)(2,1)}) async-done(((bf16[384,1536]{1,0:T(8,128)(2,1)}, bf16[384,1536]{1,0:T(8,128)(2,1)}), (bf16[384,1536]{1,0:T(8,128)(2,1)}, bf16[384,1536]{1,0:T(8,128)(2,1)})) %all-reduce.30.cloned.1.call-update) | async-done | bytes 2359312 | tf_op jit(solution)/shard_map/psum | solution.py:513
  829.0 2.4 broadcast_select_fusion
  832.6 26.8 %reduce-scatter.27.cloned.1.call-done = bf16[384,304]{1,0:T(8,128)(2,1)} async-done(((bf16[1536,304]{1,0:T(8,128)(2,1)}), bf16[384,304]{1,0:T(8,128)(2,1)}) %reduce-scatter.27.cloned.1.call-update) | async-done | bytes 233488
  860.5 29.2 %reduce-scatter.25.cloned.1.call-done = bf16[384,304]{1,0:T(8,128)(2,1)} async-done(((bf16[1536,304]{1,0:T(8,128)(2,1)}), bf16[384,304]{1,0:T(8,128)(2,1)}) %reduce-scatter.25.cloned.1.call-update) | async-done | bytes 233488
  893.5 7.7 dynamic_update_slice.56
  901.1 3.5 add_bitcast_fusion
  904.6 7.1 add.210
  915.0 25.1 %reduce-scatter.23.cloned.1.call-done = bf16[384,768]{1,0:T(8,128)(2,1)} async-done(((bf16[1536,768]{1,0:T(8,128)(2,1)}), bf16[384,768]{1,0:T(8,128)(2,1)}) %reduce-scatter.23.cloned.1.call-update) | async-done | bytes 589840 | tf_op jit(solution)/shard_map/reduce_scatter | solution.py:509
  940.1 50.5 %reduce-scatter.21.cloned.1.call-done = bf16[384,768]{1,0:T(8,128)(2,1)} async-done(((bf16[1536,768]{1,0:T(8,128)(2,1)}), bf16[384,768]{1,0:T(8,128)(2,1)}) %reduce-scatter.21.cloned.1.call-update) | async-done | bytes 589840 | tf_op jit(solution)/shard_map/reduce_scatter | solution.py:509
  996.5 5.7 all-reduce.26.cloned.1.call-done
  1002.2 5.0 broadcast_in_dim.69
  1008.3 48.2 %reduce-scatter.19.cloned.1.call-done = bf16[256,1536]{1,0:T(8,128)(2,1)} async-done(((bf16[2048,1536]{1,0:T(8,128)(2,1)}), bf16[256,1536]{1,0:T(8,128)(2,1)}) %reduce-scatter.19.cloned.1.call-update) | async-done | bytes 786448 | tf_op jit(solution)/shard_map/reduce_scatter | solution.py:457
  1056.5 2.4 fusion.20
  1060.6 2.5 pad_maximum_fusion
  1063.2 3.1 select_convert_fusion
  1066.6 116.2 %all-reduce.22.cloned.1.call-done = f32[2,21392]{1,0:T(2,128)} async-done(((f32[2,21392]{1,0:T(2,128)}), f32[2,21392]{1,0:T(2,128)}) %all-reduce.22.cloned.1.call-update) | async-done | bytes 171152 | tf_op jit(solution)/shard_map/psum | solution.py:550
  1192.6 30.6 %all-gather.28.cloned.1.call-done = bf16[8,384,768]{2,1,0:T(8,128)(2,1)} async-done(((bf16[2,384,768]{2,1,0:T(8,128)(2,1)}), bf16[8,384,768]{2,1,0:T(8,128)(2,1)}) %all-gather.28.cloned.1.call-update) | async-done | bytes 4718608 | tf_op jit(solution)/shard_map/all_gather | solution.py:530
  1223.2 10.1 convert_element_type.116
  1233.3 12.4 copy.46
  1245.8 6.9 fusion
  (313 shorter events, 81.4 us)
Async XLA Ops:
  8.0 39.7 %copy-start.31 = (bf16[1,768,1536]{2,1,0:T(8,128)(2,1)S(1)}, bf16[1,768,1536]{2,1,0:T(8,128)(2,1)}, u32[]{:S(2)}) copy-start(bf16[1,768,1536]{2,1,0:T(8,128)(2,1)} %param.29) | copy-start | bytes 7077892
  8.0 77.7 %all-reduce.28.cloned.1.call-start = ((), (), s32[]{:S(2)}) async-start(), calls=%async_computation.25 | async-start | bytes 172032
  16.2 75.0 %all-gather.26.cloned.1.call-start = ((), (), s32[]{:S(2)}) async-start(), calls=%async_computation.23 | async-start | bytes 2433024 | tf_op jit(solution)/shard_map/all_gather | solution.py:443
  18.0 198.2 %all-reduce.32.cloned.1.call-start = ((), (), s32[]{:S(2)}) async-start(), calls=%async_computation.29 | async-start | bytes 4718592 | tf_op jit(solution)/shard_map/psum | solution.py:448
  19.7 28.0 %collective-permute-start.2 = (bf16[384,1536]{1,0:T(8,128)(2,1)S(1)}, bf16[384,1536]{1,0:T(8,128)(2,1)}, u32[]{:S(2)}, u32[]{:S(2)}) collective-permute-start(bf16[384,1536]{1,0:T(8,128)(2,1)S(1)} %select_bitcast_fusion), channel_id=1, source_target_pairs={{0,16},{16,0},{1,17},{17,1},{2,18},{18,2},{3,19},{19,3},{4,20},{20... | collective-permute-start | bytes 3538952 | tf_op jit(solution)/shard_map/ppermute | solution.py:364
  51.0 165.2 %all-gather.16.cloned.1.call-start = ((), (), s32[]{:S(2)}) async-start(), calls=%async_computation.9 | async-start | bytes 2949120 | tf_op jit(solution)/shard_map/all_gather | solution.py:447
  53.0 15.1 %collective-permute-start.1 = (bf16[384,768]{1,0:T(8,128)(2,1)S(1)}, bf16[384,768]{1,0:T(8,128)(2,1)S(1)}, u32[]{:S(2)}, u32[]{:S(2)}) collective-permute-start(bf16[384,768]{1,0:T(8,128)(2,1)S(1)} %pad_maximum_fusion.4), channel_id=1, source_target_pairs={{0,16},{16,0},{1,17},{17,1},{2,18},{18,2},{3,19},{19,3},{4,20},{20... | collective-permute-start | bytes 1769480 | tf_op jit(solution)/shard_map/ppermute | solution.py:364
  55.1 14.3 %copy-start.27 = (bf16[1,2,1,256,1536]{4,3,2,1,0:T(8,128)(2,1)S(1)}, bf16[1,2,1,256,1536]{4,3,2,1,0:T(8,128)(2,1)}, u32[]{:S(2)}) copy-start(bf16[1,2,1,256,1536]{4,3,2,1,0:T(8,128)(2,1)} %param.20) | copy-start | bytes 4718596
  69.3 146.9 %all-gather.14.cloned.1.call-start = ((), (), s32[]{:S(2)}) async-start(), calls=%async_computation.8 | async-start | bytes 7077888 | tf_op jit(solution)/shard_map/all_gather | solution.py:454
  69.5 17.4 %collective-permute-start = (bf16[256,1536]{1,0:T(8,128)(2,1)S(1)}, bf16[256,1536]{1,0:T(8,128)(2,1)S(1)}, u32[]{:S(2)}, u32[]{:S(2)}) collective-permute-start(bf16[256,1536]{1,0:T(8,128)(2,1)S(1)} %bitcast_select_fusion.3), channel_id=1, source_target_pairs={{0,16},{16,0},{1,17},{17,1},{2,18},{18,2},{3,19},{19,3},{4,20},{20... | collective-permute-start | bytes 2359304 | tf_op jit(solution)/shard_map/ppermute | solution.py:364
  89.3 219.9 %reduce-scatter.13.cloned.1.call-start = ((), (), s32[]{:S(2)}) async-start(), calls=%async_computation.10 | async-start | bytes 7077888 | tf_op jit(solution)/shard_map/reduce_scatter | solution.py:457
  93.2 123.0 %copy-start.4 = (bf16[384,384]{1,0:T(8,128)(2,1)S(1)}, bf16[384,384]{1,0:T(8,128)(2,1)}, u32[]{:S(2)}) copy-start(bf16[384,384]{1,0:T(8,128)(2,1)} %constant.99.clone.spread_ref) | copy-start | bytes 884740
  93.2 123.0 %copy-start.6 = (bf16[256,256]{1,0:T(8,128)(2,1)S(1)}, bf16[256,256]{1,0:T(8,128)(2,1)}, u32[]{:S(2)}) copy-start(bf16[256,256]{1,0:T(8,128)(2,1)} %constant.98.clone.tri_ref) | copy-start | bytes 393220
  247.7 66.7 %all-gather.22.cloned.1.call-start = ((), (), s32[]{:S(2)}) async-start(), calls=%async_computation.13 | async-start | bytes 2949120 | tf_op jit(solution)/shard_map/all_gather | solution.py:447
  248.4 110.9 %all-gather.20.cloned.1.call-start = ((), (), s32[]{:S(2)}) async-start(), calls=%async_computation.12 | async-start | bytes 7077888 | tf_op jit(solution)/shard_map/all_gather | solution.py:454
  313.0 139.1 %reduce-scatter.15.cloned.1.call-start = ((), (), s32[]{:S(2)}) async-start(), calls=%async_computation.14 | async-start | bytes 7077888 | tf_op jit(solution)/shard_map/reduce_scatter | solution.py:457
  390.7 110.5 %copy-start.5 = (bf16[1152,128]{1,0:T(8,128)(2,1)S(1)}, bf16[1152,128]{1,0:T(8,128)(2,1)}, u32[]{:S(2)}) copy-start(bf16[1152,128]{1,0:T(8,128)(2,1)} %constant.100.clone.gather_ref) | copy-start | bytes 884740
  390.8 110.4 %all-gather.18.cloned.1.call-start = ((), (), s32[]{:S(2)}) async-start(), calls=%async_computation.11 | async-start | bytes 7077888 | tf_op jit(solution)/shard_map/all_gather | solution.py:454
  455.0 165.7 %reduce-scatter.17.cloned.1.call-start = ((), (), s32[]{:S(2)}) async-start(), calls=%async_computation.15 | async-start | bytes 7077888 | tf_op jit(solution)/shard_map/reduce_scatter | solution.py:457
  559.6 61.1 %copy-start.20 = (bf16[256,1536]{1,0:T(8,128)(2,1)S(1)}, bf16[256,1536]{1,0:T(8,128)(2,1)}, u32[]{:S(2)}) copy-start(bf16[256,1536]{1,0:T(8,128)(2,1)} %copy-done.19) | copy-start | bytes 2359300
  559.6 112.3 %all-gather.24.cloned.1.call-start = ((), (), s32[]{:S(2)}) async-start(), calls=%async_computation.16 | async-start | bytes 7077888 | tf_op jit(solution)/shard_map/all_gather | solution.py:454
  625.6 203.4 %all-reduce.30.cloned.1.call-start = ((), (), s32[]{:S(2)}) async-start(), calls=%async_computation.28 | async-start | bytes 4718592 | tf_op jit(solution)/shard_map/psum | solution.py:513
  625.8 46.1 %copy-start.1 = (bf16[384,1536]{1,0:T(8,128)(2,1)S(1)}, bf16[384,1536]{1,0:T(8,128)(2,1)}, u32[]{:S(2)}) copy-start(bf16[384,1536]{1,0:T(8,128)(2,1)} %get-tuple-element.80.wo_ref) | copy-start | bytes 3538948
  673.0 56.1 %copy-start.45 = (bf16[2048,1536]{1,0:T(8,128)(2,1)S(1)}, bf16[2048,1536]{1,0:T(8,128)(2,1)}, u32[]{:S(2)}) copy-start(bf16[2048,1536]{1,0:T(8,128)(2,1)} %all-gather.24.cloned.1.call-done.gb_ref) | copy-start | bytes 18874372
  734.2 125.2 %reduce-scatter.27.cloned.1.call-start = ((), (), s32[]{:S(2)}) async-start(), calls=%async_computation.27 | async-start | bytes 1474560
  742.9 146.8 %reduce-scatter.25.cloned.1.call-start = ((), (), s32[]{:S(2)}) async-start(), calls=%async_computation.26 | async-start | bytes 1474560
  750.4 189.7 %reduce-scatter.23.cloned.1.call-start = ((), (), s32[]{:S(2)}) async-start(), calls=%async_computation.20 | async-start | bytes 2949120 | tf_op jit(solution)/shard_map/reduce_scatter | solution.py:509
  750.5 9.5 copy-start.47
  759.9 230.7 %reduce-scatter.21.cloned.1.call-start = ((), (), s32[]{:S(2)}) async-start(), calls=%async_computation.19 | async-start | bytes 2949120 | tf_op jit(solution)/shard_map/reduce_scatter | solution.py:509
  769.3 226.1 %all-reduce.24.cloned.1.call-start = ((), (), s32[]{:S(2)}) async-start(), calls=%async_computation.21 | async-start | bytes 933888 | tf_op jit(solution)/shard_map/psum | solution.py:535
  831.4 60.7 %copy-start.24 = (bf16[384,1536]{1,0:T(8,128)(2,1)S(1)}, bf16[384,1536]{1,0:T(8,128)(2,1)}, u32[]{:S(2)}) copy-start(bf16[384,1536]{1,0:T(8,128)(2,1)} %get-tuple-element.78) | copy-start | bytes 3538948
  831.4 60.7 %copy-start.25 = (bf16[384,1536]{1,0:T(8,128)(2,1)S(1)}, bf16[384,1536]{1,0:T(8,128)(2,1)}, u32[]{:S(2)}) copy-start(bf16[384,1536]{1,0:T(8,128)(2,1)} %get-tuple-element.79) | copy-start | bytes 3538948
  831.4 60.7 %collective-permute-start.5 = (bf16[384,1536]{1,0:T(8,128)(2,1)}, bf16[384,1536]{1,0:T(8,128)(2,1)}, u32[]{:S(2)}, u32[]{:S(2)}) collective-permute-start(bf16[384,1536]{1,0:T(8,128)(2,1)} %broadcast_select_fusion), channel_id=1, source_target_pairs={{0,16},{16,0},{1,17},{17,1},{2,18},{18,2},{3,19},{19,3},{4,20},{20... | collective-permute-start | bytes 3538952 | tf_op jit(solution)/shard_map/ppermute | solution.py:364
  891.7 110.4 %all-reduce.26.cloned.1.call-start = ((), (), s32[]{:S(2)}) async-start(), calls=%async_computation.22 | async-start | bytes 4718592 | tf_op jit(solution)/shard_map/psum | solution.py:548
  913.2 143.3 %reduce-scatter.19.cloned.1.call-start = ((), (), s32[]{:S(2)}) async-start(), calls=%async_computation.17 | async-start | bytes 7077888 | tf_op jit(solution)/shard_map/reduce_scatter | solution.py:457
  913.8 269.0 %all-reduce.22.cloned.1.call-start = ((), (), s32[]{:S(2)}) async-start(), calls=%async_computation.18 | async-start | bytes 344064 | tf_op jit(solution)/shard_map/psum | solution.py:550
  915.0 87.2 %copy-start.43 = (f32[48]{0:T(128)}, f32[48]{0:T(128)S(1)}, u32[]{:S(2)}) copy-start(f32[48]{0:T(128)S(1)} %bitcast_dynamic-update-slice_fusion.3) | copy-start | bytes 580
  991.8 15.4 %collective-permute-start.4 = (bf16[384,768]{1,0:T(8,128)(2,1)S(1)}, bf16[384,768]{1,0:T(8,128)(2,1)S(1)}, u32[]{:S(2)}, u32[]{:S(2)}) collective-permute-start(bf16[384,768]{1,0:T(8,128)(2,1)S(1)} %broadcast_select_fusion.3), channel_id=1, source_target_pairs={{0,16},{16,0},{1,17},{17,1},{2,18},{18,2},{3,19},{19,3},{4,20},{20... | collective-permute-start | bytes 1769480 | tf_op jit(solution)/shard_map/ppermute | solution.py:364
  996.5 10.7 copy-start.32
  996.5 10.7 copy-start.33
  1007.1 49.4 %copy-start.18 = (bf16[256,1536]{1,0:T(8,128)(2,1)S(1)}, bf16[256,1536]{1,0:T(8,128)(2,1)}, u32[]{:S(2)}) copy-start(bf16[256,1536]{1,0:T(8,128)(2,1)} %copy-done.17) | copy-start | bytes 2359300
  1007.2 49.3 %copy-start.36 = (f32[256]{0:T(256)S(1)}, f32[256]{0:T(256)}, u32[]{:S(2)}) copy-start(f32[256]{0:T(256)} %copy-done.35) | copy-start | bytes 3076
  1007.2 51.7 %copy-start.42 = (f32[48]{0:T(128)S(1)}, f32[48]{0:T(128)}, u32[]{:S(2)}) copy-start(f32[48]{0:T(128)} %copy-done.41) | copy-start | bytes 580
  1007.2 51.7 %copy-start.44 = (f32[48]{0:T(128)S(1)}, f32[48]{0:T(128)}, u32[]{:S(2)}) copy-start(f32[48]{0:T(128)} %copy-done.43) | copy-start | bytes 580
  1060.5 162.8 %all-gather.28.cloned.1.call-start = ((), (), s32[]{:S(2)}) async-start(), calls=%async_computation.24 | async-start | bytes 5898240 | tf_op jit(solution)/shard_map/all_gather | solution.py:530
  1060.5 2.6 copy-start.21
  1060.5 2.6 copy-start.23
  1066.3 122.2 %collective-permute-start.3 = (bf16[256,1536]{1,0:T(8,128)(2,1)}, bf16[256,1536]{1,0:T(8,128)(2,1)}, u32[]{:S(2)}, u32[]{:S(2)}) collective-permute-start(bf16[256,1536]{1,0:T(8,128)(2,1)} %select_convert_fusion), channel_id=1, source_target_pairs={{0,16},{16,0},{1,17},{17,1},{2,18},{18,2},{3,19},{19,3},{4,20},{20... | collective-permute-start | bytes 2359304 | tf_op jit(solution)/shard_map/ppermute | solution.py:364
  (28 other events, 40.7 us)
Sparse Core Ops, SparseCore 0:
  16.3 69.3 all-reduce.27
  89.3 126.8 all-reduce.31
  250.1 49.2 all-gather.21
  313.1 46.0 all-gather.19
  390.9 61.2 reduce-scatter.14
  455.1 46.0 all-gather.17
  734.3 94.6 all-reduce.29
  831.4 27.9 reduce-scatter.26
  861.8 27.8 reduce-scatter.24
  892.6 47.5 reduce-scatter.22
  943.1 47.5 reduce-scatter.20
  994.8 61.6 reduce-scatter.18
Sparse Core Ops, SparseCore 1:
  19.6 58.8 all-gather.25
  79.9 74.7 all-gather.15
  157.0 47.2 all-gather.13
  247.7 61.3 reduce-scatter.12
  559.7 60.9 reduce-scatter.16
  625.7 46.2 all-gather.23
  891.8 52.2 all-reduce.23
  946.4 55.7 all-reduce.25
  1060.5 122.2 all-reduce.21
  1185.0 38.2 all-gather.27

commit v2 on v1

--- a/solution.py
+++ b/solution.py
@@ -70,21 +70,263 @@
     return cols <= rows
 
 
+MESH = pl.DeviceIdType.MESH
+
+
+class Plane:
+    def __init__(self, layers, ranks):
+        self.layers, self.ranks = layers, ranks
+        self.sec, self.seq = lax.axis_index("section"), lax.axis_index("seq")
+        self.low = lax.rem(self.seq, 2)
+        count = ranks.bit_length() - 1
+        outer = list(range(1, count + 1))
+        self.size = layers * ranks
+        self.orders = (outer, outer[::-1])
+        self.stages = len(outer)
+        self.masks = [m for m in range(self.size) if m % 2 == 0]
+
+    def weight(self, dim):
+        return 1 if dim == 0 else 1 << (dim - 1)
+
+    def flipped(self, dim):
+        w = self.weight(dim)
+        return self.seq + (1 - 2 * lax.rem(self.seq // w, 2)) * w
+
+    def partner(self, dim):
+        if dim == 1:
+            return {"section": self.layers - 1 - self.sec}
+        return {"seq": self.flipped(dim)}
+
+    def owner(self, mask):
+        seq = self.seq
+        for dim in range(self.stages + 1):
+            if dim != 1 and mask >> dim & 1:
+                w = self.weight(dim)
+                seq = seq + (1 - 2 * lax.rem(self.seq // w, 2)) * w
+        sec = self.layers - 1 - self.sec if mask & 2 else self.sec
+        return sec, seq
+
+    def device(self, mask):
+        sec, seq = self.owner(mask)
+        return {"section": sec, "seq": seq}
+
+    def arrival(self, half, mask):
+        order = self.orders[half]
+        return max(i for i, dim in enumerate(order) if mask >> dim & 1)
+
+    def barrier(self):
+        sem = pltpu.get_barrier_semaphore()
+        for mask in range(1, self.size):
+            pl.semaphore_signal(sem, inc=1, device_id=self.device(mask), device_id_type=MESH)
+        pl.semaphore_wait(sem, self.size - 1)
+
+
+class Spread:
+    def __init__(self, plane, ref, start, rows, send, recv):
+        self.plane, self.ref, self.start, self.rows, self.send, self.recv = plane, ref, start, rows, send, recv
+
+    def view(self, half, mask):
+        sec, seq = self.plane.owner(mask)
+        count = self.rows // 2
+        return self.ref.at[pl.ds(pl.multiple_of(self.start(sec, seq) + half * count, 16), count), :]
+
+    def copy(self, half, mask, dim):
+        view = self.view(half, mask)
+        key = mask ^ (1 << dim)
+        return pltpu.make_async_remote_copy(
+            src_ref=view, dst_ref=view, send_sem=self.send.at[half, key], recv_sem=self.recv.at[half, key],
+            device_id=self.plane.partner(dim), device_id_type=MESH,
+        )
+
+    def arrived(self, half, mask):
+        view = self.view(half, mask)
+        pltpu.make_async_remote_copy(
+            src_ref=view, dst_ref=view, send_sem=self.send.at[half, mask], recv_sem=self.recv.at[half, mask],
+            device_id=self.plane.partner(0), device_id_type=MESH,
+        ).wait_recv()
+
+    def begin(self):
+        for stage in range(self.plane.stages):
+            for half in (0, 1):
+                self.copy(half, 0, self.plane.orders[half][stage]).start()
+        for half in (0, 1):
+            self.copy(half, 0, 0).start()
+
+    def hop(self, stage):
+        for half in (0, 1):
+            order = self.plane.orders[half]
+            for mask in self.plane.masks[1:]:
+                if self.plane.arrival(half, mask) == stage:
+                    self.arrived(half, mask)
+                    for later in order[stage + 1 :]:
+                        self.copy(half, mask, later).start()
+                    self.copy(half, mask, 0).start()
+
+    def finish(self):
+        for half in (0, 1):
+            for mask in self.plane.masks:
+                self.arrived(half, mask + 1)
+
+    def drain(self):
+        for half in (0, 1):
+            for mask in range(1, self.plane.size):
+                self.copy(half, mask ^ 1, 0).wait_send()
+
+
+class Collect:
+    def __init__(self, plane, ref, base, blocks, core_in, stage_in, core_send, core_recv, send, recv):
+        self.plane, self.ref, self.base, self.blocks = plane, ref, base, blocks
+        self.core_in, self.stage_in = core_in, stage_in
+        self.core_send, self.core_recv, self.send, self.recv = core_send, core_recv, send, recv
+
+    def core_copy(self, c):
+        return pltpu.make_async_remote_copy(
+            src_ref=self.ref.at[pl.ds(self.base + c * SPAN, SPAN), :], dst_ref=self.core_in.at[c // 2],
+            send_sem=self.core_send.at[c], recv_sem=self.core_recv.at[c],
+            device_id=self.plane.partner(0), device_id_type=MESH,
+        )
+
+    def block_done(self, c):
+        @pl.when(self.plane.low != c % 2)
+        def _():
+            self.core_copy(c).start()
+
+    def block_add(self, c):
+        @pl.when(self.plane.low == c % 2)
+        def _():
+            self.core_copy(c).wait_recv()
+            rows = pl.ds(self.base + c * SPAN, SPAN)
+            self.ref[rows, :] = (self.ref[rows, :].astype(F32) + self.core_in[c // 2].astype(F32)).astype(BF16)
+
+    def rows(self, half, mask):
+        sec, seq = self.plane.owner(mask)
+        count = SPAN // self.plane.layers // 2
+        begin = self.base + seq * SPAN + sec * (2 * count) + half * count
+        return pl.ds(pl.multiple_of(begin, 16), count)
+
+    def copy(self, half, mask, dim):
+        return pltpu.make_async_remote_copy(
+            src_ref=self.ref.at[self.rows(half, mask), :], dst_ref=self.stage_in.at[half, mask // 2],
+            send_sem=self.send.at[half, mask // 2], recv_sem=self.recv.at[half, mask // 2],
+            device_id=self.plane.partner(dim), device_id_type=MESH,
+        )
+
+    def plan(self, stage):
+        for half in (0, 1):
+            order = self.plane.orders[half][::-1]
+            for mask in self.plane.masks[1:]:
+                if mask >> order[stage] & 1 and not any(mask >> dim & 1 for dim in order[:stage]):
+                    yield half, mask, order[stage]
+
+    def begin(self, stage):
+        for half, mask, dim in self.plan(stage):
+            self.copy(half, mask, dim).start()
+
+    def add(self, stage, out_ref=None, out_base=0):
+        for half, mask, dim in self.plan(stage):
+            self.copy(half, mask, dim).wait_recv()
+            rows = self.rows(half, mask ^ (1 << dim))
+            value = self.ref[rows, :].astype(F32) + self.stage_in[half, mask // 2].astype(F32)
+            if stage == self.plane.stages - 1:
+                count = value.shape[0]
+                out_ref[pl.ds(out_base + half * count, count), :] = value
+            else:
+                self.ref[rows, :] = value.astype(BF16)
+
+    def drain(self):
+        for c in range(self.blocks):
+            @pl.when(self.plane.low != c % 2)
+            def _(c=c):
+                self.core_copy(c).wait_send()
+
+        for stage in range(self.plane.stages):
+            for half, mask, dim in self.plan(stage):
+                self.copy(half, mask, dim).wait_send()
+
+
+class Share:
+    def __init__(self, plane, source, target, send, recv):
+        self.plane, self.source, self.target, self.send, self.recv = plane, source, target, send, recv
+
+    def copy(self, mask):
+        return pltpu.make_async_remote_copy(
+            src_ref=self.source, dst_ref=self.target(mask), send_sem=self.send.at[mask],
+            recv_sem=self.recv.at[mask], device_id=self.plane.device(mask), device_id_type=MESH,
+        )
+
+    def begin(self):
+        for mask in range(1, self.plane.size):
+            self.copy(mask).start()
+
+    def finish(self):
+        for mask in range(1, self.plane.size):
+            self.copy(mask).wait_recv()
+
+    def drain(self):
+        for mask in range(1, self.plane.size):
+            self.copy(mask).wait_send()
+
+
 def forward_kernel(
-    heads, blocks, taps,
-    full_ref, wgx_ref, ws_ref, wo_ref, vec_ref, tri_ref, spread_ref,
-    part_ref, ss_ref, pgx_ref, ps_ref, res_ref, ent_ref,
-    pad_ref, state_ref, within_ref,
+    layers, heads, blocks, taps,
+    own_ref, wgx_ref, ws_ref, wo_ref, vec_ref, tri_ref, spread_ref,
+    raw_ref, ss_ref, pgx_ref, ps_ref, res_ref, ent_ref, full_out_ref,
+    full_ref, part_ref, pad_ref, state_ref, within_ref, ss_mine, ss_in, core_in, stage_in,
+    out_sem, ag_send, ag_recv, core_send, core_recv, rs_send, rs_recv, ss_send, ss_recv,
 ):
     cw = heads * HEAD
-    first = lax.rem(pl.program_id(0), blocks) == 0
+    t = pl.program_id(0)
+    steps = layers * blocks
+    plane = Plane(layers, blocks)
+    piece = SPAN // layers
+    length = blocks * SPAN
+
+    def start(m):
+        return lambda sec, seq: m * length + seq * SPAN + sec * piece
+
+    gathers = [Spread(plane, full_ref, start(m), piece, ag_send.at[m], ag_recv.at[m]) for m in range(layers)]
+    sums = [
+        Collect(plane, part_ref, m * length, blocks, core_in.at[m], stage_in.at[m], core_send.at[m], core_recv.at[m],
+                rs_send.at[m], rs_recv.at[m])
+        for m in range(layers)
+    ]
+    shares = [
+        Share(plane, ss_mine.at[m], lambda mask, m=m: ss_in.at[m, mask], ss_send.at[m], ss_recv.at[m])
+        for m in range(layers)
+    ]
+
+    def keep(m):
+        rows = pl.ds(m * length, length)
+        return pltpu.make_async_copy(full_ref.at[rows, :], full_out_ref.at[rows, :], out_sem.at[m])
+
+    @pl.when(t == 0)
+    def _():
+        for m in range(layers):
+            rows = pl.multiple_of(start(m)(plane.sec, plane.seq), 16)
+            full_ref[pl.ds(rows, piece), :] = own_ref[m * piece : (m + 1) * piece, :]
+        ss_mine[...] = jnp.zeros_like(ss_mine)
+        plane.barrier()
+        gathers[0].begin()
+        gathers[0].hop(0)
+        gathers[1].begin()
+        for stage in range(1, plane.stages):
+            gathers[0].hop(stage)
+        gathers[0].finish()
+        keep(0).start()
+
+    @pl.when(t == blocks)
+    def _():
+        gathers[1].finish()
+        keep(1).start()
+
+    first = lax.rem(t, blocks) == 0
 
     @pl.when(first)
     def _():
         pad_ref[pl.ds(SPAN, 8), :] = jnp.zeros((8, pad_ref.shape[1]), F32)
         state_ref[...] = jnp.zeros_like(state_ref)
 
-    x = full_ref[...]
+    x = full_ref[pl.ds(pl.multiple_of(t * SPAN, SPAN), SPAN), :]
     pgx = dot(x, wgx_ref[...], 1, 0).astype(BF16)
     ps = dot(x, ws_ref[...], 1, 0).astype(BF16)
     pgx_ref[...] = pgx
@@ -117,8 +359,65 @@
     gate = pgx[:, :cw].astype(F32)
     g = result.astype(F32) * (gate * sigmoid(gate))
     ss = jnp.sum(g * g, axis=1, keepdims=True)
-    ss_ref[0] = jnp.broadcast_to(ss, (SPAN, STATE)).T[:8, :]
-    part_ref[...] = dot((g * vec_ref[5:6, :cw]).astype(BF16), wo_ref[...], 1, 0).astype(BF16)
+    ss_mine[t // blocks, pl.ds(lax.rem(t, blocks), 1), :] = jnp.broadcast_to(ss, (SPAN, STATE)).T[0:1, :]
+    part_ref[pl.ds(pl.multiple_of(t * SPAN, SPAN), SPAN), :] = dot(
+        (g * vec_ref[5:6, :cw]).astype(BF16), wo_ref[...], 1, 0
+    ).astype(BF16)
+
+    for m in range(layers):
+        for c in range(blocks):
+            @pl.when(t == m * blocks + c)
+            def _(m=m, c=c):
+                sums[m].block_done(c)
+
+    for stage in range(plane.stages):
+        @pl.when(t == min(stage * 2, blocks - 1))
+        def _(stage=stage):
+            gathers[1].hop(stage)
+
+    @pl.when(t == blocks - 1)
+    def _():
+        shares[0].begin()
+
+    @pl.when(t == blocks)
+    def _():
+        for c in range(blocks):
+            sums[0].block_add(c)
+        sums[0].begin(0)
+
+    for stage in range(plane.stages):
+        @pl.when(t == blocks + 1 + stage)
+        def _(stage=stage):
+            sums[0].add(stage, raw_ref, 0)
+            if stage + 1 < plane.stages:
+                sums[0].begin(stage + 1)
+
+    for c in range(blocks - 1):
+        @pl.when(t == blocks + c + 1)
+        def _(c=c):
+            sums[1].block_add(c)
+
+    @pl.when(t == steps - 1)
+    def _():
+        shares[1].begin()
+        sums[1].block_add(blocks - 1)
+        sums[1].begin(0)
+        for m in range(layers):
+            shares[m].finish()
+            total = ss_mine[m]
+            for mask in range(1, plane.size):
+                total = total + ss_in[m, mask]
+            ss_ref[m] = total
+        for m in range(layers):
+            gathers[m].drain()
+            keep(m).wait()
+            shares[m].drain()
+        sums[0].drain()
+        for stage in range(plane.stages):
+            sums[1].add(stage, raw_ref, piece)
+            if stage + 1 < plane.stages:
+                sums[1].begin(stage + 1)
+        sums[1].drain()
 
 
 def backward_kernel(
@@ -256,48 +555,77 @@
     return pl.BlockSpec(memory_space=pltpu.VMEM)
 
 
-def layer_forward(full, wgx, ws, wo, vec, taps, sequences):
-    tokens, width = full.shape
+def plane_scratch(layers, blocks, width):
+    size, piece = layers * blocks, SPAN // layers
+    dma = pltpu.SemaphoreType.DMA
+    return [
+        pltpu.VMEM((layers, blocks // 2, SPAN, width), BF16),
+        pltpu.VMEM((layers, 2, size // 2, piece // 2, width), BF16),
+        dma((layers,)),
+        dma((layers, 2, size)),
+        dma((layers, 2, size)),
+        dma((layers, blocks)),
+        dma((layers, blocks)),
+        dma((layers, 2, size // 2)),
+        dma((layers, 2, size // 2)),
+    ]
+
+
+def layer_forward(own, wgx, ws, wo, vec, taps, number):
+    layers, blocks = lax.axis_size("section"), lax.axis_size("seq")
+    width = own.shape[1]
     cw = wo.shape[0]
     heads = cw // HEAD
-    steps = tokens // SPAN
-    blocks = steps // sequences
+    steps = layers * blocks
+    tokens = steps * SPAN
     tri, spread3, _ = tables(heads)
     rows = lambda w: pl.BlockSpec((SPAN, w), lambda t: (t, 0))
     chans = cw + 2 * STATE
+    vmem = pl.BlockSpec(memory_space=pltpu.VMEM)
+    dma = pltpu.SemaphoreType.DMA
     return pl.pallas_call(
-        functools.partial(forward_kernel, heads, blocks, taps),
+        functools.partial(forward_kernel, layers, heads, blocks, taps),
         grid=(steps,),
-        in_specs=[rows(width)] + [whole(a) for a in (wgx, ws, wo, vec, tri, spread3)],
+        in_specs=[vmem] * 7,
         out_specs=[
-            rows(width),
-            pl.BlockSpec((1, 8, SPAN), lambda t: (t, 0, 0)),
+            vmem,
+            vmem,
             rows(2 * cw),
             rows(3 * STATE),
             rows(cw),
             pl.BlockSpec((1, STATE, cw), lambda t: (t, 0, 0)),
+            pl.BlockSpec(memory_space=pl.ANY),
         ],
         out_shape=[
-            jax.ShapeDtypeStruct((tokens, width), BF16),
-            jax.ShapeDtypeStruct((steps, 8, SPAN), F32),
+            jax.ShapeDtypeStruct(own.shape, F32),
+            jax.ShapeDtypeStruct((layers, 8, SPAN), F32),
             jax.ShapeDtypeStruct((tokens, 2 * cw), BF16),
             jax.ShapeDtypeStruct((tokens, 3 * STATE), BF16),
             jax.ShapeDtypeStruct((tokens, cw), BF16),
             jax.ShapeDtypeStruct((steps, STATE, cw), BF16),
+            jax.ShapeDtypeStruct((tokens, width), BF16),
         ],
         scratch_shapes=[
+            pltpu.VMEM((tokens, width), BF16),
+            pltpu.VMEM((tokens, width), BF16),
             pltpu.VMEM((SPAN + 8, chans), F32),
             pltpu.VMEM((STATE, cw), F32),
             pltpu.VMEM((SPAN, cw), F32),
-        ],
-        compiler_params=pltpu.CompilerParams(vmem_limit_bytes=48 << 20),
+            pltpu.VMEM((layers, 8, SPAN), F32),
+            pltpu.VMEM((layers, steps, 8, SPAN), F32),
+        ]
+        + plane_scratch(layers, blocks, width)
+        + [dma((layers, steps)), dma((layers, steps))],
+        compiler_params=pltpu.CompilerParams(
+            vmem_limit_bytes=60 << 20, collective_id=number, has_side_effects=True
+        ),
         cost_estimate=pl.CostEstimate(
             flops=2 * tokens * width * (3 * cw + 3 * STATE) + 2 * tokens * cw * 700,
             bytes_accessed=4 * tokens * width + 2 * width * (3 * cw + 3 * STATE) + 8 * tokens * cw,
             transcendentals=tokens * SPAN * heads,
         ),
         name="layer_forward",
-    )(full, wgx, ws, wo, vec, tri, spread3)
+    )(own, wgx, ws, wo, vec, tri, spread3)
 
 
 def layer_backward(gb, sc, pgx, ps, res, ent, wgx, ws, wo, vec, taps, sequences):
@@ -359,6 +687,299 @@
     )(gb, sc, pgx, ps, pgx, ps, res, ent, wgx, ws, wo, vec, tri, spread3, gather3)
 
 
+def line_barrier(place, count, axis):
+    sem = pltpu.get_barrier_semaphore()
+
+    @pl.when(place > 0)
+    def _():
+        pl.semaphore_signal(sem, inc=1, device_id={axis: place - 1}, device_id_type=MESH)
+
+    @pl.when(place < count - 1)
+    def _():
+        pl.semaphore_signal(sem, inc=1, device_id={axis: place + 1}, device_id_type=MESH)
+
+    inner = (place > 0) & (place < count - 1)
+
+    @pl.when(inner)
+    def _():
+        pl.semaphore_wait(sem, 2)
+
+    @pl.when(~inner)
+    def _():
+        pl.semaphore_wait(sem, 1)
+
+
+def gather_kernel(
+    count, ranks, parts, axis,
+    gx_ref, o_ref, full_ref, all_ref,
+    own_sem, send_sem, recv_sem, osend_sem, orecv_sem,
+):
+    place = lax.axis_index(axis)
+    rows = gx_ref.shape[0]
+    piece = rows // parts
+    orows = o_ref.shape[0]
+    opiece = orows // parts
+    here = lax.axis_index("section") * ranks + lax.axis_index("seq")
+    source = (here * orows) // (ranks * lax.axis_size("section") * orows // count)
+    line_barrier(place, count, axis)
+
+    def block(j, k):
+        return full_ref.at[pl.ds(pl.multiple_of(j * rows + k * piece, 16), piece), :]
+
+    def hop(src, dst, side, d, k):
+        to = place + 1 if side == 0 else place - 1
+        return pltpu.make_async_remote_copy(
+            src_ref=src, dst_ref=dst, send_sem=send_sem.at[side, d, k], recv_sem=recv_sem.at[side, d, k],
+            device_id={axis: to}, device_id_type=MESH,
+        )
+
+    def ohop(src, k, side):
+        to = place + 1 if side == 0 else place - 1
+        dst = all_ref.at[pl.ds(k * opiece, opiece), :]
+        return pltpu.make_async_remote_copy(
+            src_ref=src, dst_ref=dst, send_sem=osend_sem.at[side, k], recv_sem=orecv_sem.at[k],
+            device_id={axis: to}, device_id_type=MESH,
+        )
+
+    ends = (place < count - 1, place > 0)
+    for k in range(parts):
+        for side in (0, 1):
+            @pl.when(ends[side])
+            def _(side=side, k=k):
+                hop(gx_ref.at[pl.ds(k * piece, piece), :], block(place, k), side, 0, k).start()
+    own = pltpu.make_async_copy(gx_ref, full_ref.at[pl.ds(pl.multiple_of(place * rows, 16), rows), :], own_sem.at[0])
+    own.start()
+    oown = pltpu.make_async_copy(o_ref, all_ref, own_sem.at[1])
+
+    @pl.when(place == source)
+    def _():
+        oown.start()
+
+    for d in range(1, count):
+        for k in range(parts):
+            for side in (0, 1):
+                j = place - d if side == 0 else place + d
+                have = (j >= 0) if side == 0 else (j < count)
+
+                @pl.when(have)
+                def _(side=side, k=k, d=d, j=j):
+                    hop(block(j, k), block(j, k), side, d - 1, k).wait_recv()
+
+                if d < count - 1:
+                    @pl.when(have & ends[side])
+                    def _(side=side, k=k, d=d, j=j):
+                        hop(block(j, k), block(j, k), side, d, k).start()
+
+        if d == 1:
+            for k in range(parts):
+                for side in (0, 1):
+                    @pl.when((place == source) & ends[side])
+                    def _(side=side, k=k):
+                        ohop(o_ref.at[pl.ds(k * opiece, opiece), :], k, side).start()
+
+    for k in range(parts):
+        part = all_ref.at[pl.ds(k * opiece, opiece), :]
+
+        @pl.when(place != source)
+        def _(k=k, part=part):
+            ohop(part, k, 0).wait_recv()
+
+        @pl.when((place > source) & ends[0])
+        def _(k=k, part=part):
+            ohop(part, k, 0).start()
+
+        @pl.when((place < source) & ends[1])
+        def _(k=k, part=part):
+            ohop(part, k, 1).start()
+
+    own.wait()
+
+    @pl.when(place == source)
+    def _():
+        oown.wait()
+
+    for k in range(parts):
+        part = all_ref.at[pl.ds(k * opiece, opiece), :]
+
+        @pl.when((place >= source) & ends[0])
+        def _(k=k, part=part):
+            ohop(part, k, 0).wait_send()
+
+        @pl.when((place <= source) & ends[1])
+        def _(k=k, part=part):
+            ohop(part, k, 1).wait_send()
+
+        for d in range(count - 1):
+            for side in (0, 1):
+                j = place - d if side == 0 else place + d
+                have = (j >= 0) if side == 0 else (j < count)
+
+                @pl.when(have & ends[side])
+                def _(side=side, k=k, d=d, j=j):
+                    hop(block(j, k), block(j, k), side, d, k).wait_send()
+
+
+def gather_weights(gx, o, number):
+    count, ranks = lax.axis_size("fsdp"), lax.axis_size("seq")
+    parts = 4 if gx.shape[0] % 64 == 0 and o.shape[0] % 64 == 0 else 2
+    anywhere = pl.BlockSpec(memory_space=pl.ANY)
+    return pl.pallas_call(
+        functools.partial(gather_kernel, count, ranks, parts, "fsdp"),
+        in_specs=[anywhere] * 2,
+        out_specs=[anywhere] * 2,
+        out_shape=[
+            jax.ShapeDtypeStruct((count * gx.shape[0], gx.shape[1]), BF16),
+            jax.ShapeDtypeStruct(o.shape, BF16),
+        ],
+        scratch_shapes=[
+            pltpu.SemaphoreType.DMA((2,)),
+            pltpu.SemaphoreType.DMA((2, count, parts)),
+            pltpu.SemaphoreType.DMA((2, count, parts)),
+            pltpu.SemaphoreType.DMA((2, parts)),
+            pltpu.SemaphoreType.DMA((parts,)),
+        ],
+        compiler_params=pltpu.CompilerParams(collective_id=number, has_side_effects=True),
+        name="gather_weights",
+    )(gx, o)
+
+
+def reduce_kernel(
+    count, ranks, parts, axis,
+    full_ref, gp_ref, no_ref, gb_ref, out_ref, oout_ref,
+    sum_ref, osum_ref, in_ref, oin_ref,
+    send_sem, recv_sem, osend_sem, orecv_sem,
+):
+    place = lax.axis_index(axis)
+    rows = out_ref.shape[0]
+    piece = rows // parts
+    orows = oout_ref.shape[0]
+    opiece = orows // parts
+    here = lax.axis_index("section") * ranks + lax.axis_index("seq")
+    source = (here * orows) // (ranks * lax.axis_size("section") * orows // count)
+    line_barrier(place, count, axis)
+
+    def hop(j, k, side):
+        to = place + 1 if side == 0 else place - 1
+        return pltpu.make_async_remote_copy(
+            src_ref=sum_ref.at[j, k], dst_ref=in_ref.at[side, j, k],
+            send_sem=send_sem.at[j, k], recv_sem=recv_sem.at[side, j, k],
+            device_id={axis: to}, device_id_type=MESH,
+        )
+
+    def ohop(k, side):
+        to = place + 1 if side == 0 else place - 1
+        return pltpu.make_async_remote_copy(
+            src_ref=osum_ref.at[k], dst_ref=oin_ref.at[side, k],
+            send_sem=osend_sem.at[k], recv_sem=orecv_sem.at[side, k],
+            device_id={axis: to}, device_id_type=MESH,
+        )
+
+    ends = (place < count - 1, place > 0)
+    before = (place > 0, place < count - 1)
+
+    def work(j, k):
+        sum_ref[j, k] = dot(
+            full_ref[:, j * rows + k * piece : j * rows + (k + 1) * piece], gp_ref[...], 0, 0
+        ).astype(BF16)
+
+    def shift(j, k):
+        for side in (0, 1):
+            beyond = (place < j) if side == 0 else (place > j)
+
+            @pl.when(beyond & before[side])
+            def _(side=side):
+                hop(j, k, side).wait_recv()
+                sum_ref[j, k] = (sum_ref[j, k].astype(F32) + in_ref[side, j, k].astype(F32)).astype(BF16)
+
+            @pl.when(beyond)
+            def _(side=side):
+                hop(j, k, side).start()
+
+    order = []
+    low, high = 0, count - 1
+    while low <= high:
+        order += [high] if low == high else [high, low]
+        low, high = low + 1, high - 1
+    order = [(j, k) for pair in range(0, len(order), 2) for k in range(parts) for j in order[pair : pair + 2]]
+    for j, k in order:
+        work(j, k)
+        shift(j, k)
+    for k in range(parts):
+        osum_ref[k] = dot(no_ref[:, k * opiece : (k + 1) * opiece], gb_ref[...], 0, 0).astype(BF16)
+        for side in (0, 1):
+            beyond = (place < source) if side == 0 else (place > source)
+
+            @pl.when(beyond & before[side])
+            def _(side=side, k=k):
+                ohop(k, side).wait_recv()
+                osum_ref[k] = (osum_ref[k].astype(F32) + oin_ref[side, k].astype(F32)).astype(BF16)
+
+            @pl.when(beyond)
+            def _(side=side, k=k):
+                ohop(k, side).start()
+
+    for k in range(parts):
+        for j in range(count):
+            for side in (0, 1):
+                @pl.when((place == j) & before[side])
+                def _(side=side, k=k, j=j):
+                    hop(j, k, side).wait_recv()
+                    sum_ref[j, k] = (sum_ref[j, k].astype(F32) + in_ref[side, j, k].astype(F32)).astype(BF16)
+
+            @pl.when(place == j)
+            def _(k=k, j=j):
+                out_ref[pl.ds(k * piece, piece), :] = sum_ref[j, k]
+
+    for k in range(parts):
+        for side in (0, 1):
+            @pl.when((place == source) & before[side])
+            def _(side=side, k=k):
+                ohop(k, side).wait_recv()
+                osum_ref[k] = (osum_ref[k].astype(F32) + oin_ref[side, k].astype(F32)).astype(BF16)
+
+        oout_ref[pl.ds(k * opiece, opiece), :] = osum_ref[k]
+
+        @pl.when(place != source)
+        def _(k=k):
+            ohop(k, 0).wait_send()
+
+        for j in range(count):
+            @pl.when(place != j)
+            def _(k=k, j=j):
+                hop(j, k, 0).wait_send()
+
+
+def reduce_gradients(full, gp, no, gb, number):
+    count, ranks = lax.axis_size("fsdp"), lax.axis_size("seq")
+    tokens, width = full.shape
+    rows, cols, orows = width // count, gp.shape[1], no.shape[1]
+    parts = 3 if rows % 384 == 0 and orows % 384 == 0 else 1
+    return pl.pallas_call(
+        functools.partial(reduce_kernel, count, ranks, parts, "fsdp"),
+        in_specs=[whole(a) for a in (full, gp, no, gb)],
+        out_specs=[pl.BlockSpec(memory_space=pltpu.VMEM)] * 2,
+        out_shape=[jax.ShapeDtypeStruct((rows, cols), BF16), jax.ShapeDtypeStruct((orows, width), BF16)],
+        scratch_shapes=[
+            pltpu.VMEM((count, parts, rows // parts, cols), BF16),
+            pltpu.VMEM((parts, orows // parts, width), BF16),
+            pltpu.VMEM((2, count, parts, rows // parts, cols), BF16),
+            pltpu.VMEM((2, parts, orows // parts, width), BF16),
+            pltpu.SemaphoreType.DMA((count, parts)),
+            pltpu.SemaphoreType.DMA((2, count, parts)),
+            pltpu.SemaphoreType.DMA((parts,)),
+            pltpu.SemaphoreType.DMA((2, parts)),
+        ],
+        compiler_params=pltpu.CompilerParams(
+            collective_id=number, has_side_effects=True, vmem_limit_bytes=56 << 20
+        ),
+        cost_estimate=pl.CostEstimate(
+            flops=2 * tokens * (width * cols + orows * width), bytes_accessed=2 * tokens * (2 * width + cols + orows),
+            transcendentals=0,
+        ),
+        name="reduce_gradients",
+    )(full, gp, no, gb)
+
+
 def swapped(value, axis):
     count = lax.axis_size(axis)
     return lax.ppermute(value, axis, [(i, count - 1 - i) for i in range(count)])
@@ -387,11 +1008,23 @@
     shared = 2 * STATE
 
     ends = section_ends[0, :, 0]
-    sent = jnp.where(low_layer, ends[1], ends[0])
+    piece = ends.shape[1] // layers
+    sent = jnp.where(low_layer, ends[:, piece:], ends[:, :piece])
     got = swapped(sent, "section")
-    hidden = jnp.where(low_layer, ends[0], got).astype(F32)
-    cot = jnp.where(low_layer, got, ends[1]).astype(F32)
-    local = hidden.shape[0]
+    hidden = jnp.where(low_layer, ends[:, :piece], got).astype(F32).reshape(layers * piece, width)
+    cot = jnp.where(low_layer, got, ends[:, piece:]).astype(F32).reshape(layers * piece, width)
+
+    def own_tokens(v):
+        v = lax.dynamic_slice_in_dim(v, seq, 1, 1)[:, 0]
+        return lax.dynamic_slice_in_dim(v, sec * piece, piece, 1).reshape(-1, 1)
+
+    def token_order(v):
+        v = v.reshape(layers, ranks, layers, piece, -1)
+        return jnp.transpose(v, (2, 1, 0, 3, 4)).reshape(layers * layers * ranks * piece, -1)
+
+    def device_order(v):
+        v = v.reshape(layers, ranks, layers, piece, -1)
+        return jnp.transpose(v, (2, 1, 0, 3, 4)).reshape(layers * layers * ranks * piece, -1)
 
     flat = [norm_gain, conv_weight, conv_bias, step_bias, log_decay, skip_gain, gate_gain]
     sizes = [v.size for v in flat]
@@ -438,34 +1071,33 @@
 
     mine, theirs = own_columns(here), swapped(own_columns(there), "section")
     mine_o, theirs_o = own_rows(here), swapped(own_rows(there), "section")
-    piece = in_weight.shape[1] // ranks
-    thin = lax.dynamic_slice(in_weight[0], (seq * piece, inner + chans - shared), (piece, shared + heads_all))
+    strip = in_weight.shape[1] // ranks
+    thin = lax.dynamic_slice(in_weight[0], (seq * strip, inner + chans - shared), (strip, shared + heads_all))
     thin = lax.all_gather(thin, ("section", "fsdp", "seq"), axis=0, tiled=True).reshape(layers, width, -1)
     weights = []
     for layer in range(layers):
         own = low_layer if layer == 0 else ~low_layer
-        wgx = lax.all_gather(jnp.where(own, mine, theirs), "fsdp", axis=0, tiled=True)
-        wo = lax.psum(jnp.where(own, mine_o, theirs_o), "fsdp")
+        wgx, wo = gather_weights(jnp.where(own, mine, theirs), jnp.where(own, mine_o, theirs_o), layer)
         steps_w = head_columns(thin[layer, :, shared:], here * heads, heads)
         ws = jnp.concatenate([thin[layer, :, :shared], steps_w, jnp.zeros((width, STATE - heads), BF16)], 1)
         weights.append((wgx, ws, wo))
 
     def spread_rows(v):
-        return lax.all_gather(v, PLANE, axis=0, tiled=True)
+        return token_order(lax.all_gather(v, PLANE, axis=0, tiled=True))
 
     def collect_rows(v):
-        return lax.psum_scatter(v, PLANE, scatter_dimension=0, tiled=True).astype(F32)
+        return lax.psum_scatter(device_order(v), PLANE, scatter_dimension=0, tiled=True).astype(F32)
 
     saved = []
     for layer in range(layers):
         wgx, ws, wo = weights[layer]
         rs = lax.rsqrt(jnp.mean(hidden * hidden, axis=-1, keepdims=True) + EPS)
-        full = spread_rows((hidden * rs * gains[layer]).astype(BF16))
-        part, ss, pgx, ps, res, ent = layer_forward(full, wgx, ws, wo, vecs[layer], taps, layers)
-        raw = collect_rows(part)
-        ss = lax.psum_scatter(ss[:, 0, :].reshape(-1), PLANE, scatter_dimension=0, tiled=True)[:, None]
-        r = lax.rsqrt(ss / inner + EPS)
-        saved.append((hidden, rs, full, pgx, ps, res, ent, raw, r))
+        raw, ss, pgx, ps, res, ent, full = layer_forward(
+            (hidden * rs * gains[layer]).astype(BF16), wgx, ws, wo, vecs[layer], taps, 2 * layers + layer
+        )
+        r_rows = lax.rsqrt(ss / inner + EPS)
+        r = own_tokens(r_rows)
+        saved.append((hidden, rs, full, pgx, ps, res, ent, raw, r, r_rows))
         hidden = hidden + r * raw
         if layer + 1 < layers:
             hidden = hidden.astype(BF16).astype(F32)
@@ -475,20 +1107,19 @@
     big, small = [None] * layers, [None] * layers
     for layer in reversed(range(layers)):
         wgx, ws, wo = weights[layer]
-        before, rs, full, pgx, ps, res, ent, raw, r = saved[layer]
+        before, rs, full, pgx, ps, res, ent, raw, r, r_rows = saved[layer]
         low = grad.astype(BF16)
         pull = r * r * r * jnp.sum(low.astype(F32) * raw, axis=-1, keepdims=True) / inner
-        sc = jnp.concatenate([r.T, pull.T, jnp.zeros((6, local), F32)], 0)
         gb = spread_rows(low)
-        sc = lax.all_gather(sc, PLANE).reshape(-1, 8, local)
-        if local != SPAN:
-            sc = jnp.transpose(sc.reshape(-1, 8, local // SPAN, SPAN), (0, 2, 1, 3)).reshape(-1, 8, SPAN)
+        pull = lax.all_gather(pull.reshape(layers, piece), PLANE).reshape(layers, ranks, layers, piece)
+        pull = jnp.transpose(pull, (2, 1, 0, 3)).reshape(layers * ranks, SPAN)
+        sc = jnp.stack([r_rows[:, :ranks].reshape(-1, SPAN), pull], 1)
+        sc = jnp.pad(sc, ((0, 0), (0, 6), (0, 0)))
         pg, gpgx, gps, no, tiny = layer_backward(
             gb, sc, pgx, ps, res, ent, wgx, ws, wo, vecs[layer], taps, layers
         )
-        g_gx = dot(full, gpgx, 0, 0).astype(BF16)
+        g_gx, g_o = reduce_gradients(full, gpgx, no, gb, layers + layer)
         g_s = dot(full, gps, 0, 0).astype(BF16)
-        g_o = dot(no, gb, 0, 0).astype(BF16)
         gn = collect_rows(pg)
         unit = before * rs
         g_gain = jnp.sum(gn * unit, axis=0)
@@ -506,18 +1137,16 @@
             [g_gain, conv.reshape(-1), placed(tiny[5, :cw], inner, here * cw)]
             + [placed(tiny[n, :heads], heads_all, here * heads) for n in (6, 7, 8)]
         )
-        g_gx = lax.psum_scatter(g_gx, "fsdp", scatter_dimension=0, tiled=True)
         steps_g = lax.dynamic_update_slice(jnp.zeros((width, heads_all), BF16), g_s[:, shared : shared + heads], (0, here * heads))
         g_s = jnp.concatenate([g_s[:, :shared], steps_g], 1)
         g_s = lax.psum_scatter(g_s, "fsdp", scatter_dimension=0, tiled=True)
-        g_o = lax.psum(g_o, "fsdp")
         big[layer] = (g_gx, g_s, g_o)
 
-    sent = jnp.where(low_layer, output, grad).astype(BF16)
-    got = swapped(sent, "section").astype(F32)
-    first = jnp.where(low_layer, grad, got)
-    second = jnp.where(low_layer, got, output)
-    section_results = jnp.stack([first, second])[None, :, None]
+    output = output.reshape(layers, piece, width)
+    grad = grad.reshape(layers, piece, width)
+    got = swapped(jnp.where(low_layer, output, grad).astype(BF16), "section").astype(F32)
+    results = jnp.where(low_layer, jnp.concatenate([grad, got], 1), jnp.concatenate([got, output], 1))
+    section_results = results[None, :, None]
 
     def own_layer(values):
         own = jnp.where(low_layer, values[0], values[1])
@@ -528,7 +1157,6 @@
     other = swapped(other, "section")
     pair = jnp.stack([jnp.where(low_layer, own, other), jnp.where(low_layer, other, own)])
     gx = lax.all_gather(pair, "seq")
-    gx = jnp.transpose(gx, (3, 1, 0, 2, 4)) if False else gx
     rows = gx.shape[2]
     gx = gx.reshape(ranks, layers, rows, 2, cw)
     gx = jnp.transpose(gx, (2, 3, 1, 0, 4)).reshape(rows, 2 * inner)

time: 1270 us -> 1220 us (0.961)
  waiting for transfers between devices: 838 us -> 422 us
  Pallas kernels: 166 us -> 560 us
  matrix products: 41.6 us -> 8.07 us
  blocking collectives: 42.6 us -> 27.3 us
  local copies, waits for them, and re-layouts: 85 us -> 97.9 us
    pallas_call x2 -> x6, Pallas kernels: 56.1 us -> 451 us  [the longest x2 166 us: reduce_gradients(): pl.pallas_call(functools.partial(reduce_kernel, count, ranks, parts, 'fsd...]
    reduce_scatter x6 -> x2, waiting for transfers between devices: 294 us -> 97.9 us  [collect_rows(): lax.psum_scatter(device_order(v), PLANE, scatter_dimension=0, tiled=True)]
    psum x2 -> x0, waiting for transfers between devices: 182 us -> none  [the longest x1 122 us: per_device(): wo = lax.psum(jnp.where(own, mine_o, theirs_o), 'fsdp')]
    all_gather x6 -> x2, waiting for transfers between devices: 98.6 us -> 0.05 us  [spread_rows(): return token_order(lax.all_gather(v, PLANE, axis=0, tiled=True))]
    psum x1, waiting for transfers between devices: 5.66 us -> 57.6 us  [per_device(): grad_out = lax.psum(spread, 'seq').astype(F32)[None]]
    unnamed x25 -> x15, waiting for transfers between devices: 71.4 us -> 34.7 us
    dot_general x6 -> x2, matrix products: 41.6 us -> 8.07 us  [dot(): lax.dot_general(a, b, (((ca,), (cb,)), ((), ())), preferred_element_type=...]
    unnamed x2 -> x0, blocking collectives: 23.5 us -> none
  transfers between devices with their start and end apart: 28 -> 18, of which waited for: 19 -> 10; matrix products, arithmetic and copies ran while one was open for 9% -> 11% of each run, Pallas kernels for 0% -> 42%
where the time goes in v2:
time: 1220 us; the launch traced here: 1210 us
  Pallas kernels  560 us (46%)
  waiting for transfers between devices  422 us (35%)
  local copies, waits for them, and re-layouts  97.9 us (8%)
  other arithmetic  64.2 us (5%)
  blocking collectives  27.3 us (2%)
  between operations  17.6 us (1%)
  starting transfers between devices  15.6 us (1%)
    pallas_call x2, Pallas kernels, reduce_gradients(): pl.pallas_call(functools.partial(reduce_kernel, count, ranks, parts, 'fsd...  166 us
    pallas_call x2, Pallas kernels, layer_forward(): pl.pallas_call(functools.partial(forward_kernel, layers, heads, blocks, t...  159 us
    pallas_call x2, Pallas kernels, gather_weights(): pl.pallas_call(functools.partial(gather_kernel, count, ranks, parts, 'fsd...  126 us
    psum x1, waiting for transfers between devices, per_device(): tiny = lax.psum(jnp.stack(small), EVERY)  121 us
    pallas_call x2, Pallas kernels, layer_backward(): pl.pallas_call(functools.partial(backward_kernel, heads, blocks, taps), g...  109 us
    reduce_scatter x2, waiting for transfers between devices, collect_rows(): lax.psum_scatter(device_order(v), PLANE, scatter_dimension=0, tiled=True)  97.9 us
    psum x1, waiting for transfers between devices, per_device(): grad_out = lax.psum(spread, 'seq').astype(F32)[None]  57.6 us
    ppermute x6, waiting for transfers between devices, swapped(): return lax.ppermute(value, axis, [(i, count - 1 - i) for i in range(count)])  52.9 us
  transfers between devices with their start and end apart: 18, of which 10 were waited for; matrix products, arithmetic and copies ran while one was open for 11% of the time, Pallas kernels for 42%

profile of v2, /device:TPU:19, one launch (start us, length us, event | category | flops | bytes accessed | tf_op | source)
XLA Modules:
  0.0 1213.4 jit_solution(4755497190099907505)
XLA Ops:
  13.0 2.1 concatenate.77
  20.8 18.1 %collective-permute-done = bf16[2,128,1536]{2,1,0:T(8,128)(2,1)S(1)} collective-permute-done((bf16[2,128,1536]{2,1,0:T(8,128)(2,1)S(1)}, bf16[2,128,1536]{2,1,0:T(8,128)(2,1)S(1)}, u32[]{:S(2)}, u32[]{:S(2)}) %collective-permute-start) | collective-permute-done | bytes 786464 | tf_op jit(solution)/shard_map/ppermute | solution.py:985
  40.0 2.1 constant_dynamic-slice_fusion.12
  42.0 1.8 copy.62
  44.8 1.9 pad_maximum_fusion.4
  47.7 2.6 select_bitcast_fusion
  51.3 34.5 %all-reduce.24.cloned.1.call-done = bf16[42784]{0:T(1024)(128)(2,1)} async-done(((bf16[42784]{0:T(1024)(128)(2,1)}), bf16[42784]{0:T(1024)(128)(2,1)}) %all-reduce.24.cloned.1.call-update) | async-done | bytes 85584
  91.8 2.3 broadcast_select_fusion.5
  96.3 3.3 bitcast_select_fusion
  99.6 62.3 %gather_weights.2 = (bf16[1536,768]{1,0:T(8,128)(2,1)}, bf16[384,1536]{1,0:T(8,128)(2,1)}) custom-call(bf16[384,768]{1,0:T(8,128)(2,1)} %get-tuple-element.100.gx_ref, bf16[384,1536]{1,0:T(8,128)(2,1)} %get-tuple-element.92.o_ref), custom_call_target="tpu_custom_call" | custom-call | tf_op jit(solution)/shard_map/gather_weights/pallas_call | solution.py:826
  161.9 63.5 %gather_weights.3 = (bf16[1536,768]{1,0:T(8,128)(2,1)}, bf16[384,1536]{1,0:T(8,128)(2,1)}) custom-call(bf16[384,768]{1,0:T(8,128)(2,1)} %get-tuple-element.99.gx_ref, bf16[384,1536]{1,0:T(8,128)(2,1)} %get-tuple-element.91.o_ref), custom_call_target="tpu_custom_call" | custom-call | tf_op jit(solution)/shard_map/gather_weights/pallas_call | solution.py:826
  227.4 2.0 maximum_maximum_fusion.1
  229.4 81.0 %layer_forward.2 = (f32[256,1536]{1,0:T(8,128)}, f32[2,8,256]{2,1,0:T(8,128)}, bf16[2048,768]{1,0:T(8,128)(2,1)}, bf16[2048,384]{1,0:T(8,128)(2,1)}, bf16[2048,3...) custom-call(bf16[256,1536]{1,0:T(8,128)(2,1)} %fusion.21.own_ref, ...), custom_call_target="tpu_custom_call" | custom-call | flops 10764681216 | bytes 23592960 | tf_op jit(solution)/shard_map/layer_forward/pallas_call | solution.py:586
  314.2 78.3 %layer_forward.3 = (f32[256,1536]{1,0:T(8,128)}, f32[2,8,256]{2,1,0:T(8,128)}, bf16[2048,768]{1,0:T(8,128)(2,1)}, bf16[2048,384]{1,0:T(8,128)(2,1)}, bf16[2048,3...) custom-call(bf16[256,1536]{1,0:T(8,128)(2,1)} %fusion.15.own_ref, ...), custom_call_target="tpu_custom_call" | custom-call | flops 10764681216 | bytes 23592960 | tf_op jit(solution)/shard_map/layer_forward/pallas_call | solution.py:586
  395.0 8.1 all_gather.31
  403.3 6.2 copy.66
  409.6 54.7 %layer_backward.2 = (bf16[2048,1536]{1,0:T(8,128)(2,1)}, bf16[2048,768]{1,0:T(8,128)(2,1)}, bf16[2048,384]{1,0:T(8,128)(2,1)S(1)}, bf16[2048,384]{1,0:T(8,128)(2,1)}, f32[16,640]{1,0:T(8,128)S(1)}) custom-call(bf16[2048,1536]{1,0:T(8,128)(2,1)} %bitcast.152, f32[8,8,256]{2,1,0:T(8,128)S(1)} %select_maximum_fusion.1.sc_ref, ...), custom_call_target="tpu_custom_call" | custom-call | flops 12809404416 | bytes 23592960 | tf_op jit(solution)/shard_map/layer_backward/pallas_call | solution.py:645
  464.3 6.0 copy.70
  470.4 62.9 %reduce-scatter.9.cloned.1.call-done = bf16[256,1536]{1,0:T(8,128)(2,1)} async-done(((bf16[2048,1536]{1,0:T(8,128)(2,1)}), bf16[256,1536]{1,0:T(8,128)(2,1)}) %reduce-scatter.9.cloned.1.call-update) | async-done | bytes 786448 | tf_op jit(solution)/shard_map/reduce_scatter | solution.py:1089
  533.3 1.9 fusion.17
  535.2 3.0 fusion.13
  538.3 5.4 convolution_convert_fusion
  545.6 82.1 %reduce_gradients.3 = (bf16[384,768]{1,0:T(8,128)(2,1)}, bf16[384,1536]{1,0:T(8,128)(2,1)}) custom-call(bf16[2048,1536]{1,0:T(8,128)(2,1)} %get-tuple-element.66.full_ref, bf16[2048,768]{1,0:T(8,128)(2,1)} %get-tuple-element.67.gp_ref, bf16[2048,384]{1,0:T(8,128)(2,1)} %get-tuple-element.68.no_ref, bf16[2048,1536]{1,0:T(8,128)(2,1)} %bitcast.153), custom_call_target="tpu_custom_call" | custom-call | flops 7247757312 | bytes 17301504 | tf_op jit(solution)/shard_map/reduce_gradients/pallas_call | solution.py:957
  627.8 19.1 %all_gather.33 = f32[8,2,128]{2,1,0:T(2,128)S(1)} all-gather(f32[1,2,128]{2,1,0:T(2,128)S(1)} %fusion.36), channel_id=1, replica_groups=mesh['section'=2,'seq'=4,'fsdp'=4] {'section','seq'}, dimensions={0}, use_global_device_ids=true | all-gather | bytes 9216 | tf_op jit(solution)/shard_map/all_gather | solution.py:1114
  647.0 6.2 copy.71
  653.2 54.6 %layer_backward.3 = (bf16[2048,1536]{1,0:T(8,128)(2,1)}, bf16[2048,768]{1,0:T(8,128)(2,1)}, bf16[2048,384]{1,0:T(8,128)(2,1)S(1)}, bf16[2048,384]{1,0:T(8,128)(2,1)}, f32[16,640]{1,0:T(8,128)S(1)}) custom-call(bf16[2048,1536]{1,0:T(8,128)(2,1)} %bitcast.155, f32[8,8,256]{2,1,0:T(8,128)S(1)} %select_maximum_fusion.sc_ref, ...), custom_call_target="tpu_custom_call" | custom-call | flops 12809404416 | bytes 23592960 | tf_op jit(solution)/shard_map/layer_backward/pallas_call | solution.py:645
  707.9 2.7 convolution_convert_fusion.1
  712.4 83.9 %reduce_gradients.2 = (bf16[384,768]{1,0:T(8,128)(2,1)}, bf16[384,1536]{1,0:T(8,128)(2,1)}) custom-call(bf16[2048,1536]{1,0:T(8,128)(2,1)} %get-tuple-element.62.full_ref, bf16[2048,768]{1,0:T(8,128)(2,1)} %get-tuple-element.63.gp_ref, bf16[2048,384]{1,0:T(8,128)(2,1)} %get-tuple-element.64.no_ref, bf16[2048,1536]{1,0:T(8,128)(2,1)} %bitcast.156), custom_call_target="tpu_custom_call" | custom-call | flops 7247757312 | bytes 17301504 | tf_op jit(solution)/shard_map/reduce_gradients/pallas_call | solution.py:957
  798.7 9.5 collective-permute-start.5
  809.4 22.8 %collective-permute-done.5 = bf16[384,1536]{1,0:T(8,128)(2,1)} collective-permute-done((bf16[384,1536]{1,0:T(8,128)(2,1)}, bf16[384,1536]{1,0:T(8,128)(2,1)}, u32[]{:S(2)}, u32[]{:S(2)}) %collective-permute-start.5) | collective-permute-done | bytes 1179680 | tf_op jit(solution)/shard_map/ppermute | solution.py:985
  833.6 7.6 dynamic_update_slice.56
  845.1 3.5 add_bitcast_fusion
  848.6 7.1 add.209
  858.4 2.2 collective-permute-start.4
  860.5 11.9 collective-permute-done.4
  873.7 6.0 copy.74
  881.2 22.7 %all-reduce.20.cloned.1.call-done = bf16[2,384,304]{1,2,0:T(8,128)(2,1)} async-done(((bf16[2,384,304]{1,2,0:T(8,128)(2,1)}), bf16[2,384,304]{1,2,0:T(8,128)(2,1)}) %all-reduce.20.cloned.1.call-update) | async-done | bytes 466960 | tf_op jit(solution)/shard_map/psum | solution.py:1163
  905.0 57.6 %all-reduce.22.cloned.1.call-done = bf16[1,768,1536]{2,1,0:T(8,128)(2,1)} async-done(((bf16[1,768,1536]{2,1,0:T(8,128)(2,1)}), bf16[1,768,1536]{2,1,0:T(8,128)(2,1)}) %all-reduce.22.cloned.1.call-update) | async-done | bytes 2359312 | tf_op jit(solution)/shard_map/psum | solution.py:1176
  962.6 4.5 broadcast_in_dim.64
  967.1 35.3 %all-gather.14.cloned.1.call-done = bf16[8,384,768]{2,1,0:T(8,128)(2,1)} async-done(((bf16[2,384,768]{2,1,0:T(8,128)(2,1)}), bf16[8,384,768]{2,1,0:T(8,128)(2,1)}) %all-gather.14.cloned.1.call-update) | async-done | bytes 4718608 | tf_op jit(solution)/shard_map/all_gather | solution.py:1159
  1002.3 10.1 convert_element_type.95
  1012.4 12.7 %copy.77 = bf16[384,2,2,4,384]{0,4,3,2,1:T(8,128)(2,1)} copy(bf16[384,2,2,4,384]{4,1,0,2,3:T(2,128)(2,1)} %bitcast.146) | data formatting | bytes 9437184 | tf_op jit(solution)/shard_map/convert_element_type | solution.py:1165
  1025.1 7.4 fusion
  1032.5 35.0 %reduce-scatter.11.cloned.1.call-done = bf16[256,1536]{1,0:T(8,128)(2,1)} async-done(((bf16[2048,1536]{1,0:T(8,128)(2,1)}), bf16[256,1536]{1,0:T(8,128)(2,1)}) %reduce-scatter.11.cloned.1.call-update) | async-done | bytes 786448 | tf_op jit(solution)/shard_map/reduce_scatter | solution.py:1089
  1067.5 1.9 fusion.14
  1070.4 4.3 select_convert_fusion
  1075.0 121.3 %all-reduce.18.cloned.1.call-done = f32[2,21392]{1,0:T(2,128)} async-done(((f32[2,21392]{1,0:T(2,128)}), f32[2,21392]{1,0:T(2,128)}) %all-reduce.18.cloned.1.call-update) | async-done | bytes 171152 | tf_op jit(solution)/shard_map/psum | solution.py:1178
  1202.1 3.5 maximum_select_fusion
  (257 shorter events, 56.5 us)
Async XLA Ops:
  8.0 30.9 %copy-start.19 = (bf16[1,2,1,256,1536]{4,3,2,1,0:T(8,128)(2,1)S(1)}, bf16[1,2,1,256,1536]{4,3,2,1,0:T(8,128)(2,1)}, u32[]{:S(2)}) copy-start(bf16[1,2,1,256,1536]{4,3,2,1,0:T(8,128)(2,1)} %param.20) | copy-start | bytes 4718596
  8.0 77.8 %all-reduce.24.cloned.1.call-start = ((), (), s32[]{:S(2)}) async-start(), calls=%async_computation.13 | async-start | bytes 172032
  15.5 0.6 copy-start.27
  16.1 209.3 %all-gather.12.cloned.1.call-start = ((), (), s32[]{:S(2)}) async-start(), calls=%async_computation.11 | async-start | bytes 2433024 | tf_op jit(solution)/shard_map/all_gather | solution.py:1076
  17.9 385.3 %all-gather.8.cloned.1.call-start = ((), (), s32[]{:S(2)}) async-start(), calls=%async_computation.4 | async-start | bytes 7077888 | tf_op jit(solution)/shard_map/all_gather | solution.py:1086
  19.5 19.4 %collective-permute-start = (bf16[2,128,1536]{2,1,0:T(8,128)(2,1)S(1)}, bf16[2,128,1536]{2,1,0:T(8,128)(2,1)S(1)}, u32[]{:S(2)}, u32[]{:S(2)}) collective-permute-start(bf16[2,128,1536]{2,1,0:T(8,128)(2,1)S(1)} %broadcast_select_fusion.4), channel_id=1, source_target_pairs={{0,16},{16,0},{1,17},{17,1},{2,18},{18,2},{3,19},{19,3},{4,20},{20... | collective-permute-start | bytes 2359304 | tf_op jit(solution)/shard_map/ppermute | solution.py:985
  39.9 493.4 %reduce-scatter.9.cloned.1.call-start = ((), (), s32[]{:S(2)}) async-start(), calls=%async_computation.5 | async-start | bytes 7077888 | tf_op jit(solution)/shard_map/reduce_scatter | solution.py:1089
  46.7 45.1 %collective-permute-start.1 = (bf16[384,768]{1,0:T(8,128)(2,1)}, bf16[384,768]{1,0:T(8,128)(2,1)}, u32[]{:S(2)}, u32[]{:S(2)}) collective-permute-start(bf16[384,768]{1,0:T(8,128)(2,1)} %pad_maximum_fusion.4), channel_id=1, source_target_pairs={{0,16},{16,0},{1,17},{17,1},{2,18},{18,2},{3,19},{19,3},{4,20},{20... | collective-permute-start | bytes 1769480 | tf_op jit(solution)/shard_map/ppermute | solution.py:985
  50.4 45.2 %collective-permute-start.2 = (bf16[384,1536]{1,0:T(8,128)(2,1)}, bf16[384,1536]{1,0:T(8,128)(2,1)}, u32[]{:S(2)}, u32[]{:S(2)}) collective-permute-start(bf16[384,1536]{1,0:T(8,128)(2,1)} %select_bitcast_fusion), channel_id=1, source_target_pairs={{0,16},{16,0},{1,17},{17,1},{2,18},{18,2},{3,19},{19,3},{4,20},{20... | collective-permute-start | bytes 3538952 | tf_op jit(solution)/shard_map/ppermute | solution.py:985
  94.1 2.2 copy-start.24
  94.4 216.8 %copy-start.11 = (bf16[2,128,1536]{2,1,0:T(8,128)(2,1)}, bf16[2,128,1536]{2,1,0:T(8,128)(2,1)S(1)}, u32[]{:S(2)}) copy-start(bf16[2,128,1536]{2,1,0:T(8,128)(2,1)S(1)} %get-tuple-element.86) | copy-start | bytes 2359300
  225.4 1.9 copy-start.23
  314.2 79.1 %copy-start.14 = (bf16[2,128,1536]{2,1,0:T(8,128)(2,1)S(1)}, bf16[2,128,1536]{2,1,0:T(8,128)(2,1)}, u32[]{:S(2)}) copy-start(bf16[2,128,1536]{2,1,0:T(8,128)(2,1)} %broadcast_select_fusion.3) | copy-start | bytes 2359300
  403.2 6.3 copy-start.1
  403.3 6.3 copy-start.3
  403.3 6.3 copy-start.5
  403.3 6.3 copy-start.6
  403.3 6.3 copy-start.7
  403.3 6.2 copy-start.8
  403.3 6.2 copy-start.10
  470.3 176.7 %all-gather.10.cloned.1.call-start = ((), (), s32[]{:S(2)}) async-start(), calls=%async_computation.6 | async-start | bytes 7077888 | tf_op jit(solution)/shard_map/all_gather | solution.py:1086
  533.3 1.9 copy-start.15
  533.3 1.9 copy-start.22
  538.2 270.0 %reduce-scatter.15.cloned.1.call-start = ((), (), s32[]{:S(2)}) async-start(), calls=%async_computation.15 | async-start | bytes 1474560
  627.7 213.5 %reduce-scatter.13.cloned.1.call-start = ((), (), s32[]{:S(2)}) async-start(), calls=%async_computation.14 | async-start | bytes 1474560
  647.0 6.2 copy-start
  647.0 6.2 copy-start.2
  647.0 6.2 copy-start.4
  647.0 6.2 copy-start.9
  647.0 60.9 %slice-start = ((s8[6291456]{0:T(1024)(128)(4,1)}), s8[4194304]{0:T(1024)(128)(4,1)S(1)}, s32[]{:S(2)}) async-start(s8[6291456]{0:T(1024)(128)(4,1)} %bitcast.186), calls=%async_computation.16 | async-start | bytes 8388608
  653.2 54.7 %slice-start.1 = ((s8[6291456]{0:T(1024)(128)(4,1)}), s8[2097152]{0:T(1024)(128)(4,1)S(1)}, s32[]{:S(2)}) async-start(s8[6291456]{0:T(1024)(128)(4,1)} %bitcast.186), calls=%async_computation.17 | async-start | bytes 4194304
  796.3 1.3 copy-start.16
  796.3 107.5 %all-reduce.20.cloned.1.call-start = ((), (), s32[]{:S(2)}) async-start(), calls=%async_computation.9 | async-start | bytes 933888 | tf_op jit(solution)/shard_map/psum | solution.py:1163
  797.6 34.7 %copy-start.17 = (bf16[384,1536]{1,0:T(8,128)(2,1)S(1)}, bf16[384,1536]{1,0:T(8,128)(2,1)}, u32[]{:S(2)}) copy-start(bf16[384,1536]{1,0:T(8,128)(2,1)} %get-tuple-element.72) | copy-start | bytes 3538948
  798.7 33.5 %collective-permute-start.5 = (bf16[384,1536]{1,0:T(8,128)(2,1)}, bf16[384,1536]{1,0:T(8,128)(2,1)}, u32[]{:S(2)}, u32[]{:S(2)}) collective-permute-start(bf16[384,1536]{1,0:T(8,128)(2,1)} %broadcast_select_fusion), channel_id=1, source_target_pairs={{0,16},{16,0},{1,17},{17,1},{2,18},{18,2},{3,19},{19,3},{4,20},{20... | collective-permute-start | bytes 3538952 | tf_op jit(solution)/shard_map/ppermute | solution.py:985
  844.8 117.8 %all-reduce.22.cloned.1.call-start = ((), (), s32[]{:S(2)}) async-start(), calls=%async_computation.10 | async-start | bytes 4718592 | tf_op jit(solution)/shard_map/psum | solution.py:1176
  855.6 1.4 copy-start.13
  857.1 15.4 %copy-start.25 = (bf16[384,768]{1,0:T(8,128)(2,1)S(1)}, bf16[384,768]{1,0:T(8,128)(2,1)}, u32[]{:S(2)}) copy-start(bf16[384,768]{1,0:T(8,128)(2,1)} %get-tuple-element.69) | copy-start | bytes 1769476
  857.1 15.3 %copy-start.26 = (bf16[384,768]{1,0:T(8,128)(2,1)S(1)}, bf16[384,768]{1,0:T(8,128)(2,1)}, u32[]{:S(2)}) copy-start(bf16[384,768]{1,0:T(8,128)(2,1)} %get-tuple-element.65) | copy-start | bytes 1769476
  857.1 145.2 %all-gather.14.cloned.1.call-start = ((), (), s32[]{:S(2)}) async-start(), calls=%async_computation.12 | async-start | bytes 5898240 | tf_op jit(solution)/shard_map/all_gather | solution.py:1159
  858.4 14.1 %collective-permute-start.4 = (bf16[384,768]{1,0:T(8,128)(2,1)S(1)}, bf16[384,768]{1,0:T(8,128)(2,1)S(1)}, u32[]{:S(2)}, u32[]{:S(2)}) collective-permute-start(bf16[384,768]{1,0:T(8,128)(2,1)S(1)} %broadcast_select_fusion.6), channel_id=1, source_target_pairs={{0,16},{16,0},{1,17},{17,1},{2,18},{18,2},{3,19},{19,3},{4,20},{20... | collective-permute-start | bytes 1769480 | tf_op jit(solution)/shard_map/ppermute | solution.py:985
  873.7 193.8 %reduce-scatter.11.cloned.1.call-start = ((), (), s32[]{:S(2)}) async-start(), calls=%async_computation.7 | async-start | bytes 7077888 | tf_op jit(solution)/shard_map/reduce_scatter | solution.py:1089
  879.8 316.5 %all-reduce.18.cloned.1.call-start = ((), (), s32[]{:S(2)}) async-start(), calls=%async_computation.8 | async-start | bytes 344064 | tf_op jit(solution)/shard_map/psum | solution.py:1178
  1025.1 42.4 %copy-start.12 = (bf16[2,128,1536]{2,1,0:T(8,128)(2,1)S(1)}, bf16[2,128,1536]{2,1,0:T(8,128)(2,1)}, u32[]{:S(2)}) copy-start(bf16[2,128,1536]{2,1,0:T(8,128)(2,1)} %copy-done.11) | copy-start | bytes 2359300
  1032.5 37.8 %copy-start.18 = (bf16[256,1536]{1,0:T(8,128)(2,1)S(1)}, bf16[256,1536]{1,0:T(8,128)(2,1)}, u32[]{:S(2)}) copy-start(bf16[256,1536]{1,0:T(8,128)(2,1)} %get-tuple-element.82) | copy-start | bytes 2359300
  1067.5 2.8 copy-start.21
  1074.6 127.5 %copy-start.20 = (f32[256,1536]{1,0:T(8,128)S(1)}, f32[256,1536]{1,0:T(8,128)}, u32[]{:S(2)}) copy-start(f32[256,1536]{1,0:T(8,128)} %get-tuple-element.79) | copy-start | bytes 4718596
  1074.6 127.3 %collective-permute-start.3 = (bf16[2,128,1536]{2,1,0:T(8,128)(2,1)}, bf16[2,128,1536]{2,1,0:T(8,128)(2,1)S(1)}, u32[]{:S(2)}, u32[]{:S(2)}) collective-permute-start(bf16[2,128,1536]{2,1,0:T(8,128)(2,1)} %bitcast.51), channel_id=1, source_target_pairs={{0,16},{16,0},{1,17},{17,1},{2,18},{18,2},{3,19},{19,3},{4,20},{20... | collective-permute-start | bytes 2359304 | tf_op jit(solution)/shard_map/ppermute | solution.py:985
Sparse Core Ops, SparseCore 0:
  16.2 69.5 all-reduce.23
  627.8 39.5 reduce-scatter.14
  796.4 38.8 reduce-scatter.12
Sparse Core Ops, SparseCore 1:
  19.5 60.4 all-gather.11
  81.8 46.2 all-gather.7
  470.4 62.8 reduce-scatter.8
  538.3 45.9 all-gather.9
  844.9 58.9 all-reduce.19
  906.8 55.7 all-reduce.21
  964.6 37.7 all-gather.13
  1005.6 61.9 reduce-scatter.10
  1073.8 122.4 all-reduce.17

commit v3 on v2

--- a/solution.py
+++ b/solution.py
@@ -114,6 +114,12 @@
         order = self.orders[half]
         return max(i for i, dim in enumerate(order) if mask >> dim & 1)
 
+    def own_lanes(self, v, heads):
+        return pltpu.roll(v, STATE - (self.sec * self.ranks + self.seq) * heads, 1)
+
+    def all_lanes(self, v, heads):
+        return pltpu.roll(v, (self.sec * self.ranks + self.seq) * heads, 1)
+
     def barrier(self):
         sem = pltpu.get_barrier_semaphore()
         for mask in range(1, self.size):
@@ -174,14 +180,14 @@
 
 
 class Collect:
-    def __init__(self, plane, ref, base, blocks, core_in, stage_in, core_send, core_recv, send, recv):
-        self.plane, self.ref, self.base, self.blocks = plane, ref, base, blocks
+    def __init__(self, plane, ref, base, span, core_in, stage_in, core_send, core_recv, send, recv):
+        self.plane, self.ref, self.base, self.blocks, self.span = plane, ref, base, plane.ranks, span
         self.core_in, self.stage_in = core_in, stage_in
         self.core_send, self.core_recv, self.send, self.recv = core_send, core_recv, send, recv
 
     def core_copy(self, c):
         return pltpu.make_async_remote_copy(
-            src_ref=self.ref.at[pl.ds(self.base + c * SPAN, SPAN), :], dst_ref=self.core_in.at[c // 2],
+            src_ref=self.ref.at[pl.ds(self.base + c * self.span, self.span), :], dst_ref=self.core_in.at[c // 2],
             send_sem=self.core_send.at[c], recv_sem=self.core_recv.at[c],
             device_id=self.plane.partner(0), device_id_type=MESH,
         )
@@ -195,13 +201,13 @@
         @pl.when(self.plane.low == c % 2)
         def _():
             self.core_copy(c).wait_recv()
-            rows = pl.ds(self.base + c * SPAN, SPAN)
+            rows = pl.ds(self.base + c * self.span, self.span)
             self.ref[rows, :] = (self.ref[rows, :].astype(F32) + self.core_in[c // 2].astype(F32)).astype(BF16)
 
     def rows(self, half, mask):
         sec, seq = self.plane.owner(mask)
-        count = SPAN // self.plane.layers // 2
-        begin = self.base + seq * SPAN + sec * (2 * count) + half * count
+        count = self.span // self.plane.layers // 2
+        begin = self.base + seq * self.span + sec * (2 * count) + half * count
         return pl.ds(pl.multiple_of(begin, 16), count)
 
     def copy(self, half, mask, dim):
@@ -267,13 +273,105 @@
             self.copy(mask).wait_send()
 
 
+def chain_barrier(plane, place, count):
+    sem = pltpu.get_barrier_semaphore()
+    for mask in range(1, plane.size):
+        pl.semaphore_signal(sem, inc=1, device_id=plane.device(mask), device_id_type=MESH)
+    for d in range(1, count):
+        other = lax.rem(place + d, count)
+        for sec in (plane.sec, plane.layers - 1 - plane.sec):
+            pl.semaphore_signal(sem, inc=1, device_id={"section": sec, "fsdp": other}, device_id_type=MESH)
+    pl.semaphore_wait(sem, plane.size - 1 + 2 * (count - 1))
+
+
+class Row:
+    def __init__(self, place, count, source, target, send, recv):
+        self.place, self.count, self.source, self.target, self.send, self.recv = place, count, source, target, send, recv
+
+    def copy(self, d):
+        return pltpu.make_async_remote_copy(
+            src_ref=self.source(d), dst_ref=self.target(d), send_sem=self.send.at[d], recv_sem=self.recv.at[d],
+            device_id={"fsdp": lax.rem(self.place + d, self.count)}, device_id_type=MESH,
+        )
+
+    def begin(self):
+        for d in range(1, self.count):
+            self.copy(d).start()
+
+    def finish(self):
+        for d in range(1, self.count):
+            self.copy(d).wait_recv()
+
+    def drain(self):
+        for d in range(1, self.count):
+            self.copy(d).wait_send()
+
+
+class Line:
+    def __init__(self, place, count, block, parts, send, recv):
+        self.place, self.count, self.block, self.parts, self.send, self.recv = place, count, block, parts, send, recv
+        self.ends = (place < count - 1, place > 0)
+
+    def hop(self, side, d, k):
+        j = self.place - d if side == 0 else self.place + d
+        return pltpu.make_async_remote_copy(
+            src_ref=self.block(j, k), dst_ref=self.block(j, k), send_sem=self.send.at[side, d, k],
+            recv_sem=self.recv.at[side, d, k], device_id={"fsdp": self.place + 1 if side == 0 else self.place - 1},
+            device_id_type=MESH,
+        )
+
+    def arrived(self, side, d, k):
+        j = self.place - d if side == 0 else self.place + d
+        pltpu.make_async_remote_copy(
+            src_ref=self.block(j, k), dst_ref=self.block(j, k), send_sem=self.send.at[side, d, k],
+            recv_sem=self.recv.at[side, d - 1, k], device_id={"fsdp": self.place + 1 if side == 0 else self.place - 1},
+            device_id_type=MESH,
+        ).wait_recv()
+
+    def have(self, side, d):
+        return self.place >= d if side == 0 else self.place + d < self.count
+
+    def begin(self, k):
+        for side in (0, 1):
+            @pl.when(self.ends[side])
+            def _(side=side):
+                self.hop(side, 0, k).start()
+
+    def forward(self, d, k):
+        for side in (0, 1):
+            @pl.when(self.have(side, d))
+            def _(side=side):
+                self.arrived(side, d, k)
+
+            if d < self.count - 1:
+                @pl.when(self.have(side, d) & self.ends[side])
+                def _(side=side):
+                    self.hop(side, d, k).start()
+
+    def drain(self):
+        for k in range(self.parts):
+            for d in range(self.count - 1):
+                for side in (0, 1):
+                    @pl.when(self.have(side, d) & self.ends[side])
+                    def _(side=side, d=d, k=k):
+                        self.hop(side, d, k).wait_send()
+
+
 def forward_kernel(
-    layers, heads, blocks, taps,
-    own_ref, wgx_ref, ws_ref, wo_ref, vec_ref, tri_ref, spread_ref,
-    raw_ref, ss_ref, pgx_ref, ps_ref, res_ref, ent_ref, full_out_ref,
-    full_ref, part_ref, pad_ref, state_ref, within_ref, ss_mine, ss_in, core_in, stage_in,
-    out_sem, ag_send, ag_recv, core_send, core_recv, rs_send, rs_recv, ss_send, ss_recv,
+    layers, heads, blocks, taps, ahead, *refs
 ):
+    own_ref, wgx_ref, ws_ref, wo_ref, vec_ref, tri_ref, spread_ref = refs[:7]
+    refs = refs[7:]
+    if ahead:
+        next_gx, next_o = refs[:2]
+        refs = refs[2:]
+    raw_ref, ss_ref, pgx_ref, ps_ref, res_ref, ent_ref, full_out_ref = refs[:7]
+    refs = refs[7:]
+    if ahead:
+        ahead_gx, ahead_o = refs[:2]
+        refs = refs[2:]
+    full_ref, part_ref, pad_ref, state_ref, within_ref, ss_mine, ss_in, core_in, stage_in = refs[:9]
+    out_sem, ag_send, ag_recv, core_send, core_recv, rs_send, rs_recv, ss_send, ss_recv = refs[9:18]
     cw = heads * HEAD
     t = pl.program_id(0)
     steps = layers * blocks
@@ -286,7 +384,7 @@
 
     gathers = [Spread(plane, full_ref, start(m), piece, ag_send.at[m], ag_recv.at[m]) for m in range(layers)]
     sums = [
-        Collect(plane, part_ref, m * length, blocks, core_in.at[m], stage_in.at[m], core_send.at[m], core_recv.at[m],
+        Collect(plane, part_ref, m * length, SPAN, core_in.at[m], stage_in.at[m], core_send.at[m], core_recv.at[m],
                 rs_send.at[m], rs_recv.at[m])
         for m in range(layers)
     ]
@@ -299,14 +397,34 @@
         rows = pl.ds(m * length, length)
         return pltpu.make_async_copy(full_ref.at[rows, :], full_out_ref.at[rows, :], out_sem.at[m])
 
+    if ahead:
+        own_sem, row_send, row_recv, o_send, o_recv = refs[18:]
+        spot, count = lax.axis_index("fsdp"), lax.axis_size("fsdp")
+        grows = next_gx.shape[0]
+        target = ahead_gx.at[pl.ds(pl.multiple_of(spot * grows, 16), grows), :]
+        row = Row(spot, count, lambda d: next_gx, lambda d: target, row_send, row_recv)
+        orow = Row(spot, count, lambda d: next_o, lambda d: ahead_o.at[spot], o_send, o_recv)
+        own_gx = pltpu.make_async_copy(next_gx, target, own_sem.at[0])
+        own_o = pltpu.make_async_copy(next_o, ahead_o.at[spot], own_sem.at[1])
+
+        @pl.when(t == 0)
+        def _():
+            chain_barrier(plane, spot, count)
+            own_gx.start()
+            own_o.start()
+
     @pl.when(t == 0)
     def _():
         for m in range(layers):
             rows = pl.multiple_of(start(m)(plane.sec, plane.seq), 16)
             full_ref[pl.ds(rows, piece), :] = own_ref[m * piece : (m + 1) * piece, :]
         ss_mine[...] = jnp.zeros_like(ss_mine)
-        plane.barrier()
+        if not ahead:
+            plane.barrier()
         gathers[0].begin()
+        if ahead:
+            row.begin()
+            orow.begin()
         gathers[0].hop(0)
         gathers[1].begin()
         for stage in range(1, plane.stages):
@@ -337,7 +455,7 @@
     run = running_conv(pad_ref, vec_ref, taps)
     mixed = (run * sigmoid(run)).astype(BF16)
     xs, b, c = mixed[:, :cw], mixed[:, cw : cw + STATE], mixed[:, cw + STATE :]
-    _, _, dt, _, _, cum = step_sizes(ps[:, 2 * STATE :].astype(F32), vec_ref, tri_ref[...])
+    _, _, dt, _, _, cum = step_sizes(plane.own_lanes(ps[:, 2 * STATE :].astype(F32), heads), vec_ref, tri_ref[...])
     cum_t, dt_t = cum.T, dt.T
     inside = inside_mask()
     scores = dot(c, b, 1, 1)
@@ -418,22 +536,74 @@
             if stage + 1 < plane.stages:
                 sums[1].begin(stage + 1)
         sums[1].drain()
+        if ahead:
+            own_gx.wait()
+            own_o.wait()
+            for each in (row, orow):
+                each.finish()
+                each.drain()
 
 
 def backward_kernel(
-    heads, blocks, taps,
-    gb_ref, sc_ref, pgx_ref, ps_ref, hgx_ref, hs_ref, res_ref, ent_ref,
+    layers, heads, blocks, taps,
+    own_ref, pull_own, r_ref, pgx_ref, ps_ref, hgx_ref, hs_ref, res_ref, ent_ref,
     wgx_ref, ws_ref, wo_ref, vec_ref, tri_ref, spread_ref, gather_ref,
-    pg_ref, gpgx_ref, gps_ref, no_ref, small_ref,
-    pad_ref, next_ref, ge_ref, within_ref, gxm_ref,
+    raw_ref, gpgx_ref, gps_ref, no_ref, small_ref, full_out_ref,
+    full_ref, part_ref, pad_ref, next_ref, ge_ref, within_ref, gxm_ref, pull_ref, core_in, stage_in,
+    out_sem, ag_send, ag_recv, core_send, core_recv, rs_send, rs_recv, ss_send, ss_recv,
 ):
     cw = heads * HEAD
-    step = pl.program_id(0)
-    place = lax.rem(step, blocks)
-
-    @pl.when(step == 0)
+    t = pl.program_id(0)
+    steps = layers * blocks
+    place = lax.rem(t, blocks)
+    micro, block = t // blocks, blocks - 1 - place
+    plane = Plane(layers, blocks)
+    piece = SPAN // layers
+    length = blocks * SPAN
+    rows_now = pl.ds(pl.multiple_of(micro * length + block * SPAN, SPAN), SPAN)
+
+    def start(m):
+        return lambda sec, seq: m * length + seq * SPAN + sec * piece
+
+    gathers = [Spread(plane, full_ref, start(m), piece, ag_send.at[m], ag_recv.at[m]) for m in range(layers)]
+    collects = [
+        Collect(plane, part_ref, m * length, SPAN, core_in.at[m], stage_in.at[m], core_send.at[m], core_recv.at[m],
+                rs_send.at[m], rs_recv.at[m])
+        for m in range(layers)
+    ]
+
+    def pull_place(sec, seq):
+        return pull_ref.at[:, seq, :, pl.ds(pl.multiple_of(sec * piece, piece), piece)]
+
+    share = Share(plane, pull_own, lambda mask: pull_place(plane.sec, plane.seq), ss_send, ss_recv)
+
+    def saving(m):
+        rows = pl.ds(m * length, length)
+        return pltpu.make_async_copy(full_ref.at[rows, :], full_out_ref.at[rows, :], out_sem.at[m])
+
+    @pl.when(t == 0)
     def _():
         small_ref[...] = jnp.zeros_like(small_ref)
+        for m in range(layers):
+            rows = pl.multiple_of(start(m)(plane.sec, plane.seq), 16)
+            full_ref[pl.ds(rows, piece), :] = own_ref[m * piece : (m + 1) * piece, :]
+        for m in range(layers):
+            pull_ref[m, plane.seq, :, pl.ds(pl.multiple_of(plane.sec * piece, piece), piece)] = pull_own[m]
+        plane.barrier()
+        share.begin()
+        gathers[0].begin()
+        gathers[0].hop(0)
+        gathers[1].begin()
+        for stage in range(1, plane.stages):
+            gathers[0].hop(stage)
+        gathers[0].finish()
+        share.finish()
+        saving(0).start()
+
+    @pl.when(t == blocks)
+    def _():
+        gathers[1].finish()
+        saving(1).start()
 
     @pl.when(place == 0)
     def _():
@@ -453,17 +623,16 @@
     xs, b, c = mixed[:, :cw], mixed[:, cw : cw + STATE], mixed[:, cw + STATE :]
     xs_f = xs.astype(F32)
     tri = tri_ref[...]
-    x, e, dt, decay, rate, cum = step_sizes(ps[:, 2 * STATE :].astype(F32), vec_ref, tri)
+    x, e, dt, decay, rate, cum = step_sizes(plane.own_lanes(ps[:, 2 * STATE :].astype(F32), heads), vec_ref, tri)
     cum_t, dt_t = cum.T, dt.T
     tail = jnp.exp(cum[SPAN - 1 : SPAN, :] - cum) * dt
     growth = jnp.exp(cum)
     both = expand(jnp.concatenate([tail, growth], 0), spread_ref[...])
     tail_e, growth_e = both[:SPAN], both[SPAN:]
 
-    gb = gb_ref[...]
-    gu = dot(gb, wo_ref[...], 1, 1)
-    columns = jnp.concatenate([sc_ref[0]] * (STATE // 8), 0).T
-    r, pull = columns[:, 0:1], columns[:, 1:2]
+    gu = dot(full_ref[rows_now, :], wo_ref[...], 1, 1)
+    r = jnp.broadcast_to(r_ref[micro, pl.ds(block, 1), :], (STATE, SPAN)).T[:, 0:1]
+    pull = jnp.broadcast_to(pull_ref[micro, block][0:1, :], (STATE, SPAN)).T[:, 0:1]
     gain = vec_ref[5:6, :cw]
     gate = pgx[:, :cw].astype(F32)
     sg = sigmoid(gate)
@@ -536,10 +705,54 @@
         )
         gbefore = gbefore + vec_ref[k : k + 1, :] * next_ref[pl.ds(taps - 1 - k, SPAN), :]
     gpgx = jnp.concatenate([ggate, gbefore[:, :cw]], 1).astype(BF16)
-    gps = jnp.concatenate([gbefore[:, cw:], grad_raw], 1).astype(BF16)
+    gps = jnp.concatenate([gbefore[:, cw:], plane.all_lanes(grad_raw, heads)], 1).astype(BF16)
     gpgx_ref[...] = gpgx
     gps_ref[...] = gps
-    pg_ref[...] = (dot(gpgx, wgx_ref[...], 1, 1) + dot(gps, ws_ref[...], 1, 1)).astype(BF16)
+    part_ref[rows_now, :] = (dot(gpgx, wgx_ref[...], 1, 1) + dot(gps, ws_ref[...], 1, 1)).astype(BF16)
+
+    for m in range(layers):
+        for c in range(blocks):
+            @pl.when(t == m * blocks + blocks - 1 - c)
+            def _(m=m, c=c):
+                collects[m].block_done(c)
+
+    for stage in range(plane.stages):
+        @pl.when(t == min(stage, blocks - 1))
+        def _(stage=stage):
+            gathers[1].hop(stage)
+
+    @pl.when(t == blocks)
+    def _():
+        for c in range(blocks):
+            collects[0].block_add(c)
+        collects[0].begin(0)
+
+    for stage in range(plane.stages):
+        @pl.when(t == blocks + 1 + stage)
+        def _(stage=stage):
+            collects[0].add(stage, raw_ref, 0)
+            if stage + 1 < plane.stages:
+                collects[0].begin(stage + 1)
+
+    for c in range(1, blocks):
+        @pl.when(t == blocks + blocks - c)
+        def _(c=c):
+            collects[1].block_add(c)
+
+    @pl.when(t == steps - 1)
+    def _():
+        collects[1].block_add(0)
+        collects[1].begin(0)
+        share.drain()
+        for m in range(layers):
+            gathers[m].drain()
+            saving(m).wait()
+        collects[0].drain()
+        for stage in range(plane.stages):
+            collects[1].add(stage, raw_ref, piece)
+            if stage + 1 < plane.stages:
+                collects[1].begin(stage + 1)
+        collects[1].drain()
 
 
 def tables(heads):
@@ -571,8 +784,8 @@
     ]
 
 
-def layer_forward(own, wgx, ws, wo, vec, taps, number):
-    layers, blocks = lax.axis_size("section"), lax.axis_size("seq")
+def layer_forward(own, wgx, ws, wo, vec, taps, number, *following):
+    layers, blocks, depth = lax.axis_size("section"), lax.axis_size("seq"), lax.axis_size("fsdp")
     width = own.shape[1]
     cw = wo.shape[0]
     heads = cw // HEAD
@@ -584,9 +797,9 @@
     vmem = pl.BlockSpec(memory_space=pltpu.VMEM)
     dma = pltpu.SemaphoreType.DMA
     return pl.pallas_call(
-        functools.partial(forward_kernel, layers, heads, blocks, taps),
+        functools.partial(forward_kernel, layers, heads, blocks, taps, bool(following)),
         grid=(steps,),
-        in_specs=[vmem] * 7,
+        in_specs=[vmem] * 7 + [pl.BlockSpec(memory_space=pl.ANY)] * len(following),
         out_specs=[
             vmem,
             vmem,
@@ -595,7 +808,8 @@
             rows(cw),
             pl.BlockSpec((1, STATE, cw), lambda t: (t, 0, 0)),
             pl.BlockSpec(memory_space=pl.ANY),
-        ],
+        ]
+        + [pl.BlockSpec(memory_space=pl.ANY)] * len(following),
         out_shape=[
             jax.ShapeDtypeStruct(own.shape, F32),
             jax.ShapeDtypeStruct((layers, 8, SPAN), F32),
@@ -604,7 +818,8 @@
             jax.ShapeDtypeStruct((tokens, cw), BF16),
             jax.ShapeDtypeStruct((steps, STATE, cw), BF16),
             jax.ShapeDtypeStruct((tokens, width), BF16),
-        ],
+        ]
+        + ([jax.ShapeDtypeStruct(wgx.shape, BF16), jax.ShapeDtypeStruct((depth,) + following[1].shape, BF16)] if following else []),
         scratch_shapes=[
             pltpu.VMEM((tokens, width), BF16),
             pltpu.VMEM((tokens, width), BF16),
@@ -615,7 +830,8 @@
             pltpu.VMEM((layers, steps, 8, SPAN), F32),
         ]
         + plane_scratch(layers, blocks, width)
-        + [dma((layers, steps)), dma((layers, steps))],
+        + [dma((layers, steps)), dma((layers, steps))]
+        + ([dma((2,))] + [dma((depth,))] * 4 if following else []),
         compiler_params=pltpu.CompilerParams(
             vmem_limit_bytes=60 << 20, collective_id=number, has_side_effects=True
         ),
@@ -625,17 +841,20 @@
             transcendentals=tokens * SPAN * heads,
         ),
         name="layer_forward",
-    )(own, wgx, ws, wo, vec, tri, spread3)
-
-
-def layer_backward(gb, sc, pgx, ps, res, ent, wgx, ws, wo, vec, taps, sequences):
-    tokens, width = gb.shape
+    )(own, wgx, ws, wo, vec, tri, spread3, *following)
+
+
+def layer_backward(own, pull, r_rows, pgx, ps, res, ent, wgx, ws, wo, vec, taps, number):
+    layers, blocks = lax.axis_size("section"), lax.axis_size("seq")
+    width = own.shape[1]
     cw = wo.shape[0]
     heads = cw // HEAD
-    steps = tokens // SPAN
-    blocks = steps // sequences
+    steps = layers * blocks
+    tokens = steps * SPAN
     tri, spread3, gather3 = tables(heads)
     chans = cw + 2 * STATE
+    vmem = pl.BlockSpec(memory_space=pltpu.VMEM)
+    dma = pltpu.SemaphoreType.DMA
 
     def at(t):
         return t - lax.rem(t, blocks) + (blocks - 1 - lax.rem(t, blocks))
@@ -643,11 +862,12 @@
     rows = lambda w: pl.BlockSpec((SPAN, w), lambda t: (at(t), 0))
     edge = lambda w: pl.BlockSpec((16, w), lambda t: (jnp.maximum(at(t) * (SPAN // 16) - 1, 0), 0))
     return pl.pallas_call(
-        functools.partial(backward_kernel, heads, blocks, taps),
+        functools.partial(backward_kernel, layers, heads, blocks, taps),
         grid=(steps,),
         in_specs=[
-            rows(width),
-            pl.BlockSpec((1, 8, SPAN), lambda t: (at(t), 0, 0)),
+            vmem,
+            vmem,
+            vmem,
             rows(2 * cw),
             rows(3 * STATE),
             edge(2 * cw),
@@ -655,36 +875,45 @@
             rows(cw),
             pl.BlockSpec((1, STATE, cw), lambda t: (at(t), 0, 0)),
         ]
-        + [whole(a) for a in (wgx, ws, wo, vec, tri, spread3, gather3)],
+        + [vmem] * 7,
         out_specs=[
-            rows(width),
+            vmem,
             rows(2 * cw),
             rows(3 * STATE),
             rows(cw),
-            pl.BlockSpec((16, chans), lambda t: (0, 0)),
+            vmem,
+            pl.BlockSpec(memory_space=pl.ANY),
         ],
         out_shape=[
-            jax.ShapeDtypeStruct((tokens, width), BF16),
+            jax.ShapeDtypeStruct(own.shape, F32),
             jax.ShapeDtypeStruct((tokens, 2 * cw), BF16),
             jax.ShapeDtypeStruct((tokens, 3 * STATE), BF16),
             jax.ShapeDtypeStruct((tokens, cw), BF16),
             jax.ShapeDtypeStruct((16, chans), F32),
+            jax.ShapeDtypeStruct((tokens, width), BF16),
         ],
         scratch_shapes=[
+            pltpu.VMEM((tokens, width), BF16),
+            pltpu.VMEM((tokens, width), BF16),
             pltpu.VMEM((SPAN + 8, chans), F32),
             pltpu.VMEM((SPAN + 8, chans), F32),
             pltpu.VMEM((STATE, cw), F32),
             pltpu.VMEM((SPAN, cw), F32),
             pltpu.VMEM((SPAN, cw), F32),
-        ],
-        compiler_params=pltpu.CompilerParams(vmem_limit_bytes=48 << 20),
+            pltpu.VMEM((layers, blocks, 8, SPAN), F32),
+        ]
+        + plane_scratch(layers, blocks, width)
+        + [dma((steps,)), dma((steps,))],
+        compiler_params=pltpu.CompilerParams(
+            vmem_limit_bytes=60 << 20, collective_id=number, has_side_effects=True
+        ),
         cost_estimate=pl.CostEstimate(
             flops=2 * tokens * width * (3 * cw + 3 * STATE) + 2 * tokens * cw * 2000,
             bytes_accessed=4 * tokens * width + 2 * width * (3 * cw + 3 * STATE) + 8 * tokens * cw,
             transcendentals=tokens * SPAN * heads,
         ),
         name="layer_backward",
-    )(gb, sc, pgx, ps, pgx, ps, res, ent, wgx, ws, wo, vec, tri, spread3, gather3)
+    )(own, pull, r_rows, pgx, ps, pgx, ps, res, ent, wgx, ws, wo, vec, tri, spread3, gather3)
 
 
 def line_barrier(place, count, axis):
@@ -707,140 +936,6 @@
     @pl.when(~inner)
     def _():
         pl.semaphore_wait(sem, 1)
-
-
-def gather_kernel(
-    count, ranks, parts, axis,
-    gx_ref, o_ref, full_ref, all_ref,
-    own_sem, send_sem, recv_sem, osend_sem, orecv_sem,
-):
-    place = lax.axis_index(axis)
-    rows = gx_ref.shape[0]
-    piece = rows // parts
-    orows = o_ref.shape[0]
-    opiece = orows // parts
-    here = lax.axis_index("section") * ranks + lax.axis_index("seq")
-    source = (here * orows) // (ranks * lax.axis_size("section") * orows // count)
-    line_barrier(place, count, axis)
-
-    def block(j, k):
-        return full_ref.at[pl.ds(pl.multiple_of(j * rows + k * piece, 16), piece), :]
-
-    def hop(src, dst, side, d, k):
-        to = place + 1 if side == 0 else place - 1
-        return pltpu.make_async_remote_copy(
-            src_ref=src, dst_ref=dst, send_sem=send_sem.at[side, d, k], recv_sem=recv_sem.at[side, d, k],
-            device_id={axis: to}, device_id_type=MESH,
-        )
-
-    def ohop(src, k, side):
-        to = place + 1 if side == 0 else place - 1
-        dst = all_ref.at[pl.ds(k * opiece, opiece), :]
-        return pltpu.make_async_remote_copy(
-            src_ref=src, dst_ref=dst, send_sem=osend_sem.at[side, k], recv_sem=orecv_sem.at[k],
-            device_id={axis: to}, device_id_type=MESH,
-        )
-
-    ends = (place < count - 1, place > 0)
-    for k in range(parts):
-        for side in (0, 1):
-            @pl.when(ends[side])
-            def _(side=side, k=k):
-                hop(gx_ref.at[pl.ds(k * piece, piece), :], block(place, k), side, 0, k).start()
-    own = pltpu.make_async_copy(gx_ref, full_ref.at[pl.ds(pl.multiple_of(place * rows, 16), rows), :], own_sem.at[0])
-    own.start()
-    oown = pltpu.make_async_copy(o_ref, all_ref, own_sem.at[1])
-
-    @pl.when(place == source)
-    def _():
-        oown.start()
-
-    for d in range(1, count):
-        for k in range(parts):
-            for side in (0, 1):
-                j = place - d if side == 0 else place + d
-                have = (j >= 0) if side == 0 else (j < count)
-
-                @pl.when(have)
-                def _(side=side, k=k, d=d, j=j):
-                    hop(block(j, k), block(j, k), side, d - 1, k).wait_recv()
-
-                if d < count - 1:
-                    @pl.when(have & ends[side])
-                    def _(side=side, k=k, d=d, j=j):
-                        hop(block(j, k), block(j, k), side, d, k).start()
-
-        if d == 1:
-            for k in range(parts):
-                for side in (0, 1):
-                    @pl.when((place == source) & ends[side])
-                    def _(side=side, k=k):
-                        ohop(o_ref.at[pl.ds(k * opiece, opiece), :], k, side).start()
-
-    for k in range(parts):
-        part = all_ref.at[pl.ds(k * opiece, opiece), :]
-
-        @pl.when(place != source)
-        def _(k=k, part=part):
-            ohop(part, k, 0).wait_recv()
-
-        @pl.when((place > source) & ends[0])
-        def _(k=k, part=part):
-            ohop(part, k, 0).start()
-
-        @pl.when((place < source) & ends[1])
-        def _(k=k, part=part):
-            ohop(part, k, 1).start()
-
-    own.wait()
-
-    @pl.when(place == source)
-    def _():
-        oown.wait()
-
-    for k in range(parts):
-        part = all_ref.at[pl.ds(k * opiece, opiece), :]
-
-        @pl.when((place >= source) & ends[0])
-        def _(k=k, part=part):
-            ohop(part, k, 0).wait_send()
-
-        @pl.when((place <= source) & ends[1])
-        def _(k=k, part=part):
-            ohop(part, k, 1).wait_send()
-
-        for d in range(count - 1):
-            for side in (0, 1):
-                j = place - d if side == 0 else place + d
-                have = (j >= 0) if side == 0 else (j < count)
-
-                @pl.when(have & ends[side])
-                def _(side=side, k=k, d=d, j=j):
-                    hop(block(j, k), block(j, k), side, d, k).wait_send()
-
-
-def gather_weights(gx, o, number):
-    count, ranks = lax.axis_size("fsdp"), lax.axis_size("seq")
-    parts = 4 if gx.shape[0] % 64 == 0 and o.shape[0] % 64 == 0 else 2
-    anywhere = pl.BlockSpec(memory_space=pl.ANY)
-    return pl.pallas_call(
-        functools.partial(gather_kernel, count, ranks, parts, "fsdp"),
-        in_specs=[anywhere] * 2,
-        out_specs=[anywhere] * 2,
-        out_shape=[
-            jax.ShapeDtypeStruct((count * gx.shape[0], gx.shape[1]), BF16),
-            jax.ShapeDtypeStruct(o.shape, BF16),
-        ],
-        scratch_shapes=[
-            pltpu.SemaphoreType.DMA((2,)),
-            pltpu.SemaphoreType.DMA((2, count, parts)),
-            pltpu.SemaphoreType.DMA((2, count, parts)),
-            pltpu.SemaphoreType.DMA((2, parts)),
-            pltpu.SemaphoreType.DMA((parts,)),
-        ],
-        compiler_params=pltpu.CompilerParams(collective_id=number, has_side_effects=True),
-        name="gather_weights",
-    )(gx, o)
 
 
 def reduce_kernel(
@@ -980,6 +1075,245 @@
     )(full, gp, no, gb)
 
 
+def start_kernel(
+    layers, ranks, parts, oparts,
+    mine, theirs, mine_o, theirs_o, ends_ref, strip_ref, packed_ref,
+    full, all_o, next_gx, next_o, got_ref, thin_ref, params_ref,
+    own_sem, y_send, y_recv, x_send, x_recv, send, recv, o_send, o_recv, cut_send, cut_recv,
+    st_send, st_recv, ag_send, ag_recv, pa_send, pa_recv,
+):
+    place, count = lax.axis_index("fsdp"), lax.axis_size("fsdp")
+    plane = Plane(layers, ranks)
+    low = plane.sec == 0
+    rows = mine.shape[0]
+    piece = rows // parts
+    opiece = mine_o.shape[1] // oparts
+    orows = mine_o.shape[0] * mine_o.shape[1]
+    out_rows = layers * ranks * orows // count
+    here = plane.sec * ranks + plane.seq
+    there = (layers - 1 - plane.sec) * ranks + plane.seq
+    source = (here * orows) // out_rows == place
+    source_there = (there * orows) // out_rows == place
+    across = plane.partner(1)
+
+    def block(j, k):
+        return full.at[pl.ds(pl.multiple_of(j * rows + k * piece, 16), piece), :]
+
+    def oblock(j, k):
+        return all_o.at[j, pl.ds(k * opiece, opiece), :]
+
+    def y_copy(k, dst):
+        return pltpu.make_async_remote_copy(
+            src_ref=theirs.at[pl.ds(k * piece, piece), :], dst_ref=dst, send_sem=y_send.at[k], recv_sem=y_recv.at[k],
+            device_id=across, device_id_type=MESH,
+        )
+
+    def cut(d, same, first):
+        spot = lax.rem(place + d, count)
+        return pltpu.make_async_remote_copy(
+            src_ref=(mine_o if same else theirs_o).at[spot], dst_ref=all_o.at[spot] if first else next_o,
+            send_sem=cut_send.at[0 if same else 1, d], recv_sem=cut_recv.at[0 if first else 1],
+            device_id={"section": plane.sec if same else layers - 1 - plane.sec, "fsdp": spot}, device_id_type=MESH,
+        )
+
+    def own_cut(first):
+        return pltpu.make_async_copy(mine_o.at[place], all_o.at[place] if first else next_o, own_sem.at[3])
+
+    def begin_cuts(same, first, condition):
+        @pl.when(condition)
+        def _():
+            if same:
+                own_cut(first).start()
+            for d in range(1 if same else 0, count):
+                cut(d, same, first).start()
+
+    half = ends_ref.shape[1] // layers
+    x_copy = pltpu.make_async_remote_copy(
+        src_ref=ends_ref.at[:, pl.ds(pl.multiple_of((layers - 1 - plane.sec) * half, 16), half), :], dst_ref=got_ref,
+        send_sem=x_send.at[0], recv_sem=x_recv.at[0], device_id=across, device_id_type=MESH,
+    )
+    strips = Row(
+        place, count, lambda d: strip_ref, lambda d: thin_ref.at[plane.sec, plane.seq, place], st_send, st_recv
+    )
+    hold = count // 2
+    spread = Spread(plane, thin_ref, None, 0, ag_send, ag_recv)
+    spread.view = lambda h, mask: thin_ref.at[plane.owner(mask)[0], plane.owner(mask)[1], pl.ds(h * hold, hold)]
+
+    def p_copy(d, same):
+        sec = plane.sec if same else layers - 1 - plane.sec
+        number = d if same else count + d
+        return pltpu.make_async_remote_copy(
+            src_ref=packed_ref, dst_ref=params_ref.at[plane.sec, place], send_sem=pa_send.at[number],
+            recv_sem=pa_recv.at[number], device_id={"section": sec, "fsdp": lax.rem(place + d, count)},
+            device_id_type=MESH,
+        )
+
+    pairs = [(d, same) for d in range(count) for same in (True, False) if d or not same]
+    own_strip = pltpu.make_async_copy(strip_ref, thin_ref.at[plane.sec, plane.seq, place], own_sem.at[0])
+    own_packed = pltpu.make_async_copy(packed_ref, params_ref.at[plane.sec, place], own_sem.at[1])
+    own_block = pltpu.make_async_copy(mine, full.at[pl.ds(pl.multiple_of(place * rows, 16), rows), :], own_sem.at[2])
+    own_next = pltpu.make_async_copy(mine, next_gx, own_sem.at[2])
+    line = Line(place, count, block, parts, send, recv)
+    oline = Line(place, count, oblock, oparts, o_send, o_recv)
+
+    chain_barrier(plane, place, count)
+    own_strip.start()
+    own_packed.start()
+
+    @pl.when(low)
+    def _():
+        own_block.start()
+        for k in range(parts):
+            y_copy(k, block(place, k)).start()
+
+    strips.begin()
+    for d, same in pairs:
+        p_copy(d, same).start()
+    begin_cuts(True, True, low & source)
+
+    @pl.when(low)
+    def _():
+        own_block.wait()
+
+    for k in range(parts):
+        @pl.when(~low)
+        def _(k=k):
+            y_copy(k, block(place, k)).wait_recv()
+
+        line.begin(k)
+
+    @pl.when(low)
+    def _():
+        for k in range(parts):
+            y_copy(k, block(place, k)).wait_send()
+
+    begin_cuts(False, True, low & source_there)
+    x_copy.start()
+    for k in range(parts):
+        line.forward(1, k)
+
+    @pl.when(~low)
+    def _():
+        own_next.start()
+        for k in range(parts):
+            y_copy(k, next_gx.at[pl.ds(k * piece, piece), :]).start()
+
+    own_strip.wait()
+    strips.finish()
+    spread.begin()
+
+    @pl.when(low & source)
+    def _():
+        own_cut(True).wait()
+
+    @pl.when(~(low & source))
+    def _():
+        cut(0, True, True).wait_recv()
+
+    for k in range(oparts):
+        oline.begin(k)
+    spread.hop(0)
+    begin_cuts(True, False, ~low & source)
+    begin_cuts(False, False, ~low & source_there)
+    for d in range(2, count):
+        for k in range(parts):
+            line.forward(d, k)
+        for k in range(oparts):
+            oline.forward(d - 1, k)
+        if d == 2:
+            for stage in range(1, plane.stages):
+                spread.hop(stage)
+    for k in range(oparts):
+        oline.forward(count - 1, k)
+    spread.finish()
+
+    own_packed.wait()
+    x_copy.wait()
+
+    @pl.when(low)
+    def _():
+        for k in range(parts):
+            y_copy(k, next_gx.at[pl.ds(k * piece, piece), :]).wait_recv()
+
+    @pl.when(~low)
+    def _():
+        own_next.wait()
+        for k in range(parts):
+            y_copy(k, block(place, k)).wait_send()
+
+    @pl.when(~low & source)
+    def _():
+        own_cut(False).wait()
+
+    @pl.when(~(~low & source))
+    def _():
+        cut(0, True, False).wait_recv()
+
+    @pl.when(source)
+    def _():
+        for d in range(1, count):
+            cut(d, True, False).wait_send()
+
+    @pl.when(source_there)
+    def _():
+        for d in range(count):
+            cut(d, False, False).wait_send()
+
+    for d, same in pairs:
+        p_copy(d, same).wait()
+    strips.drain()
+    spread.drain()
+    line.drain()
+    oline.drain()
+
+
+def start_up(mine, theirs, mine_o, theirs_o, ends, strip, packed, number):
+    layers, ranks, count = lax.axis_size("section"), lax.axis_size("seq"), lax.axis_size("fsdp")
+    parts = 4 if mine.shape[0] % 64 == 0 else 2
+    mine_o = mine_o.reshape(count, -1, mine_o.shape[1])
+    theirs_o = theirs_o.reshape(mine_o.shape)
+    oparts = 2 if mine_o.shape[1] % 32 == 0 else 1
+    anywhere = pl.BlockSpec(memory_space=pl.ANY)
+    dma = pltpu.SemaphoreType.DMA
+    size = layers * ranks
+    half = ends.shape[1] // layers
+    return pl.pallas_call(
+        functools.partial(start_kernel, layers, ranks, parts, oparts),
+        in_specs=[anywhere] * 7,
+        out_specs=[anywhere] * 7,
+        out_shape=[
+            jax.ShapeDtypeStruct((count * mine.shape[0], mine.shape[1]), BF16),
+            jax.ShapeDtypeStruct(mine_o.shape, BF16),
+            jax.ShapeDtypeStruct(mine.shape, BF16),
+            jax.ShapeDtypeStruct(mine_o.shape[1:], BF16),
+            jax.ShapeDtypeStruct((ends.shape[0], half, ends.shape[2]), BF16),
+            jax.ShapeDtypeStruct((layers, ranks, count) + strip.shape, BF16),
+            jax.ShapeDtypeStruct((layers, count) + packed.shape, BF16),
+        ],
+        scratch_shapes=[
+            dma((4,)),
+            dma((parts,)),
+            dma((parts,)),
+            dma((1,)),
+            dma((1,)),
+            dma((2, count, parts)),
+            dma((2, count, parts)),
+            dma((2, count, oparts)),
+            dma((2, count, oparts)),
+            dma((2, count)),
+            dma((2,)),
+            dma((count,)),
+            dma((count,)),
+            dma((2, size)),
+            dma((2, size)),
+            dma((2 * count,)),
+            dma((2 * count,)),
+        ],
+        compiler_params=pltpu.CompilerParams(collective_id=number, has_side_effects=True),
+        name="start_up",
+    )(mine, theirs, mine_o, theirs_o, ends, strip, packed)
+
+
 def swapped(value, axis):
     count = lax.axis_size(axis)
     return lax.ppermute(value, axis, [(i, count - 1 - i) for i in range(count)])
@@ -1009,8 +1343,33 @@
 
     ends = section_ends[0, :, 0]
     piece = ends.shape[1] // layers
-    sent = jnp.where(low_layer, ends[:, piece:], ends[:, :piece])
-    got = swapped(sent, "section")
+
+    def head_columns(v, begin, count):
+        return lax.dynamic_slice_in_dim(v, begin, count, v.ndim - 1)
+
+    def own_columns(rank):
+        return jnp.concatenate(
+            [head_columns(in_weight[0], rank * cw, cw), head_columns(in_weight[0], inner + rank * cw, cw)], 1
+        )
+
+    out_rows = out_weight.shape[1]
+
+    def own_rows(rank):
+        start = jnp.clip(rank * cw - dep * out_rows, 0, out_rows - cw)
+        return lax.dynamic_slice_in_dim(out_weight[0], start, cw, 0)
+
+    strip = in_weight.shape[1] // ranks
+    thin = lax.dynamic_slice(in_weight[0], (seq * strip, inner + chans - shared), (strip, shared + heads_all))
+    thin = jnp.pad(thin, ((0, 0), (0, STATE - heads_all)))
+    flat = [norm_gain, conv_weight, conv_bias, step_bias, log_decay, skip_gain, gate_gain]
+    sizes = [v.size for v in flat]
+    packed = jnp.concatenate([v.reshape(-1) for v in flat])
+    packed = jnp.pad(packed, (0, -packed.size % 2048)).reshape(-1, STATE)
+    wgx, wo, next_gx, next_o, got, thin, packed = start_up(
+        own_columns(here), own_columns(there), own_rows(here), own_rows(there), ends, thin, packed, 0
+    )
+    packed = packed.reshape(layers, depth, -1).astype(F32)
+    thin = jnp.transpose(thin, (0, 2, 1, 3, 4)).reshape(layers, width, -1)
     hidden = jnp.where(low_layer, ends[:, :piece], got).astype(F32).reshape(layers * piece, width)
     cot = jnp.where(low_layer, got, ends[:, piece:]).astype(F32).reshape(layers * piece, width)
 
@@ -1018,25 +1377,9 @@
         v = lax.dynamic_slice_in_dim(v, seq, 1, 1)[:, 0]
         return lax.dynamic_slice_in_dim(v, sec * piece, piece, 1).reshape(-1, 1)
 
-    def token_order(v):
-        v = v.reshape(layers, ranks, layers, piece, -1)
-        return jnp.transpose(v, (2, 1, 0, 3, 4)).reshape(layers * layers * ranks * piece, -1)
-
-    def device_order(v):
-        v = v.reshape(layers, ranks, layers, piece, -1)
-        return jnp.transpose(v, (2, 1, 0, 3, 4)).reshape(layers * layers * ranks * piece, -1)
-
-    flat = [norm_gain, conv_weight, conv_bias, step_bias, log_decay, skip_gain, gate_gain]
-    sizes = [v.size for v in flat]
-    packed = jnp.concatenate([v.reshape(-1) for v in flat])
-    packed = lax.all_gather(packed, ("section", "fsdp")).reshape(layers, depth, -1).astype(F32)
-
     def member(layer, number):
         begin = sum(sizes[:number])
         return packed[layer, :, begin : begin + sizes[number]]
-
-    def head_columns(v, begin, count):
-        return lax.dynamic_slice_in_dim(v, begin, count, v.ndim - 1)
 
     def vectors(layer):
         kernel = jnp.transpose(member(layer, 1).reshape(depth, taps, -1), (1, 0, 2)).reshape(taps, chans)
@@ -1056,45 +1399,17 @@
     gains = [member(layer, 0).reshape(1, -1) for layer in range(layers)]
     vecs = [vectors(layer) for layer in range(layers)]
 
-    def own_columns(rank):
-        return jnp.concatenate(
-            [head_columns(in_weight[0], rank * cw, cw), head_columns(in_weight[0], inner + rank * cw, cw)], 1
+    saved, weights = [], []
+    for layer in range(layers):
+        ws, wo = thin[layer], wo.reshape(cw, width)
+        weights.append((wgx, ws, wo))
+        rs = lax.rsqrt(jnp.mean(hidden * hidden, axis=-1, keepdims=True) + EPS)
+        following = (next_gx, next_o) if layer + 1 < layers else ()
+        raw, ss, pgx, ps, res, ent, full, *after = layer_forward(
+            (hidden * rs * gains[layer]).astype(BF16), wgx, ws, wo, vecs[layer], taps, 2 * layers + layer, *following
         )
-
-    out_rows = out_weight.shape[1]
-
-    def own_rows(rank):
-        start = rank * cw - dep * out_rows
-        inside = (start >= 0) & (start < out_rows)
-        block = lax.dynamic_slice_in_dim(out_weight[0], jnp.clip(start, 0, out_rows - cw), cw, 0)
-        return jnp.where(inside, block, jnp.zeros_like(block))
-
-    mine, theirs = own_columns(here), swapped(own_columns(there), "section")
-    mine_o, theirs_o = own_rows(here), swapped(own_rows(there), "section")
-    strip = in_weight.shape[1] // ranks
-    thin = lax.dynamic_slice(in_weight[0], (seq * strip, inner + chans - shared), (strip, shared + heads_all))
-    thin = lax.all_gather(thin, ("section", "fsdp", "seq"), axis=0, tiled=True).reshape(layers, width, -1)
-    weights = []
-    for layer in range(layers):
-        own = low_layer if layer == 0 else ~low_layer
-        wgx, wo = gather_weights(jnp.where(own, mine, theirs), jnp.where(own, mine_o, theirs_o), layer)
-        steps_w = head_columns(thin[layer, :, shared:], here * heads, heads)
-        ws = jnp.concatenate([thin[layer, :, :shared], steps_w, jnp.zeros((width, STATE - heads), BF16)], 1)
-        weights.append((wgx, ws, wo))
-
-    def spread_rows(v):
-        return token_order(lax.all_gather(v, PLANE, axis=0, tiled=True))
-
-    def collect_rows(v):
-        return lax.psum_scatter(device_order(v), PLANE, scatter_dimension=0, tiled=True).astype(F32)
-
-    saved = []
-    for layer in range(layers):
-        wgx, ws, wo = weights[layer]
-        rs = lax.rsqrt(jnp.mean(hidden * hidden, axis=-1, keepdims=True) + EPS)
-        raw, ss, pgx, ps, res, ent, full = layer_forward(
-            (hidden * rs * gains[layer]).astype(BF16), wgx, ws, wo, vecs[layer], taps, 2 * layers + layer
-        )
+        if after:
+            wgx, wo = after
         r_rows = lax.rsqrt(ss / inner + EPS)
         r = own_tokens(r_rows)
         saved.append((hidden, rs, full, pgx, ps, res, ent, raw, r, r_rows))
@@ -1110,17 +1425,12 @@
         before, rs, full, pgx, ps, res, ent, raw, r, r_rows = saved[layer]
         low = grad.astype(BF16)
         pull = r * r * r * jnp.sum(low.astype(F32) * raw, axis=-1, keepdims=True) / inner
-        gb = spread_rows(low)
-        pull = lax.all_gather(pull.reshape(layers, piece), PLANE).reshape(layers, ranks, layers, piece)
-        pull = jnp.transpose(pull, (2, 1, 0, 3)).reshape(layers * ranks, SPAN)
-        sc = jnp.stack([r_rows[:, :ranks].reshape(-1, SPAN), pull], 1)
-        sc = jnp.pad(sc, ((0, 0), (0, 6), (0, 0)))
-        pg, gpgx, gps, no, tiny = layer_backward(
-            gb, sc, pgx, ps, res, ent, wgx, ws, wo, vecs[layer], taps, layers
+        pull = jnp.broadcast_to(pull.reshape(layers, 1, piece), (layers, 8, piece))
+        gn, gpgx, gps, no, tiny, gb = layer_backward(
+            low, pull, r_rows, pgx, ps, res, ent, wgx, ws, wo, vecs[layer], taps, 3 * layers + layer
         )
         g_gx, g_o = reduce_gradients(full, gpgx, no, gb, layers + layer)
         g_s = dot(full, gps, 0, 0).astype(BF16)
-        gn = collect_rows(pg)
         unit = before * rs
         g_gain = jnp.sum(gn * unit, axis=0)
         gn = gn * gains[layer]
@@ -1137,8 +1447,7 @@
             [g_gain, conv.reshape(-1), placed(tiny[5, :cw], inner, here * cw)]
             + [placed(tiny[n, :heads], heads_all, here * heads) for n in (6, 7, 8)]
         )
-        steps_g = lax.dynamic_update_slice(jnp.zeros((width, heads_all), BF16), g_s[:, shared : shared + heads], (0, here * heads))
-        g_s = jnp.concatenate([g_s[:, :shared], steps_g], 1)
+        g_s = g_s[:, : shared + heads_all]
         g_s = lax.psum_scatter(g_s, "fsdp", scatter_dimension=0, tiled=True)
         big[layer] = (g_gx, g_s, g_o)
 

time: 1220 us -> 1070 us (0.88)
  waiting for transfers between devices: 422 us -> 253 us
  Pallas kernels: 560 us -> 638 us
  blocking collectives: 27.3 us -> 0 us
  local copies, waits for them, and re-layouts: 97.9 us -> 77.4 us
  other arithmetic: 64.2 us -> 51.2 us
    reduce_scatter x2 -> x0, waiting for transfers between devices: 97.9 us -> none  [collect_rows(): lax.psum_scatter(device_order(v), PLANE, scatter_dimension=0, tiled=True)]
    psum x1, waiting for transfers between devices: 121 us -> 72.9 us  [per_device(): tiny = lax.psum(jnp.stack(small), EVERY)]
    pallas_call x4 -> x3, Pallas kernels: 235 us -> 278 us  [the longest x2 195 us: layer_backward(): pl.pallas_call(functools.partial(backward_kernel, layers, heads, blocks,...]
    ppermute x6 -> x3, waiting for transfers between devices: 52.9 us -> 19.8 us  [swapped(): return lax.ppermute(value, axis, [(i, count - 1 - i) for i in range(count)])]
    all_gather x2 -> x0, blocking collectives: 27.3 us -> none  [per_device(): lax.all_gather(pull.reshape(layers, piece), PLANE)]
    psum x1, waiting for transfers between devices: 22.7 us -> 47.4 us  [per_device(): s_all = lax.psum(jnp.stack([b[1] for b in big]), PLANE)]
    pallas_call x2, Pallas kernels: 159 us -> 179 us  [layer_forward(): pl.pallas_call(functools.partial(forward_kernel, layers, heads, blocks, t...]
    pallas_call x2, Pallas kernels: 166 us -> 181 us  [reduce_gradients(): pl.pallas_call(functools.partial(reduce_kernel, count, ranks, parts, 'fsd...]
  transfers between devices with their start and end apart: 18 -> 9, of which waited for: 10 -> 7; matrix products, arithmetic and copies ran while one was open for 11% -> 5% of each run, Pallas kernels for 42% -> 17%
where the time goes in v3:
time: 1070 us; the launch traced here: 1060 us
  Pallas kernels  638 us (60%)
  waiting for transfers between devices  253 us (24%)
  local copies, waits for them, and re-layouts  77.4 us (7%)
  other arithmetic  51.2 us (5%)
  between operations  16.6 us (2%)
  matrix products  11.3 us (1%)
    pallas_call x2, Pallas kernels, layer_backward(): pl.pallas_call(functools.partial(backward_kernel, layers, heads, blocks,...  195 us
    pallas_call x2, Pallas kernels, reduce_gradients(): pl.pallas_call(functools.partial(reduce_kernel, count, ranks, parts, 'fsd...  181 us
    pallas_call x2, Pallas kernels, layer_forward(): pl.pallas_call(functools.partial(forward_kernel, layers, heads, blocks, t...  179 us
    pallas_call x1, Pallas kernels, start_up(): pl.pallas_call(functools.partial(start_kernel, layers, ranks, parts, opar...  82.7 us
    psum x1, waiting for transfers between devices, per_device(): tiny = lax.psum(jnp.stack(small), EVERY)  72.9 us
    psum x1, waiting for transfers between devices, per_device(): grad_out = lax.psum(spread, 'seq').astype(F32)[None]  57.6 us
    psum x1, waiting for transfers between devices, per_device(): s_all = lax.psum(jnp.stack([b[1] for b in big]), PLANE)  47.4 us
    all_gather x1, waiting for transfers between devices, per_device(): gx = lax.all_gather(pair, 'seq')  34.9 us
  transfers between devices with their start and end apart: 9, of which 7 were waited for; matrix products, arithmetic and copies ran while one was open for 5% of the time, Pallas kernels for 17%

profile of v3, /device:TPU:19, one launch (start us, length us, event | category | flops | bytes accessed | tf_op | source)
XLA Modules:
  0.0 1057.5 jit_solution(11288882987937532017)
XLA Ops:
  8.1 2.2 constant_dynamic-slice_fusion.12
  10.8 1.4 copy.44
  12.2 1.8 copy.45
  16.7 1.9 constant_dynamic-slice_fusion.9
  19.8 82.7 %start_up.1 = (bf16[1536,768]{1,0:T(8,128)(2,1)}, bf16[4,96,1536]{2,1,0:T(8,128)(2,1)}, bf16[384,768]{1,0:T(8,128)(2,1)}, bf16[96,1536]{1,0:T(8,128)(2,1)}, bf16...) custom-call(bf16[384,768]{1,0:T(8,128)(2,1)} %get-tuple-element.130.mine, ...), custom_call_target="tpu_custom_call" | custom-call | tf_op jit(solution)/shard_map/start_up/pallas_call | solution.py:1280
  104.7 1.2 slice_select_fusion.1
  111.0 1.9 fusion.40
  115.8 1.2 concatenate.70.refs_4_.vec_ref
  117.0 100.9 %layer_forward.2 = (f32[256,1536]{1,0:T(8,128)}, f32[2,8,256]{2,1,0:T(8,128)}, bf16[2048,768]{1,0:T(8,128)(2,1)}, bf16[2048,384]{1,0:T(8,128)(2,1)}, bf16[2048,3...) custom-call(bf16[256,1536]{1,0:T(8,128)(2,1)} %fusion.18.refs_0_, ...), custom_call_target="tpu_custom_call" | custom-call | flops 10764681216 | bytes 23592960 | tf_op jit(solution)/shard_map/layer_forward/pallas_call | solution.py:799
  219.3 1.8 fusion.13
  222.4 1.2 copy.49
  224.8 1.2 concatenate.73.refs_4_.vec_ref
  226.1 78.4 %layer_forward.3 = (f32[256,1536]{1,0:T(8,128)}, f32[2,8,256]{2,1,0:T(8,128)}, bf16[2048,768]{1,0:T(8,128)(2,1)}, bf16[2048,384]{1,0:T(8,128)(2,1)}, bf16[2048,3...) custom-call(bf16[256,1536]{1,0:T(8,128)(2,1)} %fusion.8.refs_0_, ...), custom_call_target="tpu_custom_call" | custom-call | flops 10764681216 | bytes 23592960 | tf_op jit(solution)/shard_map/layer_forward/pallas_call | solution.py:799
  305.2 1.6 fusion.5
  307.5 95.7 %layer_backward.2 = (f32[256,1536]{1,0:T(8,128)}, bf16[2048,768]{1,0:T(8,128)(2,1)}, bf16[2048,384]{1,0:T(8,128)(2,1)}, bf16[2048,384]{1,0:T(8,128)(2,1)}, f32[1...) custom-call(bf16[256,1536]{1,0:T(8,128)(2,1)} %bitcast.126, f32[2,8,128]{2,1,0:T(8,128)} %broadcast_in_dim.75.pull_own, ...), custom_call_target="tpu_custom_call" | custom-call | flops 12809404416 | bytes 23592960 | tf_op jit(solution)/shard_map/layer_backward/pallas_call | solution.py:864
  403.3 2.1 fusion.12
  405.4 3.0 fusion.7
  409.8 99.1 %layer_backward.3 = (f32[256,1536]{1,0:T(8,128)}, bf16[2048,768]{1,0:T(8,128)(2,1)}, bf16[2048,384]{1,0:T(8,128)(2,1)}, bf16[2048,384]{1,0:T(8,128)(2,1)}, f32[1...) custom-call(bf16[256,1536]{1,0:T(8,128)(2,1)} %get-tuple-element.96.own_ref, f32[2,8,128]{2,1,0:T(8,128)} %broadcast_in_dim.77.pull_own, ...), custom_call_target="tpu_custom_call" | custom-call | flops 12809404416 | bytes 23592960 | tf_op jit(solution)/shard_map/layer_backward/pallas_call | solution.py:864
  508.9 5.9 fusion.47
  514.9 1.4 copy.54
  516.3 100.1 %reduce_gradients.2 = (bf16[384,768]{1,0:T(8,128)(2,1)}, bf16[384,1536]{1,0:T(8,128)(2,1)}) custom-call(bf16[2048,1536]{1,0:T(8,128)(2,1)} %get-tuple-element.74.full_ref, bf16[2048,768]{1,0:T(8,128)(2,1)} %get-tuple-element.75.gp_ref, bf16[2048,384]{1,0:T(8,128)(2,1)} %get-tuple-element.76.no_ref, bf16[2048,1536]{1,0:T(8,128)(2,1)} %get-tuple-element.77.gb_ref), custom_call_target="tpu_custom_call" | custom-call | flops 7247757312 | bytes 17301504 | tf_op jit(solution)/shard_map/reduce_gradients/pallas_call | solution.py:1052
  616.4 81.3 %reduce_gradients.3 = (bf16[384,768]{1,0:T(8,128)(2,1)}, bf16[384,1536]{1,0:T(8,128)(2,1)}) custom-call(bf16[2048,1536]{1,0:T(8,128)(2,1)} %get-tuple-element.79.full_ref, bf16[2048,768]{1,0:T(8,128)(2,1)} %get-tuple-element.80.gp_ref, bf16[2048,384]{1,0:T(8,128)(2,1)} %get-tuple-element.81.no_ref, bf16[2048,1536]{1,0:T(8,128)(2,1)} %get-tuple-element.82.gb_ref), custom_call_target="tpu_custom_call" | custom-call | flops 7247757312 | bytes 17301504 | tf_op jit(solution)/shard_map/reduce_gradients/pallas_call | solution.py:1052
  697.7 2.5 broadcast_select_fusion
  700.3 7.1 collective-permute-start.2
  707.4 5.4 fusion.48
  713.8 2.3 copy.56
  716.7 1.9 fusion.22
  720.6 6.6 collective-permute-done.2
  727.1 1.2 select_select_fusion
  728.3 1.6 broadcast.130
  729.9 6.6 dynamic_update_slice.48
  737.6 20.1 %reduce-scatter.9.cloned.1.call-done = bf16[384,304]{1,0:T(8,128)(2,1)} async-done(((bf16[1536,304]{1,0:T(8,128)(2,1)}), bf16[384,304]{1,0:T(8,128)(2,1)}) %reduce-scatter.9.cloned.1.call-update) | async-done | bytes 233488
  759.7 3.5 add_bitcast_fusion
  763.2 6.0 add.201
  770.5 1.2 collective-permute-start.1
  771.7 13.2 %collective-permute-done.1 = bf16[384,768]{1,0:T(8,128)(2,1)S(1)} collective-permute-done((bf16[384,768]{1,0:T(8,128)(2,1)S(1)}, bf16[384,768]{1,0:T(8,128)(2,1)S(1)}, u32[]{:S(2)}, u32[]{:S(2)}) %collective-permute-start.1) | collective-permute-done | bytes 589856 | tf_op jit(solution)/shard_map/ppermute | solution.py:1319
  785.1 1.2 pad_maximum_fusion
  786.9 4.4 select_convert_fusion
  791.3 1.2 collective-permute-start
  792.5 72.9 %all-reduce.16.cloned.1.call-done = f32[2,21392]{1,0:T(2,128)} async-done(((f32[2,21392]{1,0:T(2,128)}), f32[2,21392]{1,0:T(2,128)}) %all-reduce.16.cloned.1.call-update) | async-done | bytes 171152 | tf_op jit(solution)/shard_map/psum | solution.py:1487
  871.3 3.5 maximum_select_fusion
  874.8 47.4 %all-reduce.18.cloned.1.call-done = bf16[2,384,304]{1,2,0:T(8,128)(2,1)} async-done(((bf16[2,384,304]{1,2,0:T(8,128)(2,1)}), bf16[2,384,304]{1,2,0:T(8,128)(2,1)}) %all-reduce.18.cloned.1.call-update) | async-done | bytes 466960 | tf_op jit(solution)/shard_map/psum | solution.py:1472
  923.3 57.6 %all-reduce.20.cloned.1.call-done = bf16[1,768,1536]{2,1,0:T(8,128)(2,1)} async-done(((bf16[1,768,1536]{2,1,0:T(8,128)(2,1)}), bf16[1,768,1536]{2,1,0:T(8,128)(2,1)}) %all-reduce.20.cloned.1.call-update) | async-done | bytes 2359312 | tf_op jit(solution)/shard_map/psum | solution.py:1485
  980.9 4.5 broadcast_in_dim.82
  985.4 34.9 %all-gather.3.cloned.1.call-done = bf16[8,384,768]{2,1,0:T(8,128)(2,1)} async-done(((bf16[2,384,768]{2,1,0:T(8,128)(2,1)}), bf16[8,384,768]{2,1,0:T(8,128)(2,1)}) %all-gather.3.cloned.1.call-update) | async-done | bytes 4718608 | tf_op jit(solution)/shard_map/all_gather | solution.py:1468
  1020.3 10.1 convert_element_type.88
  1030.4 12.5 %copy.53 = bf16[384,2,2,4,384]{0,4,3,2,1:T(8,128)(2,1)} copy(bf16[384,2,2,4,384]{4,1,0,2,3:T(2,128)(2,1)} %bitcast.123) | data formatting | bytes 9437184 | tf_op jit(solution)/shard_map/convert_element_type | solution.py:1474
  1042.8 6.9 fusion
  (214 shorter events, 36.4 us)
Async XLA Ops:
  8.0 728.4 %reduce-scatter.7.cloned.1.call-start = ((), (), s32[]{:S(2)}) async-start(), calls=%async_computation.6 | async-start | bytes 1474560
  10.2 4.9 copy-start.23
  10.2 5.0 copy-start.26
  10.2 5.0 copy-start.27
  10.3 5.0 copy-start.28
  10.3 5.1 copy-start.29
  10.3 5.1 copy-start.30
  10.3 5.1 copy-start.31
  10.3 6.4 copy-start.8
  16.7 1.9 copy-start.11
  19.8 84.5 %copy-start.4 = (bf16[1,2,1,256,1536]{4,3,2,1,0:T(8,128)(2,1)S(1)}, bf16[1,2,1,256,1536]{4,3,2,1,0:T(8,128)(2,1)}, u32[]{:S(2)}) copy-start(bf16[1,2,1,256,1536]{4,3,2,1,0:T(8,128)(2,1)} %param.20) | copy-start | bytes 4718596
  102.5 2.2 copy-start.7
  105.9 199.2 %copy-start.1 = (bf16[2,128,1536]{2,1,0:T(8,128)(2,1)}, bf16[2,128,1536]{2,1,0:T(8,128)(2,1)S(1)}, u32[]{:S(2)}) copy-start(bf16[2,128,1536]{2,1,0:T(8,128)(2,1)S(1)} %slice_select_fusion.1) | copy-start | bytes 2359300
  114.1 0.5 copy-start.17
  115.8 102.2 %copy-start.12 = (f32[7,640]{1,0:T(8,128)}, f32[7,640]{1,0:T(8,128)S(1)}, u32[]{:S(2)}) copy-start(f32[7,640]{1,0:T(8,128)S(1)} %broadcast.122) | copy-start | bytes 53764
  218.7 0.6 copy-start.15
  222.4 1.2 copy-start.24
  222.4 1.2 copy-start.25
  222.4 1.2 copy-start.32
  222.4 1.2 copy-start.33
  222.4 1.3 copy-start.19
  223.6 1.2 copy-start.13
  223.6 1.3 copy-start.14
  305.2 2.4 copy-start.16
  307.5 95.8 %copy-start.20 = (f32[256]{0:T(256)S(1)}, f32[256]{0:T(256)}, u32[]{:S(2)}) copy-start(f32[256]{0:T(256)} %add_rsqrt_fusion.2) | copy-start | bytes 3076
  403.3 2.1 copy-start.2
  403.3 2.1 copy-start.5
  516.3 241.4 %reduce-scatter.9.cloned.1.call-start = ((), (), s32[]{:S(2)}) async-start(), calls=%async_computation.7 | async-start | bytes 1474560
  616.4 81.3 %copy-start = (bf16[384,1536]{1,0:T(8,128)(2,1)S(1)}, bf16[384,1536]{1,0:T(8,128)(2,1)}, u32[]{:S(2)}) copy-start(bf16[384,1536]{1,0:T(8,128)(2,1)} %get-tuple-element.86) | copy-start | bytes 3538948
  697.7 9.6 copy-start.34
  700.3 26.8 %collective-permute-start.2 = (bf16[384,1536]{1,0:T(8,128)(2,1)}, bf16[384,1536]{1,0:T(8,128)(2,1)}, u32[]{:S(2)}, u32[]{:S(2)}) collective-permute-start(bf16[384,1536]{1,0:T(8,128)(2,1)} %broadcast_select_fusion), channel_id=1, source_target_pairs={{0,16},{16,0},{1,17},{17,1},{2,18},{18,2},{3,19},{19,3},{4,20},{20... | collective-permute-start | bytes 3538952 | tf_op jit(solution)/shard_map/ppermute | solution.py:1319
  713.8 2.4 copy-start.22
  713.8 2.5 copy-start.21
  713.8 2.9 copy-start.18
  716.2 149.3 %all-reduce.16.cloned.1.call-start = ((), (), s32[]{:S(2)}) async-start(), calls=%async_computation.2 | async-start | bytes 344064 | tf_op jit(solution)/shard_map/psum | solution.py:1487
  720.5 201.7 %all-reduce.18.cloned.1.call-start = ((), (), s32[]{:S(2)}) async-start(), calls=%async_computation.3 | async-start | bytes 933888 | tf_op jit(solution)/shard_map/psum | solution.py:1472
  759.7 221.2 %all-reduce.20.cloned.1.call-start = ((), (), s32[]{:S(2)}) async-start(), calls=%async_computation.4 | async-start | bytes 4718592 | tf_op jit(solution)/shard_map/psum | solution.py:1485
  769.2 1.1 copy-start.9
  769.2 1.2 copy-start.10
  769.2 251.1 %all-gather.3.cloned.1.call-start = ((), (), s32[]{:S(2)}) async-start(), calls=%async_computation.5 | async-start | bytes 5898240 | tf_op jit(solution)/shard_map/all_gather | solution.py:1468
  770.5 14.5 %collective-permute-start.1 = (bf16[384,768]{1,0:T(8,128)(2,1)S(1)}, bf16[384,768]{1,0:T(8,128)(2,1)S(1)}, u32[]{:S(2)}, u32[]{:S(2)}) collective-permute-start(bf16[384,768]{1,0:T(8,128)(2,1)S(1)} %broadcast_select_fusion.2), channel_id=1, source_target_pairs={{0,16},{16,0},{1,17},{17,1},{2,18},{18,2},{3,19},{19,3},{4,20},{20... | collective-permute-start | bytes 1769480 | tf_op jit(solution)/shard_map/ppermute | solution.py:1319
  785.1 1.8 copy-start.3
  791.3 80.0 %copy-start.6 = (f32[256,1536]{1,0:T(8,128)S(1)}, f32[256,1536]{1,0:T(8,128)}, u32[]{:S(2)}) copy-start(f32[256,1536]{1,0:T(8,128)} %get-tuple-element.93) | copy-start | bytes 4718596
  791.3 79.8 %collective-permute-start = (bf16[2,128,1536]{2,1,0:T(8,128)(2,1)}, bf16[2,128,1536]{2,1,0:T(8,128)(2,1)S(1)}, u32[]{:S(2)}, u32[]{:S(2)}) collective-permute-start(bf16[2,128,1536]{2,1,0:T(8,128)(2,1)} %bitcast.34), channel_id=1, source_target_pairs={{0,16},{16,0},{1,17},{17,1},{2,18},{18,2},{3,19},{19,3},{4,20},{20... | collective-permute-start | bytes 2359304 | tf_op jit(solution)/shard_map/ppermute | solution.py:1319
Sparse Core Ops, SparseCore 0:
  516.4 51.0 reduce-scatter.6
  716.3 41.3 reduce-scatter.8
Sparse Core Ops, SparseCore 1:
  722.2 143.2 all-reduce.15
  868.5 53.7 all-reduce.17
  925.2 55.7 all-reduce.19
  982.5 37.7 all-gather.2

commit v4 on v3

--- a/solution.py
+++ b/solution.py
@@ -916,163 +916,464 @@
     )(own, pull, r_rows, pgx, ps, pgx, ps, res, ent, wgx, ws, wo, vec, tri, spread3, gather3)
 
 
-def line_barrier(place, count, axis):
-    sem = pltpu.get_barrier_semaphore()
-
-    @pl.when(place > 0)
-    def _():
-        pl.semaphore_signal(sem, inc=1, device_id={axis: place - 1}, device_id_type=MESH)
-
-    @pl.when(place < count - 1)
-    def _():
-        pl.semaphore_signal(sem, inc=1, device_id={axis: place + 1}, device_id_type=MESH)
-
-    inner = (place > 0) & (place < count - 1)
-
-    @pl.when(inner)
-    def _():
-        pl.semaphore_wait(sem, 2)
-
-    @pl.when(~inner)
-    def _():
-        pl.semaphore_wait(sem, 1)
-
-
 def reduce_kernel(
-    count, ranks, parts, axis,
-    full_ref, gp_ref, no_ref, gb_ref, out_ref, oout_ref,
-    sum_ref, osum_ref, in_ref, oin_ref,
-    send_sem, recv_sem, osend_sem, orecv_sem,
+    layers, ranks, parts, pr,
+    full_ref, gp_ref, gps_ref, no_ref, gb_ref, out_ref, oout_ref, tout_ref,
+    sum_ref, osum_ref, in_ref, oin_ref, thin_ref, thin_f, tz_ref, tin_ref, core_in, stage_in,
+    send_sem, recv_sem, osend_sem, orecv_sem, core_send, core_recv, rs_send, rs_recv, tz_send, tz_recv,
 ):
-    place = lax.axis_index(axis)
+    place, count = lax.axis_index("fsdp"), lax.axis_size("fsdp")
+    plane = Plane(layers, ranks)
     rows = out_ref.shape[0]
     piece = rows // parts
     orows = oout_ref.shape[0]
-    opiece = orows // parts
-    here = lax.axis_index("section") * ranks + lax.axis_index("seq")
-    source = (here * orows) // (ranks * lax.axis_size("section") * orows // count)
-    line_barrier(place, count, axis)
-
-    def hop(j, k, side):
-        to = place + 1 if side == 0 else place - 1
+    chain_barrier(plane, place, count)
+
+    thin_rows = gps_ref.shape[1]
+    thin_ref[pl.ds(0, thin_rows), :] = dot(gps_ref[...], full_ref[...], 0, 0).astype(BF16)
+    if thin_ref.shape[0] > thin_rows:
+        rest = thin_ref.shape[0] - thin_rows
+        thin_ref[pl.ds(thin_rows, rest), :] = jnp.zeros((rest, thin_ref.shape[1]), BF16)
+    thin = Collect(plane, thin_ref, 0, layers * pr, core_in, stage_in, core_send, core_recv, rs_send, rs_recv)
+    for c in range(ranks):
+        thin.block_done(c)
+    lines = Row(
+        place, count, lambda d: tz_ref.at[lax.rem(place + d, count)], lambda d: tin_ref.at[place], tz_send, tz_recv
+    )
+
+    def pair(j, k, side):
+        to = {"fsdp": place + 1 if side == 0 else place - 1}
+        if k == parts:
+            return pltpu.make_async_remote_copy(
+                src_ref=osum_ref.at[j], dst_ref=oin_ref.at[side, j], send_sem=osend_sem.at[j],
+                recv_sem=orecv_sem.at[side, j], device_id=to, device_id_type=MESH,
+            )
         return pltpu.make_async_remote_copy(
-            src_ref=sum_ref.at[j, k], dst_ref=in_ref.at[side, j, k],
-            send_sem=send_sem.at[j, k], recv_sem=recv_sem.at[side, j, k],
-            device_id={axis: to}, device_id_type=MESH,
+            src_ref=sum_ref.at[j, k], dst_ref=in_ref.at[side, j, k], send_sem=send_sem.at[j, k],
+            recv_sem=recv_sem.at[side, j, k], device_id=to, device_id_type=MESH,
         )
 
-    def ohop(k, side):
-        to = place + 1 if side == 0 else place - 1
-        return pltpu.make_async_remote_copy(
-            src_ref=osum_ref.at[k], dst_ref=oin_ref.at[side, k],
-            send_sem=osend_sem.at[k], recv_sem=orecv_sem.at[side, k],
-            device_id={axis: to}, device_id_type=MESH,
-        )
-
-    ends = (place < count - 1, place > 0)
-    before = (place > 0, place < count - 1)
-
     def work(j, k):
-        sum_ref[j, k] = dot(
-            full_ref[:, j * rows + k * piece : j * rows + (k + 1) * piece], gp_ref[...], 0, 0
-        ).astype(BF16)
+        if k == parts:
+            osum_ref[j] = dot(no_ref[:, j * orows : (j + 1) * orows], gb_ref[...], 0, 0).astype(BF16)
+        else:
+            cut = slice(j * rows + k * piece, j * rows + (k + 1) * piece)
+            sum_ref[j, k] = dot(full_ref[:, cut], gp_ref[...], 0, 0).astype(BF16)
+
+    def absorb(j, k, side):
+        pair(j, k, side).wait_recv()
+        if k == parts:
+            osum_ref[j] = (osum_ref[j].astype(F32) + oin_ref[side, j].astype(F32)).astype(BF16)
+        else:
+            sum_ref[j, k] = (sum_ref[j, k].astype(F32) + in_ref[side, j, k].astype(F32)).astype(BF16)
+
+    behind = (place > 0, place < count - 1)
 
     def shift(j, k):
         for side in (0, 1):
             beyond = (place < j) if side == 0 else (place > j)
 
-            @pl.when(beyond & before[side])
+            @pl.when(beyond & behind[side])
             def _(side=side):
-                hop(j, k, side).wait_recv()
-                sum_ref[j, k] = (sum_ref[j, k].astype(F32) + in_ref[side, j, k].astype(F32)).astype(BF16)
+                absorb(j, k, side)
 
             @pl.when(beyond)
             def _(side=side):
-                hop(j, k, side).start()
+                pair(j, k, side).start()
 
     order = []
     low, high = 0, count - 1
     while low <= high:
         order += [high] if low == high else [high, low]
         low, high = low + 1, high - 1
-    order = [(j, k) for pair in range(0, len(order), 2) for k in range(parts) for j in order[pair : pair + 2]]
-    for j, k in order:
+    items = [(j, k) for p in range(0, len(order), 2) for k in range(parts + 1) for j in order[p : p + 2]]
+    todo = [lambda: ([thin.block_add(c) for c in range(ranks)], thin.begin(0))]
+    for stage in range(plane.stages):
+        def advance(stage=stage):
+            thin.add(stage, thin_f, 0)
+            if stage + 1 < plane.stages:
+                thin.begin(stage + 1)
+        todo.append(advance)
+
+    def across():
+        wide = tz_ref.shape[2]
+        for j in range(count):
+            tz_ref[j] = thin_f[:, j * wide : (j + 1) * wide].astype(BF16)
+        lines.begin()
+
+    todo.append(across)
+    for number, (j, k) in enumerate(items):
         work(j, k)
         shift(j, k)
-    for k in range(parts):
-        osum_ref[k] = dot(no_ref[:, k * opiece : (k + 1) * opiece], gb_ref[...], 0, 0).astype(BF16)
-        for side in (0, 1):
-            beyond = (place < source) if side == 0 else (place > source)
-
-            @pl.when(beyond & before[side])
-            def _(side=side, k=k):
-                ohop(k, side).wait_recv()
-                osum_ref[k] = (osum_ref[k].astype(F32) + oin_ref[side, k].astype(F32)).astype(BF16)
-
-            @pl.when(beyond)
-            def _(side=side, k=k):
-                ohop(k, side).start()
-
-    for k in range(parts):
+        if number % 2 == 1 and todo:
+            todo.pop(0)()
+    while todo:
+        todo.pop(0)()
+    for k in range(parts + 1):
         for j in range(count):
             for side in (0, 1):
-                @pl.when((place == j) & before[side])
+                @pl.when((place == j) & behind[side])
                 def _(side=side, k=k, j=j):
-                    hop(j, k, side).wait_recv()
-                    sum_ref[j, k] = (sum_ref[j, k].astype(F32) + in_ref[side, j, k].astype(F32)).astype(BF16)
+                    absorb(j, k, side)
 
             @pl.when(place == j)
             def _(k=k, j=j):
-                out_ref[pl.ds(k * piece, piece), :] = sum_ref[j, k]
-
-    for k in range(parts):
-        for side in (0, 1):
-            @pl.when((place == source) & before[side])
-            def _(side=side, k=k):
-                ohop(k, side).wait_recv()
-                osum_ref[k] = (osum_ref[k].astype(F32) + oin_ref[side, k].astype(F32)).astype(BF16)
-
-        oout_ref[pl.ds(k * opiece, opiece), :] = osum_ref[k]
-
-        @pl.when(place != source)
-        def _(k=k):
-            ohop(k, 0).wait_send()
-
+                if k == parts:
+                    oout_ref[...] = osum_ref[j]
+                else:
+                    out_ref[pl.ds(k * piece, piece), :] = sum_ref[j, k]
+
+    lines.finish()
+    total = tz_ref[place].astype(F32)
+    for d in range(1, count):
+        total = total + tin_ref[lax.rem(place + d, count)].astype(F32)
+    tout_ref[...] = total.astype(BF16)
+    lines.drain()
+    thin.drain()
+    for k in range(parts + 1):
         for j in range(count):
             @pl.when(place != j)
             def _(k=k, j=j):
-                hop(j, k, 0).wait_send()
-
-
-def reduce_gradients(full, gp, no, gb, number):
-    count, ranks = lax.axis_size("fsdp"), lax.axis_size("seq")
+                pair(j, k, 0).wait_send()
+
+
+def reduce_gradients(full, gp, gps, no, gb, number):
+    layers, ranks, count = lax.axis_size("section"), lax.axis_size("seq"), lax.axis_size("fsdp")
+    size = layers * ranks
     tokens, width = full.shape
-    rows, cols, orows = width // count, gp.shape[1], no.shape[1]
-    parts = 3 if rows % 384 == 0 and orows % 384 == 0 else 1
+    rows, cols, orows = width // count, gp.shape[1], no.shape[1] // count
+    parts = 3 if rows % 384 == 0 else 1
+    pr = -(-gps.shape[1] // (32 * size)) * 32
+    dma = pltpu.SemaphoreType.DMA
     return pl.pallas_call(
-        functools.partial(reduce_kernel, count, ranks, parts, "fsdp"),
-        in_specs=[whole(a) for a in (full, gp, no, gb)],
-        out_specs=[pl.BlockSpec(memory_space=pltpu.VMEM)] * 2,
-        out_shape=[jax.ShapeDtypeStruct((rows, cols), BF16), jax.ShapeDtypeStruct((orows, width), BF16)],
+        functools.partial(reduce_kernel, layers, ranks, parts, pr),
+        in_specs=[whole(a) for a in (full, gp, gps, no, gb)],
+        out_specs=[pl.BlockSpec(memory_space=pltpu.VMEM)] * 3,
+        out_shape=[
+            jax.ShapeDtypeStruct((rows, cols), BF16),
+            jax.ShapeDtypeStruct((orows, width), BF16),
+            jax.ShapeDtypeStruct((pr, width // count), BF16),
+        ],
         scratch_shapes=[
             pltpu.VMEM((count, parts, rows // parts, cols), BF16),
-            pltpu.VMEM((parts, orows // parts, width), BF16),
+            pltpu.VMEM((count, orows, width), BF16),
             pltpu.VMEM((2, count, parts, rows // parts, cols), BF16),
-            pltpu.VMEM((2, parts, orows // parts, width), BF16),
-            pltpu.SemaphoreType.DMA((count, parts)),
-            pltpu.SemaphoreType.DMA((2, count, parts)),
-            pltpu.SemaphoreType.DMA((parts,)),
-            pltpu.SemaphoreType.DMA((2, parts)),
+            pltpu.VMEM((2, count, orows, width), BF16),
+            pltpu.VMEM((size * pr, width), BF16),
+            pltpu.VMEM((pr, width), F32),
+            pltpu.VMEM((count, pr, width // count), BF16),
+            pltpu.VMEM((count, pr, width // count), BF16),
+            pltpu.VMEM((ranks // 2, layers * pr, width), BF16),
+            pltpu.VMEM((2, size // 2, pr // 2, width), BF16),
+            dma((count, parts)),
+            dma((2, count, parts)),
+            dma((count,)),
+            dma((2, count)),
+            dma((ranks,)),
+            dma((ranks,)),
+            dma((2, size // 2)),
+            dma((2, size // 2)),
+            dma((count,)),
+            dma((count,)),
         ],
         compiler_params=pltpu.CompilerParams(
-            collective_id=number, has_side_effects=True, vmem_limit_bytes=56 << 20
+            collective_id=number, has_side_effects=True, vmem_limit_bytes=60 << 20
         ),
         cost_estimate=pl.CostEstimate(
-            flops=2 * tokens * (width * cols + orows * width), bytes_accessed=2 * tokens * (2 * width + cols + orows),
-            transcendentals=0,
+            flops=2 * tokens * (width * cols + orows * count * width),
+            bytes_accessed=2 * tokens * (2 * width + cols + orows), transcendentals=0,
         ),
         name="reduce_gradients",
-    )(full, gp, no, gb)
+    )(full, gp, gps, no, gb)
+
+
+class Publish:
+    def __init__(self, plane, cells, view, other, condition, send, recv):
+        self.plane, self.cells, self.view, self.other, self.condition = plane, cells, view, other, condition
+        self.send, self.recv = send, recv
+        self.outer = [dim for dim in range(2, plane.stages + 1)]
+
+    def number(self, mask):
+        sec, seq = self.plane.owner(mask)
+        return sec * self.plane.ranks + seq
+
+    def copy(self, mask, dim, cell):
+        dst = self.view(self.number(mask), cell)
+        src = self.other(cell) if dim == 1 else dst
+        key = mask ^ (1 << dim)
+        return pltpu.make_async_remote_copy(
+            src_ref=src, dst_ref=dst, send_sem=self.send.at[key, cell], recv_sem=self.recv.at[key, cell],
+            device_id=self.plane.partner(dim), device_id_type=MESH,
+        )
+
+    def each(self, mask, act):
+        @pl.when(self.condition(self.number(mask)))
+        def _():
+            for cell in range(self.cells):
+                act(cell)
+
+    def stage(self, mask):
+        return max([i for i, dim in enumerate(self.outer) if mask >> dim & 1], default=-1)
+
+    def forward(self, mask):
+        later = self.outer[self.stage(mask) + 1 :] + [0]
+
+        def act(cell):
+            for dim in later:
+                self.copy(mask, dim, cell).start()
+
+        self.each(mask, act)
+
+    def begin(self):
+        self.each(0, lambda cell: self.copy(0, 1, cell).start())
+        self.forward(0)
+
+    def arrived(self, mask):
+        def act(cell):
+            view = self.view(self.number(mask), cell)
+            pltpu.make_async_remote_copy(
+                src_ref=view, dst_ref=view, send_sem=self.send.at[mask, cell], recv_sem=self.recv.at[mask, cell],
+                device_id=self.plane.partner(0), device_id_type=MESH,
+            ).wait_recv()
+
+        self.each(mask, act)
+
+    def step(self, stage):
+        for mask in self.plane.masks[1:]:
+            if self.stage(mask) == stage:
+                self.arrived(mask)
+                self.forward(mask)
+
+    def finish(self):
+        for mask in self.plane.masks:
+            self.arrived(mask + 1)
+
+    def drain(self):
+        for mask in self.plane.masks:
+            dims = self.outer[self.stage(mask) + 1 :] + [0] + ([1] if mask == 0 else [])
+
+            def act(cell, mask=mask, dims=dims):
+                for dim in dims:
+                    self.copy(mask, dim, cell).wait_send()
+
+            self.each(mask, act)
+
+
+def publish_kernel(
+    layers, ranks, parts, wide, pr,
+    gx0, gx1, o0, o1, thin_ref, sm_ref, gn_ref, swap_ref,
+    gall, oall, tall, sm_all, gn_out, got_ref,
+    tmp_o, sm_in, gn_in, gn_plane,
+    own_sem, swap_send, swap_recv, z_send, z_recv, g_send, g_recv, p_send, p_recv, q_send, q_recv, t_send, t_recv,
+    s_send, s_recv, n_send, n_recv, zs_send, zs_recv, zn_send, zn_recv,
+):
+    place, count = lax.axis_index("fsdp"), lax.axis_size("fsdp")
+    plane = Plane(layers, ranks)
+    low = plane.sec == 0
+    here = plane.sec * ranks + plane.seq
+    rows, cols = gx0.shape
+    cw = cols // 2
+    piece = rows // parts
+    per = plane.size // count
+    chain_barrier(plane, place, count)
+
+    sm_lines = Row(place, count, lambda d: sm_ref, lambda d: sm_in.at[d], zs_send, zs_recv)
+    gn_lines = Row(place, count, lambda d: gn_ref, lambda d: gn_in.at[d], zn_send, zn_recv)
+    sm_lines.begin()
+    gn_lines.begin()
+
+    def gx_window(d, cell):
+        k, w = cell // wide, cell % wide
+        span = pl.ds(k * piece, piece)
+        if wide == 1:
+            return gall.at[d, span, :]
+        start = pl.multiple_of(d * cw + w * cw * plane.size, STATE)
+        return gall.at[span, pl.ds(start, cw)]
+
+    def gx_source(ref, cell):
+        k, w = cell // wide, cell % wide
+        span = pl.ds(k * piece, piece)
+        return ref.at[span, :] if wide == 1 else ref.at[span, pl.ds(w * cw, cw)]
+
+    home = here // per
+    at_home = home == place
+
+    def gather_o(layer, ref):
+        def copy(local):
+            dst = oall.at[lax.rem(here, per) * count + place] if local else tmp_o.at[place]
+            return dst
+
+        def remote(dst, number):
+            return pltpu.make_async_remote_copy(
+                src_ref=ref, dst_ref=dst, send_sem=z_send.at[layer], recv_sem=z_recv.at[layer, number],
+                device_id={"fsdp": home}, device_id_type=MESH,
+            )
+
+        def begin():
+            for mine in (True, False):
+                which = (plane.sec == layer) if mine else (plane.sec != layer)
+
+                @pl.when(which & at_home)
+                def _(mine=mine):
+                    pltpu.make_async_copy(ref, copy(mine), own_sem.at[1 + layer]).start()
+
+                @pl.when(which & ~at_home)
+                def _(mine=mine):
+                    remote(copy(mine), place).start()
+
+        def finish():
+            @pl.when(at_home)
+            def _():
+                pltpu.make_async_copy(ref, tmp_o.at[place], own_sem.at[1 + layer]).wait()
+                for d in range(1, count):
+                    remote(tmp_o.at[place], lax.rem(place + d, count)).wait_recv()
+
+            @pl.when(~at_home)
+            def _():
+                remote(tmp_o.at[place], place).wait_send()
+
+        return begin, finish
+
+    gathers = [gather_o(0, o0), gather_o(1, o1)]
+    for begin, _ in gathers:
+        begin()
+
+    gpub = [
+        Publish(plane, parts * wide, gx_window, lambda cell, ref=ref: gx_source(ref, cell), lambda d: d >= 0, g_send, g_recv)
+        for ref in (gx1, gx0)
+    ]
+    opub = Publish(
+        plane, count, lambda d, cell: oall.at[lax.rem(d, per) * count + cell], lambda cell: tmp_o.at[cell],
+        lambda d: d // per == place, p_send, p_recv,
+    )
+    cells = parts * wide
+
+    def own(ref):
+        return [pltpu.make_async_copy(gx_source(ref, c), gx_window(here, c), own_sem.at[4 + c]) for c in range(cells)]
+
+    for number, ref in enumerate((gx0, gx1)):
+        @pl.when(plane.sec == number)
+        def _(ref=ref):
+            for c in own(ref):
+                c.start()
+
+    for number in range(layers):
+        @pl.when(plane.sec == number)
+        def _(number=number):
+            gpub[number].each(0, lambda cell: gpub[number].copy(0, 1, cell).start())
+
+    for c in own(gx0):
+        c.wait()
+    gpub[0].forward(0)
+
+    spread = Spread(
+        plane, tall, lambda sec, seq: (seq * layers + sec) * pr, pr, t_send, t_recv
+    )
+    tall[pl.ds(pl.multiple_of((plane.seq * layers + plane.sec) * pr, 16), pr), :] = thin_ref[...]
+    spread.begin()
+    sm_lines.finish()
+    gn_lines.finish()
+    mine, gain = sm_ref[...], gn_ref[...]
+    for d in range(1, count):
+        mine, gain = mine + sm_in[d], gain + gn_in[d]
+    sm_all[here] = mine
+    gn_plane[0] = gain
+    shares = [
+        Share(plane, sm_all.at[here], lambda mask: sm_all.at[here], s_send, s_recv),
+        Share(plane, gn_plane.at[0], lambda mask: gn_plane.at[mask], n_send, n_recv),
+    ]
+    for share in shares:
+        share.begin()
+    spread.hop(0)
+    for _, finish in gathers:
+        finish()
+    opub.begin()
+    swap = pltpu.make_async_remote_copy(
+        src_ref=swap_ref, dst_ref=got_ref, send_sem=swap_send.at[0], recv_sem=swap_recv.at[0],
+        device_id=plane.partner(1), device_id_type=MESH,
+    )
+    swap.start()
+    gpub[0].step(-1)
+    for stage in range(1, plane.stages):
+        spread.hop(stage)
+    for stage in range(len(opub.outer)):
+        gpub[0].step(stage)
+    opub.step(-1)
+    for stage in range(len(opub.outer)):
+        opub.step(stage)
+    gpub[0].finish()
+    opub.finish()
+    spread.finish()
+    for share in shares:
+        share.finish()
+    total = gn_plane[0]
+    for mask in range(1, plane.size):
+        total = total + gn_plane[mask]
+    gn_out[...] = total
+    swap.wait()
+    for each in [gpub[0], opub, spread, sm_lines, gn_lines] + shares:
+        each.drain()
+
+
+def publish(gx0, gx1, o0, o1, thin, sm, gn, swap, number):
+    layers, ranks, count = lax.axis_size("section"), lax.axis_size("seq"), lax.axis_size("fsdp")
+    size = layers * ranks
+    rows, cols = gx0.shape
+    cw = cols // 2
+    wide = 2 if cw % STATE == 0 else 1
+    parts = 2
+    cells = parts * wide
+    per = size // count
+    orows, width = o0.shape
+    pr, tcols = thin.shape
+    dma = pltpu.SemaphoreType.DMA
+    anywhere = pl.BlockSpec(memory_space=pl.ANY)
+    vmem = pl.BlockSpec(memory_space=pltpu.VMEM)
+    gall = (rows, size * cols) if wide == 2 else (size, rows, cols)
+    return pl.pallas_call(
+        functools.partial(publish_kernel, layers, ranks, parts, wide, pr),
+        in_specs=[anywhere] * 4 + [vmem] * 3 + [anywhere],
+        out_specs=[anywhere, anywhere, vmem, vmem, vmem, anywhere],
+        out_shape=[
+            jax.ShapeDtypeStruct(gall, BF16),
+            jax.ShapeDtypeStruct((per * count, orows, width), BF16),
+            jax.ShapeDtypeStruct((size * pr, tcols), BF16),
+            jax.ShapeDtypeStruct((size,) + sm.shape, F32),
+            jax.ShapeDtypeStruct(gn.shape, F32),
+            jax.ShapeDtypeStruct(swap.shape, BF16),
+        ],
+        scratch_shapes=[
+            pltpu.VMEM((count, orows, width), BF16),
+            pltpu.VMEM((count,) + sm.shape, F32),
+            pltpu.VMEM((count,) + gn.shape, F32),
+            pltpu.VMEM((size,) + gn.shape, F32),
+            dma((4 + cells,)),
+            dma((1,)),
+            dma((1,)),
+            dma((layers,)),
+            dma((layers, count)),
+            dma((size, cells)),
+            dma((size, cells)),
+            dma((size, count)),
+            dma((size, count)),
+            dma((1,)),
+            dma((1,)),
+            dma((2, size)),
+            dma((2, size)),
+            dma((size,)),
+            dma((size,)),
+            dma((size,)),
+            dma((size,)),
+            dma((count,)),
+            dma((count,)),
+            dma((count,)),
+            dma((count,)),
+        ],
+        compiler_params=pltpu.CompilerParams(
+            collective_id=number, has_side_effects=True, vmem_limit_bytes=40 << 20
+        ),
+        name="publish",
+    )(gx0, gx1, o0, o1, thin, sm, gn, swap)
 
 
 def start_kernel(
@@ -1429,8 +1730,7 @@
         gn, gpgx, gps, no, tiny, gb = layer_backward(
             low, pull, r_rows, pgx, ps, res, ent, wgx, ws, wo, vecs[layer], taps, 3 * layers + layer
         )
-        g_gx, g_o = reduce_gradients(full, gpgx, no, gb, layers + layer)
-        g_s = dot(full, gps, 0, 0).astype(BF16)
+        big[layer] = reduce_gradients(full, gpgx, gps, no, gb, 4 * layers + layer)
         unit = before * rs
         g_gain = jnp.sum(gn * unit, axis=0)
         gn = gn * gains[layer]
@@ -1438,56 +1738,31 @@
         if layer > 0:
             grad = grad.astype(BF16).astype(F32)
 
-        def placed(v, count, begin):
-            return lax.dynamic_update_slice(jnp.zeros((count,), F32), v, (begin,))
-
-        conv = lax.dynamic_update_slice(jnp.zeros((taps + 1, chans), F32), tiny[: taps + 1, :cw], (0, here * cw))
-        conv = conv + jnp.pad(tiny[: taps + 1, cw:], ((0, 0), (inner, 0)))
-        small[layer] = jnp.concatenate(
-            [g_gain, conv.reshape(-1), placed(tiny[5, :cw], inner, here * cw)]
-            + [placed(tiny[n, :heads], heads_all, here * heads) for n in (6, 7, 8)]
-        )
-        g_s = g_s[:, : shared + heads_all]
-        g_s = lax.psum_scatter(g_s, "fsdp", scatter_dimension=0, tiled=True)
-        big[layer] = (g_gx, g_s, g_o)
+        small[layer] = (tiny, g_gain)
 
     output = output.reshape(layers, piece, width)
     grad = grad.reshape(layers, piece, width)
-    got = swapped(jnp.where(low_layer, output, grad).astype(BF16), "section").astype(F32)
+    g_norm = jnp.pad(jnp.stack([s[1] for s in small]), ((0, 8 - layers), (0, 0)))
+    gall, oall, tall, sm, g_norm, got = publish(
+        big[0][0], big[1][0], big[0][1], big[1][1], jnp.concatenate([b[2] for b in big], 1),
+        jnp.stack([s[0] for s in small]), g_norm, jnp.where(low_layer, output, grad).astype(BF16), 6 * layers
+    )
+    got = got.astype(F32)
     results = jnp.where(low_layer, jnp.concatenate([grad, got], 1), jnp.concatenate([got, output], 1))
     section_results = results[None, :, None]
-
-    def own_layer(values):
-        own = jnp.where(low_layer, values[0], values[1])
-        other = jnp.where(low_layer, values[1], values[0])
-        return own, other
-
-    own, other = own_layer([b[0] for b in big])
-    other = swapped(other, "section")
-    pair = jnp.stack([jnp.where(low_layer, own, other), jnp.where(low_layer, other, own)])
-    gx = lax.all_gather(pair, "seq")
-    rows = gx.shape[2]
-    gx = gx.reshape(ranks, layers, rows, 2, cw)
-    gx = jnp.transpose(gx, (2, 3, 1, 0, 4)).reshape(rows, 2 * inner)
-    s_all = lax.psum(jnp.stack([b[1] for b in big]), PLANE)
-    s_own, _ = own_layer([s_all[0], s_all[1]])
-    grad_in = jnp.concatenate([gx.astype(F32), s_own.astype(F32)], 1)[None]
-
-    own, other = own_layer([b[2] for b in big])
-    other = swapped(other, "section")
-    pair = jnp.stack([jnp.where(low_layer, own, other), jnp.where(low_layer, other, own)])
-    spread = jnp.zeros((out_rows, width), BF16)
-    for s in range(layers):
-        start = (s * ranks + seq) * cw - dep * out_rows
-        inside = (start >= 0) & (start < out_rows)
-        block = jnp.where(inside, pair[s], jnp.zeros_like(pair[s]))
-        spread = spread + lax.dynamic_update_slice(jnp.zeros_like(spread), block, (jnp.clip(start, 0, out_rows - cw), 0))
-    grad_out = lax.psum(spread, "seq").astype(F32)[None]
-
-    tiny = lax.psum(jnp.stack(small), EVERY)
-    tiny = jnp.where(low_layer, tiny[0], tiny[1])
-    cuts = np.cumsum([0, width, taps * chans, chans, inner, heads_all, heads_all, heads_all])
-    parts = [tiny[cuts[i] : cuts[i + 1]] for i in range(7)]
+    if gall.ndim == 3:
+        rows = gall.shape[1]
+        gall = jnp.transpose(gall.reshape(group, rows, 2, cw), (1, 2, 0, 3)).reshape(rows, 2 * inner)
+    share_d = tall.shape[1] // layers
+    thin = jnp.where(low_layer, tall[: shared + heads_all, :share_d], tall[: shared + heads_all, share_d:])
+    grad_in = jnp.concatenate([gall.astype(F32), thin.astype(F32).T], 1)[None]
+    grad_out = oall.reshape(out_rows, width).astype(F32)[None]
+
+    sm = jnp.where(low_layer, sm[:, 0], sm[:, 1])
+    conv = jnp.transpose(sm[:, : taps + 1, :cw], (1, 0, 2)).reshape(taps + 1, inner)
+    conv = jnp.concatenate([conv, jnp.sum(sm[:, : taps + 1, cw:], 0)], 1)
+    by_head = jnp.transpose(sm[:, 6:9, :heads], (1, 0, 2)).reshape(3, heads_all)
+    g_norm = jnp.where(low_layer, g_norm[0], g_norm[1])
 
     def share(v):
         count = v.shape[-1] // depth
@@ -1495,14 +1770,14 @@
 
     return (
         section_results,
-        share(parts[0]),
+        share(g_norm),
         grad_in,
-        share(parts[1].reshape(taps, chans)),
-        share(parts[2]),
-        share(parts[4]),
-        share(parts[5]),
-        share(parts[6]),
-        share(parts[3]),
+        share(conv[:taps]),
+        share(conv[taps]),
+        share(by_head[0]),
+        share(by_head[1]),
+        share(by_head[2]),
+        share(sm[:, 5, :cw].reshape(-1)),
         grad_out,
     )
 

time: 1070 us -> 829 us (0.77)
  waiting for transfers between devices: 253 us -> 0 us
  Pallas kernels: 638 us -> 727 us
  local copies, waits for them, and re-layouts: 77.4 us -> 48.1 us
  other arithmetic: 51.2 us -> 35.8 us
  between operations: 16.6 us -> 1.4 us
  matrix products: 11.3 us -> 0 us
    psum x3 -> x0, waiting for transfers between devices: 178 us -> none  [the longest x1 72.9 us: per_device(): tiny = lax.psum(jnp.stack(small), EVERY)]
    pallas_call x2 -> x3, Pallas kernels: 181 us -> 272 us  [the longest x2 171 us: reduce_gradients(): pl.pallas_call(functools.partial(reduce_kernel, layers, ranks, parts, pr)...]
    all_gather x1 -> x0, waiting for transfers between devices: 34.9 us -> none  [per_device(): gx = lax.all_gather(pair, 'seq')]
    convert_element_type x2 -> x0, local copies, waits for them, and re-layouts: 22.5 us -> none  [per_device(): grad_in = jnp.concatenate([gx.astype(F32), s_own.astype(F32)], 1)[None]]
    unnamed x8 -> x0, waiting for transfers between devices: 20.2 us -> none
    ppermute x3 -> x0, waiting for transfers between devices: 19.8 us -> none  [swapped(): return lax.ppermute(value, axis, [(i, count - 1 - i) for i in range(count)])]
    unnamed x74 -> x63, local copies, waits for them, and re-layouts: 8.72 us -> 20.9 us
    dot_general x2 -> x0, matrix products: 11.3 us -> none  [dot(): lax.dot_general(a, b, (((ca,), (cb,)), ((), ())), preferred_element_type=...]
  transfers between devices with their start and end apart: 9 -> 0, of which waited for: 7 -> 0; matrix products, arithmetic and copies ran while one was open for 5% -> 0% of each run, Pallas kernels for 17% -> 0%
where the time goes in v4:
time: 829 us; the launch traced here: 813 us
  Pallas kernels  727 us (88%)
  local copies, waits for them, and re-layouts  48.1 us (6%)
  other arithmetic  35.8 us (4%)
    pallas_call x2, Pallas kernels, layer_backward(): pl.pallas_call(functools.partial(backward_kernel, layers, heads, blocks,...  195 us
    pallas_call x2, Pallas kernels, layer_forward(): pl.pallas_call(functools.partial(forward_kernel, layers, heads, blocks, t...  178 us
    pallas_call x2, Pallas kernels, reduce_gradients(): pl.pallas_call(functools.partial(reduce_kernel, layers, ranks, parts, pr)...  171 us
    pallas_call x1, Pallas kernels, publish(): pl.pallas_call(functools.partial(publish_kernel, layers, ranks, parts, wi...  101 us
    pallas_call x1, Pallas kernels, start_up(): pl.pallas_call(functools.partial(start_kernel, layers, ranks, parts, opar...  82.7 us
    unnamed x63, local copies, waits for them, and re-layouts  20.9 us

profile of v4, /device:TPU:19, one launch (start us, length us, event | category | flops | bytes accessed | tf_op | source)
XLA Modules:
  0.0 812.7 jit_solution(9286253200993227540)
XLA Ops:
  0.7 2.1 constant_dynamic-slice_fusion.8
  3.4 1.3 copy.45
  4.7 1.1 pad_maximum_fusion
  5.9 2.0 constant_dynamic-slice_fusion.5
  7.9 1.0 constant_dynamic-slice_fusion.4
  10.5 82.7 %start_up.1 = (bf16[1536,768]{1,0:T(8,128)(2,1)}, bf16[4,96,1536]{2,1,0:T(8,128)(2,1)}, bf16[384,768]{1,0:T(8,128)(2,1)}, bf16[96,1536]{1,0:T(8,128)(2,1)}, bf16...) custom-call(bf16[384,768]{1,0:T(8,128)(2,1)} %get-tuple-element.166.mine, ...), custom_call_target="tpu_custom_call" | custom-call | tf_op jit(solution)/shard_map/start_up/pallas_call | solution.py:1581
  93.2 1.0 reshape.265
  95.6 1.2 concatenate.73.refs_4_.vec_ref
  98.0 1.2 concatenate.70.refs_4_.vec_ref
  99.3 2.9 fusion.38
  102.2 1.2 copy.47
  104.6 1.1 fusion.19.refs_0_
  105.7 99.8 %layer_forward.2 = (f32[256,1536]{1,0:T(8,128)}, f32[2,8,256]{2,1,0:T(8,128)}, bf16[2048,768]{1,0:T(8,128)(2,1)}, bf16[2048,384]{1,0:T(8,128)(2,1)}, bf16[2048,3...) custom-call(bf16[256,1536]{1,0:T(8,128)(2,1)} %fusion.19.refs_0_, ...), custom_call_target="tpu_custom_call" | custom-call | flops 10764681216 | bytes 23592960 | tf_op jit(solution)/shard_map/layer_forward/pallas_call | solution.py:799
  205.6 0.7 add_rsqrt_fusion.1.r_ref
  206.4 1.8 fusion.14
  208.3 1.1 fusion.9.refs_0_
  209.6 1.2 copy.49
  210.8 78.4 %layer_forward.3 = (f32[256,1536]{1,0:T(8,128)}, f32[2,8,256]{2,1,0:T(8,128)}, bf16[2048,768]{1,0:T(8,128)(2,1)}, bf16[2048,384]{1,0:T(8,128)(2,1)}, bf16[2048,3...) custom-call(bf16[256,1536]{1,0:T(8,128)(2,1)} %fusion.9.refs_0_, ...), custom_call_target="tpu_custom_call" | custom-call | flops 10764681216 | bytes 23592960 | tf_op jit(solution)/shard_map/layer_forward/pallas_call | solution.py:799
  289.3 0.8 add_rsqrt_fusion.r_ref
  290.1 1.5 slice_select_fusion.1
  292.5 95.7 %layer_backward.2 = (f32[256,1536]{1,0:T(8,128)}, bf16[2048,768]{1,0:T(8,128)(2,1)}, bf16[2048,384]{1,0:T(8,128)(2,1)}, bf16[2048,384]{1,0:T(8,128)(2,1)}, f32[1...) custom-call(bf16[256,1536]{1,0:T(8,128)(2,1)} %bitcast.112, f32[2,8,128]{2,1,0:T(8,128)} %broadcast_in_dim.78.pull_own, ...), custom_call_target="tpu_custom_call" | custom-call | flops 12809404416 | bytes 23592960 | tf_op jit(solution)/shard_map/layer_backward/pallas_call | solution.py:864
  388.2 2.1 fusion.13
  390.4 3.0 fusion.8
  394.0 99.3 %layer_backward.3 = (f32[256,1536]{1,0:T(8,128)}, bf16[2048,768]{1,0:T(8,128)(2,1)}, bf16[2048,384]{1,0:T(8,128)(2,1)}, bf16[2048,384]{1,0:T(8,128)(2,1)}, f32[1...) custom-call(bf16[256,1536]{1,0:T(8,128)(2,1)} %get-tuple-element.135.own_ref, f32[2,8,128]{2,1,0:T(8,128)} %broadcast_in_dim.80.pull_own, ...), custom_call_target="tpu_custom_call" | custom-call | flops 12809404416 | bytes 23592960 | tf_op jit(solution)/shard_map/layer_backward/pallas_call | solution.py:864
  493.3 2.1 fusion.20
  495.4 2.7 select_convert_fusion
  498.2 85.7 %reduce_gradients.3 = (bf16[384,768]{1,0:T(8,128)(2,1)}, bf16[96,1536]{1,0:T(8,128)(2,1)}, bf16[64,384]{1,0:T(8,128)(2,1)}) custom-call(bf16[2048,1536]{1,0:T(8,128)(2,1)} %get-tuple-element.86.full_ref, bf16[2048,768]{1,0:T(8,128)(2,1)} %get-tuple-element.87.gp_ref, bf16[2048,384]{1,0:T(8,128)(2,1)} %get-tuple-element.88.gps_ref, ...), custom_call_target="tpu_custom_call" | custom-call | flops 7247757312 | bytes 16121856 | tf_op jit(solution)/shard_map/reduce_gradients/pallas_call | solution.py:1048
  583.9 84.8 %reduce_gradients.2 = (bf16[384,768]{1,0:T(8,128)(2,1)}, bf16[96,1536]{1,0:T(8,128)(2,1)}, bf16[64,384]{1,0:T(8,128)(2,1)}) custom-call(bf16[2048,1536]{1,0:T(8,128)(2,1)} %get-tuple-element.80.full_ref, bf16[2048,768]{1,0:T(8,128)(2,1)} %get-tuple-element.81.gp_ref, bf16[2048,384]{1,0:T(8,128)(2,1)} %get-tuple-element.82.gps_ref, ...), custom_call_target="tpu_custom_call" | custom-call | flops 7247757312 | bytes 16121856 | tf_op jit(solution)/shard_map/reduce_gradients/pallas_call | solution.py:1048
  668.8 0.8 pad_maximum_fusion.2.thin_ref
  669.6 1.1 copy-done.1
  670.6 1.1 copy-done.2
  671.7 1.0 copy-done.3
  672.7 1.0 copy-done.4
  673.6 101.0 %publish.1 = (bf16[384,6144]{1,0:T(8,128)(2,1)S(1)}, bf16[8,96,1536]{2,1,0:T(8,128)(2,1)S(1)}, bf16[512,768]{1,0:T(8,128)(2,1)S(1)}, f32[8,2,16,640]{3,2,1,0:T(8...) custom-call(bf16[384,768]{1,0:T(8,128)(2,1)S(1)} %copy-done.2, bf16[384,768]{1,0:T(8,128)(2,1)S(1)} %copy-done.1, ...), custom_call_target="tpu_custom_call" | custom-call | tf_op jit(solution)/shard_map/publish/pallas_call | solution.py:1333
  774.6 2.2 copy-done
  776.9 0.8 copy-done.5
  777.7 0.7 copy-done.18
  778.4 0.7 fusion.31
  779.2 0.7 fusion.28
  779.8 1.8 select_bitcast_fusion.1
  781.6 1.8 copy.51
  783.4 7.0 fusion
  790.5 10.7 %copy.53 = f32[1,384,6448]{1,2,0:T(8,128)} copy(f32[1,384,6448]{2,1,0:T(8,128)} %fusion) | data formatting | bytes 19808256
  801.7 2.8 bitcast_convert_fusion
  804.7 1.2 copy-done.11
  806.0 2.1 fusion.1
  808.1 0.8 slice_bitcast_fusion
  811.0 0.9 slice.171
  (147 shorter events, 11.7 us)
Async XLA Ops:
  3.4 2.5 copy-start.17
  5.8 3.7 copy-start.24
  5.9 3.8 copy-start.25
  5.9 3.9 copy-start.26
  5.9 3.9 copy-start.27
  5.9 3.9 copy-start.28
  5.9 3.9 copy-start.29
  5.9 3.9 copy-start.30
  102.2 1.8 copy-start.10
  102.2 2.0 copy-start.15
  206.3 187.0 %copy-start.22 = (f32[2,8,256]{2,1,0:T(8,128)}, f32[2,8,256]{2,1,0:T(8,128)S(1)}, u32[]{:S(2)}) copy-start(f32[2,8,256]{2,1,0:T(8,128)S(1)} %add_rsqrt_fusion.1.r_ref) | copy-start | bytes 49156
  208.2 1.4 copy-start.14
  289.2 2.3 copy-start.8
  290.1 1.7 copy-start.23
  291.6 1.0 copy-start.6
  388.2 2.1 copy-start.7
  388.2 2.1 copy-start.13
  493.3 2.1 copy-start.9
  493.3 2.1 copy-start.16
  495.4 2.7 copy-start.20
  495.4 2.7 copy-start.21
  583.9 84.8 %copy-start.19 = (bf16[64,384]{1,0:T(8,128)(2,1)S(1)}, bf16[64,384]{1,0:T(8,128)(2,1)}, u32[]{:S(2)}) copy-start(bf16[64,384]{1,0:T(8,128)(2,1)} %get-tuple-element.95) | copy-start | bytes 147460
  669.6 1.1 copy-start.1
  670.6 1.1 copy-start.2
  671.7 1.0 copy-start.3
  672.7 1.0 copy-start.4
  774.6 2.2 copy-start
  776.8 0.9 copy-start.5
  777.7 0.7 copy-start.18
  801.7 3.0 copy-start.12
  804.6 1.4 copy-start.11

commit v5 on v3

--- a/solution.py
+++ b/solution.py
@@ -55,8 +55,8 @@
     return dot(jnp.concatenate(split3(v), 1), spread3, 1, 0)
 
 
-def per_head(v, gather3):
-    return dot(jnp.concatenate(split3(v), 1), gather3, 1, 0)
+def per_head(v, gather2):
+    return dot(jnp.concatenate(split3(v)[:2], 1), gather2, 1, 0)
 
 
 def fading(cum, cum_t, dt_t, h, inside):
@@ -256,7 +256,7 @@
 
     def copy(self, mask):
         return pltpu.make_async_remote_copy(
-            src_ref=self.source, dst_ref=self.target(mask), send_sem=self.send.at[mask],
+            src_ref=self.source(mask), dst_ref=self.target(mask), send_sem=self.send.at[mask],
             recv_sem=self.recv.at[mask], device_id=self.plane.device(mask), device_id_type=MESH,
         )
 
@@ -389,7 +389,7 @@
         for m in range(layers)
     ]
     shares = [
-        Share(plane, ss_mine.at[m], lambda mask, m=m: ss_in.at[m, mask], ss_send.at[m], ss_recv.at[m])
+        Share(plane, lambda mask, m=m: ss_mine.at[m], lambda mask, m=m: ss_in.at[m, mask], ss_send.at[m], ss_recv.at[m])
         for m in range(layers)
     ]
 
@@ -545,13 +545,21 @@
 
 
 def backward_kernel(
-    layers, heads, blocks, taps,
-    own_ref, pull_own, r_ref, pgx_ref, ps_ref, hgx_ref, hs_ref, res_ref, ent_ref,
-    wgx_ref, ws_ref, wo_ref, vec_ref, tri_ref, spread_ref, gather_ref,
-    raw_ref, gpgx_ref, gps_ref, no_ref, small_ref, full_out_ref,
-    full_ref, part_ref, pad_ref, next_ref, ge_ref, within_ref, gxm_ref, pull_ref, core_in, stage_in,
-    out_sem, ag_send, ag_recv, core_send, core_recv, rs_send, rs_recv, ss_send, ss_recv,
+    layers, heads, blocks, taps, behind, *refs
 ):
+    own_ref, pull_own, r_ref, pgx_ref, ps_ref, hgx_ref, hs_ref, res_ref, ent_ref = refs[:9]
+    wgx_ref, ws_ref, wo_ref, vec_ref, tri_ref, spread_ref, gather_ref = refs[9:16]
+    refs = refs[16:]
+    if behind:
+        late_gx, late_o = refs[:2]
+        refs = refs[2:]
+    raw_ref, gpgx_ref, gps_ref, no_ref, small_ref, full_out_ref = refs[:6]
+    refs = refs[6:]
+    if behind:
+        met_gx, home_o = refs[:2]
+        refs = refs[2:]
+    full_ref, part_ref, pad_ref, next_ref, ge_ref, within_ref, gxm_ref, pull_ref, core_in, stage_in = refs[:10]
+    out_sem, ag_send, ag_recv, core_send, core_recv, rs_send, rs_recv, ss_send, ss_recv = refs[10:19]
     cw = heads * HEAD
     t = pl.program_id(0)
     steps = layers * blocks
@@ -575,11 +583,39 @@
     def pull_place(sec, seq):
         return pull_ref.at[:, seq, :, pl.ds(pl.multiple_of(sec * piece, piece), piece)]
 
-    share = Share(plane, pull_own, lambda mask: pull_place(plane.sec, plane.seq), ss_send, ss_recv)
+    share = Share(plane, lambda mask: pull_own, lambda mask: pull_place(plane.sec, plane.seq), ss_send, ss_recv)
 
     def saving(m):
         rows = pl.ds(m * length, length)
         return pltpu.make_async_copy(full_ref.at[rows, :], full_out_ref.at[rows, :], out_sem.at[m])
+
+    if behind:
+        own_sem, row_send, row_recv, o_send, o_recv, h_send, h_recv, met_o, sum_o = refs[19:]
+        spot, count = lax.axis_index("fsdp"), lax.axis_size("fsdp")
+
+        def shard(j):
+            return late_gx.at[j]
+
+        row = Row(
+            spot, count, lambda d: shard(lax.rem(spot + d, count)), lambda d: met_gx.at[spot], row_send, row_recv
+        )
+        orow = Row(
+            spot, count, lambda d: late_o.at[lax.rem(spot + d, count)], lambda d: met_o.at[spot], o_send, o_recv
+        )
+        own_gx = pltpu.make_async_copy(shard(spot), met_gx.at[spot], own_sem.at[0])
+        own_o = pltpu.make_async_copy(late_o.at[spot], met_o.at[spot], own_sem.at[1])
+        home = (plane.sec * blocks + plane.seq) // (steps // count)
+        to_home = pltpu.make_async_remote_copy(
+            src_ref=sum_o, dst_ref=home_o.at[spot], send_sem=h_send.at[0], recv_sem=h_recv.at[spot],
+            device_id={"fsdp": home}, device_id_type=MESH,
+        )
+        at_home = pltpu.make_async_copy(sum_o, home_o.at[spot], h_send.at[0])
+
+        @pl.when(t == 0)
+        def _():
+            chain_barrier(plane, spot, count)
+            own_gx.start()
+            own_o.start()
 
     @pl.when(t == 0)
     def _():
@@ -589,9 +625,13 @@
             full_ref[pl.ds(rows, piece), :] = own_ref[m * piece : (m + 1) * piece, :]
         for m in range(layers):
             pull_ref[m, plane.seq, :, pl.ds(pl.multiple_of(plane.sec * piece, piece), piece)] = pull_own[m]
-        plane.barrier()
+        if not behind:
+            plane.barrier()
         share.begin()
         gathers[0].begin()
+        if behind:
+            orow.begin()
+            row.begin()
         gathers[0].hop(0)
         gathers[1].begin()
         for stage in range(1, plane.stages):
@@ -674,21 +714,26 @@
     grad_x = vec_ref[8:9, :cw] * gr_f + pulled + gxm
 
     gather = gather_ref[...]
-    tall = jnp.concatenate([gr_f * (within_ref[...] + growth_e * reach), xs_f * gxm, xs_f * pulled], 0)
-    sums = per_head(tall, gather)
-    s1, s2, s3 = sums[:SPAN], sums[SPAN : 2 * SPAN], sums[2 * SPAN :]
+    last = xs_f * pulled
+    sums = per_head(jnp.concatenate([gr_f * (within_ref[...] + growth_e * reach), xs_f * gxm + last], 0), gather)
+    s1, s2 = sums[:SPAN], sums[SPAN:]
     thin = jnp.concatenate(
-        [jnp.sum(gr_f * xs_f, axis=0, keepdims=True), grad_fade, jnp.zeros((6, cw), F32)], 0
+        [
+            jnp.sum(gr_f * xs_f, axis=0, keepdims=True),
+            grad_fade + jnp.sum(last, axis=0, keepdims=True),
+            jnp.zeros((6, cw), F32),
+        ],
+        0,
     )
     thin = per_head(thin, gather)
-    hi, mid, low = split3(s1 - s2 - s3)
+    hi, mid, low = split3(s1 - s2)
     packed = dot(tri, jnp.concatenate([hi, mid, low], 1), 0, 0)
     grad_rate = packed[:, :STATE] + packed[:, STATE : 2 * STATE] + packed[:, 2 * STATE :]
-    grad_rate = grad_rate + (jnp.sum(s3, axis=0, keepdims=True) + thin[1:2, :])
+    grad_rate = grad_rate + thin[1:2, :]
     denominator = 1.0 + e
     slope_x = jnp.where(x >= 0, 1.0, e) / denominator
     ratio = jnp.where(x < -20.0, 1.0, slope_x / jnp.maximum(dt, 1e-12))
-    grad_raw = (s2 + s3) * ratio - decay * grad_rate * slope_x
+    grad_raw = s2 * ratio - decay * grad_rate * slope_x
     small_ref[6:7, :STATE] += jnp.sum(grad_raw, axis=0, keepdims=True)
     small_ref[7:8, :STATE] += jnp.sum(grad_rate * rate, axis=0, keepdims=True)
     small_ref[8:9, :STATE] += thin[0:1, :]
@@ -721,6 +766,24 @@
         def _(stage=stage):
             gathers[1].hop(stage)
 
+    if behind:
+        @pl.when(t == steps - 3)
+        def _():
+            own_o.wait()
+            orow.finish()
+            total = met_o[0].astype(F32)
+            for j in range(1, count):
+                total = total + met_o[j].astype(F32)
+            sum_o[...] = total.astype(BF16)
+
+            @pl.when(spot == home)
+            def _():
+                at_home.start()
+
+            @pl.when(spot != home)
+            def _():
+                to_home.start()
+
     @pl.when(t == blocks)
     def _():
         for c in range(blocks):
@@ -753,6 +816,25 @@
             if stage + 1 < plane.stages:
                 collects[1].begin(stage + 1)
         collects[1].drain()
+        if behind:
+            own_gx.wait()
+            row.finish()
+            row.drain()
+            orow.drain()
+
+            @pl.when(spot == home)
+            def _():
+                at_home.wait()
+                for d in range(1, count):
+                    other = lax.rem(spot + d, count)
+                    pltpu.make_async_remote_copy(
+                        src_ref=sum_o, dst_ref=home_o.at[other], send_sem=h_send.at[0], recv_sem=h_recv.at[other],
+                        device_id={"fsdp": home}, device_id_type=MESH,
+                    ).wait_recv()
+
+            @pl.when(spot != home)
+            def _():
+                to_home.wait_send()
 
 
 def tables(heads):
@@ -760,7 +842,7 @@
     tri = np.tril(np.ones((SPAN, SPAN), np.float32))
     one = (np.arange(cw)[None, :] // HEAD == np.arange(STATE)[:, None]).astype(np.float32)
     spread3 = np.concatenate([one] * 3, 0)
-    gather3 = np.concatenate([one.T] * 3, 0)
+    gather3 = np.concatenate([one.T] * 2, 0)
     return jnp.asarray(tri, BF16), jnp.asarray(spread3, BF16), jnp.asarray(gather3, BF16)
 
 
@@ -844,8 +926,8 @@
     )(own, wgx, ws, wo, vec, tri, spread3, *following)
 
 
-def layer_backward(own, pull, r_rows, pgx, ps, res, ent, wgx, ws, wo, vec, taps, number):
-    layers, blocks = lax.axis_size("section"), lax.axis_size("seq")
+def layer_backward(own, pull, r_rows, pgx, ps, res, ent, wgx, ws, wo, vec, taps, number, *late):
+    layers, blocks, depth = lax.axis_size("section"), lax.axis_size("seq"), lax.axis_size("fsdp")
     width = own.shape[1]
     cw = wo.shape[0]
     heads = cw // HEAD
@@ -862,7 +944,7 @@
     rows = lambda w: pl.BlockSpec((SPAN, w), lambda t: (at(t), 0))
     edge = lambda w: pl.BlockSpec((16, w), lambda t: (jnp.maximum(at(t) * (SPAN // 16) - 1, 0), 0))
     return pl.pallas_call(
-        functools.partial(backward_kernel, layers, heads, blocks, taps),
+        functools.partial(backward_kernel, layers, heads, blocks, taps, bool(late)),
         grid=(steps,),
         in_specs=[
             vmem,
@@ -875,7 +957,8 @@
             rows(cw),
             pl.BlockSpec((1, STATE, cw), lambda t: (at(t), 0, 0)),
         ]
-        + [vmem] * 7,
+        + [vmem] * 7
+        + [pl.BlockSpec(memory_space=pl.ANY)] * len(late),
         out_specs=[
             vmem,
             rows(2 * cw),
@@ -883,7 +966,8 @@
             rows(cw),
             vmem,
             pl.BlockSpec(memory_space=pl.ANY),
-        ],
+        ]
+        + [pl.BlockSpec(memory_space=pl.ANY)] * len(late),
         out_shape=[
             jax.ShapeDtypeStruct(own.shape, F32),
             jax.ShapeDtypeStruct((tokens, 2 * cw), BF16),
@@ -891,7 +975,15 @@
             jax.ShapeDtypeStruct((tokens, cw), BF16),
             jax.ShapeDtypeStruct((16, chans), F32),
             jax.ShapeDtypeStruct((tokens, width), BF16),
-        ],
+        ]
+        + (
+            [
+                jax.ShapeDtypeStruct(late[0].shape, BF16),
+                jax.ShapeDtypeStruct(late[1].shape, BF16),
+            ]
+            if late
+            else []
+        ),
         scratch_shapes=[
             pltpu.VMEM((tokens, width), BF16),
             pltpu.VMEM((tokens, width), BF16),
@@ -903,7 +995,13 @@
             pltpu.VMEM((layers, blocks, 8, SPAN), F32),
         ]
         + plane_scratch(layers, blocks, width)
-        + [dma((steps,)), dma((steps,))],
+        + [dma((steps,)), dma((steps,))]
+        + (
+            [dma((2,))] + [dma((depth,))] * 4 + [dma((1,)), dma((depth,))]
+            + [pltpu.VMEM(late[1].shape, BF16), pltpu.VMEM(late[1].shape[1:], BF16)]
+            if late
+            else []
+        ),
         compiler_params=pltpu.CompilerParams(
             vmem_limit_bytes=60 << 20, collective_id=number, has_side_effects=True
         ),
@@ -913,166 +1011,495 @@
             transcendentals=tokens * SPAN * heads,
         ),
         name="layer_backward",
-    )(own, pull, r_rows, pgx, ps, pgx, ps, res, ent, wgx, ws, wo, vec, tri, spread3, gather3)
-
-
-def line_barrier(place, count, axis):
-    sem = pltpu.get_barrier_semaphore()
-
-    @pl.when(place > 0)
-    def _():
-        pl.semaphore_signal(sem, inc=1, device_id={axis: place - 1}, device_id_type=MESH)
-
-    @pl.when(place < count - 1)
-    def _():
-        pl.semaphore_signal(sem, inc=1, device_id={axis: place + 1}, device_id_type=MESH)
-
-    inner = (place > 0) & (place < count - 1)
-
-    @pl.when(inner)
-    def _():
-        pl.semaphore_wait(sem, 2)
-
-    @pl.when(~inner)
-    def _():
-        pl.semaphore_wait(sem, 1)
-
-
-def reduce_kernel(
-    count, ranks, parts, axis,
-    full_ref, gp_ref, no_ref, gb_ref, out_ref, oout_ref,
-    sum_ref, osum_ref, in_ref, oin_ref,
-    send_sem, recv_sem, osend_sem, orecv_sem,
+    )(own, pull, r_rows, pgx, ps, pgx, ps, res, ent, wgx, ws, wo, vec, tri, spread3, gather3, *late)
+
+
+class Publish:
+    def __init__(self, plane, cells, view, own, other, condition, send, recv):
+        self.plane, self.cells, self.view, self.own, self.other = plane, cells, view, own, other
+        self.condition = condition
+        self.send, self.recv = send, recv
+        self.outer = [dim for dim in range(2, plane.stages + 1)]
+
+    def number(self, mask):
+        sec, seq = self.plane.owner(mask)
+        return sec * self.plane.ranks + seq
+
+    def copy(self, mask, dim, cell):
+        dst = self.view(self.number(mask), cell)
+        src = self.other(cell) if dim == 1 else self.own(cell) if mask == 0 else dst
+        key = mask ^ (1 << dim)
+        return pltpu.make_async_remote_copy(
+            src_ref=src, dst_ref=dst, send_sem=self.send.at[key, cell], recv_sem=self.recv.at[key, cell],
+            device_id=self.plane.partner(dim), device_id_type=MESH,
+        )
+
+    def when(self, mask, act):
+        pl.when(self.condition(self.number(mask)))(act)
+
+    def stage(self, mask):
+        return max([i for i, dim in enumerate(self.outer) if mask >> dim & 1], default=-1)
+
+    def across(self, cell):
+        self.when(0, lambda: self.copy(0, 1, cell).start())
+
+    def forward(self, mask, cell):
+        def act():
+            for dim in self.outer[self.stage(mask) + 1 :] + [0]:
+                self.copy(mask, dim, cell).start()
+
+        self.when(mask, act)
+
+    def arrived(self, mask, cell):
+        def act():
+            view = self.view(self.number(mask), cell)
+            pltpu.make_async_remote_copy(
+                src_ref=view, dst_ref=view, send_sem=self.send.at[mask, cell], recv_sem=self.recv.at[mask, cell],
+                device_id=self.plane.partner(0), device_id_type=MESH,
+            ).wait_recv()
+
+        self.when(mask, act)
+
+    def step(self, mask, cell):
+        self.arrived(mask, cell)
+        self.forward(mask, cell)
+
+    def finish(self):
+        for mask in self.plane.masks:
+            for cell in range(self.cells):
+                self.arrived(mask + 1, cell)
+
+    def drain(self):
+        for mask in self.plane.masks:
+            dims = self.outer[self.stage(mask) + 1 :] + [0] + ([1] if mask == 0 else [])
+
+            def act(mask=mask, dims=dims):
+                for cell in range(self.cells):
+                    for dim in dims:
+                        self.copy(mask, dim, cell).wait_send()
+
+            self.when(mask, act)
+
+
+def finish_kernel(
+    layers, ranks, parts, oparts, tr, thin_rows,
+    full_ref, gp_ref, gps_ref, no_ref, gb_ref, late_ref, met_ref, home_ref, sm_ref, gn_ref, swap_ref,
+    gall, oall, sm_all, gn_out, got_ref,
+    sum_ref, osum_ref, in_ref, oin_ref, late_gx, done_gx, thin_ref, thin_f, tz_ref, tin_ref, core_in, stage_in, tall,
+    sm_in, sm_sum, gn_in, gn_plane,
+    send_sem, recv_sem, osend_sem, orecv_sem, core_send, core_recv, rs_send, rs_recv, tz_send, tz_recv,
+    g_send, g_recv, p_send, p_recv, t_send, t_recv, s_send, s_recv, n_send, n_recv, zs_send, zs_recv, zn_send, zn_recv,
+    swap_send, swap_recv, own_sem,
 ):
-    place = lax.axis_index(axis)
-    rows = out_ref.shape[0]
-    piece = rows // parts
-    orows = oout_ref.shape[0]
-    opiece = orows // parts
-    here = lax.axis_index("section") * ranks + lax.axis_index("seq")
-    source = (here * orows) // (ranks * lax.axis_size("section") * orows // count)
-    line_barrier(place, count, axis)
+    place, count = lax.axis_index("fsdp"), lax.axis_size("fsdp")
+    plane = Plane(layers, ranks)
+    here = plane.sec * ranks + plane.seq
+    per = plane.size // count
+    home = here // per
+    cols, rows = late_gx.shape
+    cw = cols // 2
+    piece = cols // parts
+    opiece = osum_ref.shape[1]
+    chain_barrier(plane, place, count)
+
+    swap = pltpu.make_async_remote_copy(
+        src_ref=swap_ref, dst_ref=got_ref, send_sem=swap_send.at[0], recv_sem=swap_recv.at[0],
+        device_id=plane.partner(1), device_id_type=MESH,
+    )
+    sm_lines = Row(place, count, lambda d: sm_ref, lambda d: sm_in.at[d], zs_send, zs_recv)
+    gn_lines = Row(place, count, lambda d: gn_ref, lambda d: gn_in.at[d], zn_send, zn_recv)
+    sm_lines.begin()
+    gn_lines.begin()
+    shares = [
+        Share(plane, lambda mask: sm_sum.at[plane.owner(mask)[0]], lambda mask: sm_all.at[here], s_send, s_recv),
+        Share(plane, lambda mask: gn_plane.at[0], lambda mask: gn_plane.at[mask], n_send, n_recv),
+    ]
+
+    def gx_window(d, cell):
+        half, rest = cell // (parts // 2), cell % (parts // 2)
+        at = half * (cw * plane.size) + d * cw + rest * piece
+        return gall.at[pl.ds(pl.multiple_of(at, 16), piece), :]
+
+    def gx_source(ref):
+        return lambda cell: ref.at[pl.ds(cell * piece, piece), :]
+
+    def o_window(d, cell):
+        return oall.at[lax.rem(d, per), pl.ds(cell * opiece, opiece), :]
+
+    def early_o(cell):
+        return home_ref.at[pl.ds(cell * opiece, opiece), :]
+
+    def new_o(cell):
+        return osum_ref.at[cell]
+
+    always, at_home = (lambda d: d >= 0), (lambda d: d // per == place)
+    early_gx, new_gx = gx_source(late_gx), gx_source(done_gx)
+    gpub = [
+        Publish(plane, parts, gx_window, new_gx, early_gx, always, g_send, g_recv),
+        Publish(plane, parts, gx_window, early_gx, new_gx, always, g_send, g_recv),
+    ]
+    opub = [
+        Publish(plane, oparts, o_window, new_o, early_o, at_home, p_send, p_recv),
+        Publish(plane, oparts, o_window, early_o, new_o, at_home, p_send, p_recv),
+    ]
+    locals_of = {}
+    base = 0
+    for name, pubs in (("gx", gpub), ("o", opub)):
+        for number in range(layers):
+            locals_of[name, number] = base
+        base += pubs[0].cells
+
+    def side(number):
+        return pltpu.make_async_copy(
+            tall.at[pl.ds(number * thin_rows, thin_rows), :],
+            gall.at[pl.ds(plane.size * cols, thin_rows), :], own_sem.at[parts + oparts],
+        )
+
+    def store(pub, name, number, cell):
+        return pltpu.make_async_copy(pub.own(cell), pub.view(here, cell), own_sem.at[locals_of[name, number] + cell])
+
+    def release(layer, name, cells):
+        for number in range(layers):
+            pub = (gpub if name == "gx" else opub)[number]
+
+            @pl.when(plane.sec == number)
+            def _(number=number, pub=pub):
+                for cell in cells:
+                    if number == layer:
+                        pub.when(0, store(pub, name, number, cell).start)
+                        pub.forward(0, cell)
+                    else:
+                        pub.across(cell)
+
+    def flow(layer, name, mask, cells):
+        pub = (gpub if name == "gx" else opub)[layer]
+
+        @pl.when(plane.sec == layer)
+        def _():
+            for cell in cells:
+                pub.step(mask, cell)
+
+    upper = [m for m in plane.masks if m > 2]
+    upper = sorted(upper, key=lambda m: (gpub[0].stage(m), m & 2))
+    gcells, ocells = range(parts), range(oparts)
+
+    total = met_ref[0].astype(F32)
+    for j in range(1, count):
+        total = total + met_ref[j].astype(F32)
+    late_gx[...] = total.astype(BF16)
+    release(1, "gx", gcells)
+    release(1, "o", ocells)
+    swap.start()
+
+    first = dot(gps_ref[...], full_ref[...], 0, 0).astype(BF16)
+    thin_ref[pl.ds(0, thin_rows), :] = first[:thin_rows, :]
+    thin_ref[pl.ds(thin_rows, thin_rows), :] = late_ref[:thin_rows, :]
+    rest = thin_ref.shape[0] - layers * thin_rows
+    thin_ref[pl.ds(layers * thin_rows, rest), :] = jnp.zeros((rest, thin_ref.shape[1]), BF16)
+    thin = Collect(plane, thin_ref, 0, layers * tr, core_in, stage_in, core_send, core_recv, rs_send, rs_recv)
+    for c in range(ranks):
+        thin.block_done(c)
+    lines = Row(
+        place, count, lambda d: tz_ref.at[lax.rem(place + d, count)], lambda d: tin_ref.at[place], tz_send, tz_recv
+    )
+    spread = Spread(plane, tall, lambda sec, seq: (seq * layers + sec) * tr, tr, t_send, t_recv)
+
+    behind = (place > 0, place < count - 1)
 
     def hop(j, k, side):
-        to = place + 1 if side == 0 else place - 1
         return pltpu.make_async_remote_copy(
-            src_ref=sum_ref.at[j, k], dst_ref=in_ref.at[side, j, k],
-            send_sem=send_sem.at[j, k], recv_sem=recv_sem.at[side, j, k],
-            device_id={axis: to}, device_id_type=MESH,
+            src_ref=sum_ref.at[j, k], dst_ref=in_ref.at[side, j, k], send_sem=send_sem.at[j, k],
+            recv_sem=recv_sem.at[side, j, k], device_id={"fsdp": place + 1 if side == 0 else place - 1},
+            device_id_type=MESH,
         )
 
     def ohop(k, side):
-        to = place + 1 if side == 0 else place - 1
         return pltpu.make_async_remote_copy(
-            src_ref=osum_ref.at[k], dst_ref=oin_ref.at[side, k],
-            send_sem=osend_sem.at[k], recv_sem=orecv_sem.at[side, k],
-            device_id={axis: to}, device_id_type=MESH,
+            src_ref=osum_ref.at[k], dst_ref=oin_ref.at[side, k], send_sem=osend_sem.at[k],
+            recv_sem=orecv_sem.at[side, k], device_id={"fsdp": place + 1 if side == 0 else place - 1},
+            device_id_type=MESH,
         )
 
-    ends = (place < count - 1, place > 0)
-    before = (place > 0, place < count - 1)
+    def absorb(j, k, side):
+        hop(j, k, side).wait_recv()
+        sum_ref[j, k] = (sum_ref[j, k].astype(F32) + in_ref[side, j, k].astype(F32)).astype(BF16)
+
+    def oabsorb(k, side):
+        ohop(k, side).wait_recv()
+        osum_ref[k] = (osum_ref[k].astype(F32) + oin_ref[side, k].astype(F32)).astype(BF16)
+
+    def oitem(k):
+        osum_ref[k] = dot(no_ref[:, k * opiece : (k + 1) * opiece], gb_ref[...], 0, 0).astype(BF16)
+        for side in (0, 1):
+            beyond = (place < home) if side == 0 else (place > home)
+
+            @pl.when(beyond & behind[side])
+            def _(side=side):
+                oabsorb(k, side)
+
+            @pl.when(beyond)
+            def _(side=side):
+                ohop(k, side).start()
 
     def work(j, k):
         sum_ref[j, k] = dot(
-            full_ref[:, j * rows + k * piece : j * rows + (k + 1) * piece], gp_ref[...], 0, 0
+            gp_ref[:, k * piece : (k + 1) * piece], full_ref[:, j * rows : (j + 1) * rows], 0, 0
         ).astype(BF16)
 
     def shift(j, k):
         for side in (0, 1):
             beyond = (place < j) if side == 0 else (place > j)
 
-            @pl.when(beyond & before[side])
+            @pl.when(beyond & behind[side])
             def _(side=side):
-                hop(j, k, side).wait_recv()
-                sum_ref[j, k] = (sum_ref[j, k].astype(F32) + in_ref[side, j, k].astype(F32)).astype(BF16)
+                absorb(j, k, side)
 
             @pl.when(beyond)
             def _(side=side):
                 hop(j, k, side).start()
 
-    order = []
-    low, high = 0, count - 1
-    while low <= high:
-        order += [high] if low == high else [high, low]
-        low, high = low + 1, high - 1
-    order = [(j, k) for pair in range(0, len(order), 2) for k in range(parts) for j in order[pair : pair + 2]]
-    for j, k in order:
-        work(j, k)
-        shift(j, k)
-    for k in range(parts):
-        osum_ref[k] = dot(no_ref[:, k * opiece : (k + 1) * opiece], gb_ref[...], 0, 0).astype(BF16)
+    def items(pair, k):
+        for j in pair:
+            work(j, k)
+
+        @pl.when(place < count // 2)
+        def _():
+            for j in pair:
+                shift(j, k)
+
+        @pl.when(place >= count // 2)
+        def _():
+            for j in pair[::-1]:
+                shift(j, k)
+
+    def final(k):
+        for j in range(count):
+            @pl.when(place == j)
+            def _(j=j):
+                for side in (0, 1):
+                    @pl.when(behind[side])
+                    def _(side=side):
+                        absorb(j, k, side)
+
+                done_gx[pl.ds(k * piece, piece), :] = sum_ref[j, k]
+
+        release(0, "gx", [k])
+
+    def ofinal(k):
         for side in (0, 1):
-            beyond = (place < source) if side == 0 else (place > source)
-
-            @pl.when(beyond & before[side])
-            def _(side=side, k=k):
-                ohop(k, side).wait_recv()
-                osum_ref[k] = (osum_ref[k].astype(F32) + oin_ref[side, k].astype(F32)).astype(BF16)
-
-            @pl.when(beyond)
-            def _(side=side, k=k):
-                ohop(k, side).start()
-
-    for k in range(parts):
+            @pl.when((place == home) & behind[side])
+            def _(side=side):
+                oabsorb(k, side)
+
+        release(0, "o", [k])
+
+    def small_sums():
+        sm_lines.finish()
+        gn_lines.finish()
+        mine, gain = sm_ref[...].astype(F32), gn_ref[...]
+        for d in range(1, count):
+            mine, gain = mine + sm_in[d].astype(F32), gain + gn_in[d]
+        sm_sum[...] = mine.astype(BF16)
+        sm_all[here] = sm_sum[plane.sec]
+        gn_plane[0] = gain
+        for share in shares:
+            share.begin()
+
+    def thin_stage(stage):
+        thin.add(stage, thin_f, 0)
+        if stage + 1 < plane.stages:
+            thin.begin(stage + 1)
+
+    def thin_across():
+        span = tz_ref.shape[2]
         for j in range(count):
-            for side in (0, 1):
-                @pl.when((place == j) & before[side])
-                def _(side=side, k=k, j=j):
-                    hop(j, k, side).wait_recv()
-                    sum_ref[j, k] = (sum_ref[j, k].astype(F32) + in_ref[side, j, k].astype(F32)).astype(BF16)
-
-            @pl.when(place == j)
-            def _(k=k, j=j):
-                out_ref[pl.ds(k * piece, piece), :] = sum_ref[j, k]
-
-    for k in range(parts):
-        for side in (0, 1):
-            @pl.when((place == source) & before[side])
-            def _(side=side, k=k):
-                ohop(k, side).wait_recv()
-                osum_ref[k] = (osum_ref[k].astype(F32) + oin_ref[side, k].astype(F32)).astype(BF16)
-
-        oout_ref[pl.ds(k * opiece, opiece), :] = osum_ref[k]
-
-        @pl.when(place != source)
+            tz_ref[j] = thin_f[:, j * span : (j + 1) * span].astype(BF16)
+        lines.begin()
+
+    def thin_back():
+        lines.finish()
+        value = tz_ref[place].astype(F32)
+        for d in range(1, count):
+            value = value + tin_ref[lax.rem(place + d, count)].astype(F32)
+        at = pl.multiple_of((plane.seq * layers + plane.sec) * tr, 16)
+        tall[pl.ds(at, tr), :] = value.astype(BF16)
+        spread.begin()
+
+    todo = [lambda: ([thin.block_add(c) for c in range(ranks)], thin.begin(0)), small_sums]
+    todo += [lambda stage=stage: thin_stage(stage) for stage in range(plane.stages)]
+    todo += [thin_across, thin_back]
+    todo += [lambda stage=stage: spread.hop(stage) for stage in range(plane.stages)]
+
+    def advance(n):
+        for _ in range(n):
+            if todo:
+                todo.pop(0)()
+
+    def part(k):
+        return [k]
+
+    pairs = [(count - 1 - i, i) for i in range(count // 2)]
+    done = {}
+
+    def onward(name, stage, upto):
+        begin = done.get((name, stage), 0)
+        cells = list(range(begin, max(begin, min(upto, parts if name == "gx" else oparts))))
+        if cells:
+            done[name, stage] = cells[-1] + 1
+            for mask in [2] if stage == 0 else upper:
+                flow(0, name, mask, cells)
+
+    rounds = max(parts, oparts, 3)
+    for k in range(rounds):
+        if k < oparts:
+            oitem(k)
+        if k == 1:
+            for mask in upper:
+                flow(1, "gx", mask, gcells)
+        if 1 <= k <= oparts:
+            ofinal(k - 1)
+        advance(1)
+        for number, pair in enumerate(pairs):
+            if k < parts:
+                items(pair, k)
+            advance(1)
+            if number == 0:
+                onward("gx", 0, k - 1)
+                onward("o", 0, k - 1)
+        onward("gx", 1, k - 1)
+        onward("o", 1, k - 2)
+        if k == 0:
+            flow(1, "gx", 2, gcells)
+        if k == 1:
+            flow(1, "o", 2, ocells)
+        if k == 2:
+            for mask in upper:
+                flow(1, "o", mask, ocells)
+        if 1 <= k <= parts:
+            final(k - 1)
+    if rounds == oparts:
+        ofinal(oparts - 1)
+    advance(len(todo))
+    if rounds == parts:
+        onward("gx", 0, parts - 1)
+        onward("gx", 1, parts - 1)
+        final(parts - 1)
+    onward("o", 0, oparts)
+    onward("o", 1, oparts - 1)
+    onward("gx", 0, parts)
+    onward("gx", 1, parts)
+    onward("o", 1, oparts)
+
+    spread.finish()
+    for number in range(layers):
+        @pl.when(plane.sec == number)
+        def _(number=number):
+            side(number).start()
+            for name, pubs in (("gx", gpub), ("o", opub)):
+                for cell in range(pubs[number].cells):
+                    pubs[number].when(0, store(pubs[number], name, number, cell).wait)
+            side(number).wait()
+    for share in shares:
+        share.finish()
+    value = gn_plane[0]
+    for mask in range(1, plane.size):
+        value = value + gn_plane[mask]
+    gn_out[...] = value
+    gpub[0].finish()
+    opub[0].finish()
+    swap.wait()
+    for each in [gpub[0], opub[0], spread, lines, thin, sm_lines, gn_lines] + shares:
+        each.drain()
+    for k in range(oparts):
+        @pl.when(place != home)
         def _(k=k):
             ohop(k, 0).wait_send()
 
+    for k in range(parts):
         for j in range(count):
             @pl.when(place != j)
             def _(k=k, j=j):
                 hop(j, k, 0).wait_send()
 
 
-def reduce_gradients(full, gp, no, gb, number):
-    count, ranks = lax.axis_size("fsdp"), lax.axis_size("seq")
+def finish(full, gp, gps, no, gb, late, met, home, sm, gn, swap, number):
+    layers, ranks, count = lax.axis_size("section"), lax.axis_size("seq"), lax.axis_size("fsdp")
+    size = layers * ranks
     tokens, width = full.shape
-    rows, cols, orows = width // count, gp.shape[1], no.shape[1]
-    parts = 3 if rows % 384 == 0 and orows % 384 == 0 else 1
+    rows, cols, cw = width // count, gp.shape[1], no.shape[1]
+    parts = 4 if cw % 384 == 0 else 2
+    oparts = cw // STATE if cw % STATE == 0 else 1
+    thin_rows = 2 * STATE + size * cw // HEAD
+    tr = -(-layers * thin_rows // (32 * size)) * 32
+    piece, opiece = cols // parts, cw // oparts
+    dma = pltpu.SemaphoreType.DMA
+    anywhere, vmem = pl.BlockSpec(memory_space=pl.ANY), pl.BlockSpec(memory_space=pltpu.VMEM)
     return pl.pallas_call(
-        functools.partial(reduce_kernel, count, ranks, parts, "fsdp"),
-        in_specs=[whole(a) for a in (full, gp, no, gb)],
-        out_specs=[pl.BlockSpec(memory_space=pltpu.VMEM)] * 2,
-        out_shape=[jax.ShapeDtypeStruct((rows, cols), BF16), jax.ShapeDtypeStruct((orows, width), BF16)],
+        functools.partial(finish_kernel, layers, ranks, parts, oparts, tr, thin_rows),
+        in_specs=[vmem] * 7 + [anywhere, vmem, vmem, anywhere],
+        out_specs=[anywhere, anywhere, vmem, vmem, anywhere],
+        out_shape=[
+            jax.ShapeDtypeStruct((size * cols + thin_rows, rows), BF16),
+            jax.ShapeDtypeStruct((size // count, cw, width), BF16),
+            jax.ShapeDtypeStruct((size,) + sm.shape[1:], BF16),
+            jax.ShapeDtypeStruct(gn.shape, F32),
+            jax.ShapeDtypeStruct(swap.shape, BF16),
+        ],
         scratch_shapes=[
-            pltpu.VMEM((count, parts, rows // parts, cols), BF16),
-            pltpu.VMEM((parts, orows // parts, width), BF16),
-            pltpu.VMEM((2, count, parts, rows // parts, cols), BF16),
-            pltpu.VMEM((2, parts, orows // parts, width), BF16),
-            pltpu.SemaphoreType.DMA((count, parts)),
-            pltpu.SemaphoreType.DMA((2, count, parts)),
-            pltpu.SemaphoreType.DMA((parts,)),
-            pltpu.SemaphoreType.DMA((2, parts)),
+            pltpu.VMEM((count, parts, piece, rows), BF16),
+            pltpu.VMEM((oparts, opiece, width), BF16),
+            pltpu.VMEM((2, count, parts, piece, rows), BF16),
+            pltpu.VMEM((2, oparts, opiece, width), BF16),
+            pltpu.VMEM((cols, rows), BF16),
+            pltpu.VMEM((cols, rows), BF16),
+            pltpu.VMEM((size * tr, width), BF16),
+            pltpu.VMEM((tr, width), F32),
+            pltpu.VMEM((count, tr, rows), BF16),
+            pltpu.VMEM((count, tr, rows), BF16),
+            pltpu.VMEM((ranks // 2, layers * tr, width), BF16),
+            pltpu.VMEM((2, size // 2, tr // 2, width), BF16),
+            pltpu.VMEM((size * tr, rows), BF16),
+            pltpu.VMEM((count,) + sm.shape, BF16),
+            pltpu.VMEM(sm.shape, BF16),
+            pltpu.VMEM((count,) + gn.shape, F32),
+            pltpu.VMEM((size,) + gn.shape, F32),
+            dma((count, parts)),
+            dma((2, count, parts)),
+            dma((oparts,)),
+            dma((2, oparts)),
+            dma((ranks,)),
+            dma((ranks,)),
+            dma((2, size // 2)),
+            dma((2, size // 2)),
+            dma((count,)),
+            dma((count,)),
+            dma((size, parts)),
+            dma((size, parts)),
+            dma((size, oparts)),
+            dma((size, oparts)),
+            dma((2, size)),
+            dma((2, size)),
+            dma((size,)),
+            dma((size,)),
+            dma((size,)),
+            dma((size,)),
+            dma((count,)),
+            dma((count,)),
+            dma((count,)),
+            dma((count,)),
+            dma((1,)),
+            dma((1,)),
+            dma((parts + oparts + 1,)),
         ],
         compiler_params=pltpu.CompilerParams(
-            collective_id=number, has_side_effects=True, vmem_limit_bytes=56 << 20
+            collective_id=number, has_side_effects=True, vmem_limit_bytes=60 << 20
         ),
         cost_estimate=pl.CostEstimate(
-            flops=2 * tokens * (width * cols + orows * width), bytes_accessed=2 * tokens * (2 * width + cols + orows),
-            transcendentals=0,
+            flops=2 * tokens * width * (cols + cw + gps.shape[1]),
+            bytes_accessed=2 * tokens * (2 * width + cols + cw), transcendentals=0,
         ),
-        name="reduce_gradients",
-    )(full, gp, no, gb)
+        name="finish",
+    )(full, gp, gps, no, gb, late, met, home, sm, gn, swap)
 
 
 def start_kernel(
@@ -1418,19 +1845,25 @@
             hidden = hidden.astype(BF16).astype(F32)
     output = hidden
 
-    grad = cot
-    big, small = [None] * layers, [None] * layers
+    grad, late = cot, ()
+    small = [None] * layers
     for layer in reversed(range(layers)):
         wgx, ws, wo = weights[layer]
         before, rs, full, pgx, ps, res, ent, raw, r, r_rows = saved[layer]
         low = grad.astype(BF16)
         pull = r * r * r * jnp.sum(low.astype(F32) * raw, axis=-1, keepdims=True) / inner
         pull = jnp.broadcast_to(pull.reshape(layers, 1, piece), (layers, 8, piece))
-        gn, gpgx, gps, no, tiny, gb = layer_backward(
-            low, pull, r_rows, pgx, ps, res, ent, wgx, ws, wo, vecs[layer], taps, 3 * layers + layer
+        gn, gpgx, gps, no, tiny, gb, *met = layer_backward(
+            low, pull, r_rows, pgx, ps, res, ent, wgx, ws, wo, vecs[layer], taps, 3 * layers + layer, *late
         )
-        g_gx, g_o = reduce_gradients(full, gpgx, no, gb, layers + layer)
-        g_s = dot(full, gps, 0, 0).astype(BF16)
+        if layer > 0:
+            late = (
+                jnp.stack([dot(gpgx, v, 0, 0).astype(BF16) for v in jnp.split(full, depth, 1)]),
+                dot(no, gb, 0, 0).astype(BF16).reshape(depth, -1, width),
+            )
+            late_thin = dot(gps, full, 0, 0).astype(BF16)
+        else:
+            last = (full, gpgx, gps, no, gb, late_thin, met[0], met[1].reshape(cw, width))
         unit = before * rs
         g_gain = jnp.sum(gn * unit, axis=0)
         gn = gn * gains[layer]
@@ -1438,56 +1871,30 @@
         if layer > 0:
             grad = grad.astype(BF16).astype(F32)
 
-        def placed(v, count, begin):
-            return lax.dynamic_update_slice(jnp.zeros((count,), F32), v, (begin,))
-
-        conv = lax.dynamic_update_slice(jnp.zeros((taps + 1, chans), F32), tiny[: taps + 1, :cw], (0, here * cw))
-        conv = conv + jnp.pad(tiny[: taps + 1, cw:], ((0, 0), (inner, 0)))
-        small[layer] = jnp.concatenate(
-            [g_gain, conv.reshape(-1), placed(tiny[5, :cw], inner, here * cw)]
-            + [placed(tiny[n, :heads], heads_all, here * heads) for n in (6, 7, 8)]
-        )
-        g_s = g_s[:, : shared + heads_all]
-        g_s = lax.psum_scatter(g_s, "fsdp", scatter_dimension=0, tiled=True)
-        big[layer] = (g_gx, g_s, g_o)
+        by_head = lax.dynamic_update_slice(jnp.zeros((3, STATE), F32), tiny[6:9, :heads], (0, here * heads))
+        small[layer] = (tiny, jnp.concatenate([g_gain, by_head.reshape(-1)]))
 
     output = output.reshape(layers, piece, width)
     grad = grad.reshape(layers, piece, width)
-    got = swapped(jnp.where(low_layer, output, grad).astype(BF16), "section").astype(F32)
+    g_norm = jnp.concatenate([s[1] for s in small])
+    lasting = g_norm.size // layers
+    g_norm = jnp.pad(g_norm, (0, -g_norm.size % (8 * STATE))).reshape(8, -1)
+    gall, oall, sm, g_norm, got = finish(
+        *last, jnp.stack([s[0] for s in small]).astype(BF16), g_norm, jnp.where(low_layer, output, grad).astype(BF16), 4 * layers
+    )
+    got = got.astype(F32)
     results = jnp.where(low_layer, jnp.concatenate([grad, got], 1), jnp.concatenate([got, output], 1))
     section_results = results[None, :, None]
-
-    def own_layer(values):
-        own = jnp.where(low_layer, values[0], values[1])
-        other = jnp.where(low_layer, values[1], values[0])
-        return own, other
-
-    own, other = own_layer([b[0] for b in big])
-    other = swapped(other, "section")
-    pair = jnp.stack([jnp.where(low_layer, own, other), jnp.where(low_layer, other, own)])
-    gx = lax.all_gather(pair, "seq")
-    rows = gx.shape[2]
-    gx = gx.reshape(ranks, layers, rows, 2, cw)
-    gx = jnp.transpose(gx, (2, 3, 1, 0, 4)).reshape(rows, 2 * inner)
-    s_all = lax.psum(jnp.stack([b[1] for b in big]), PLANE)
-    s_own, _ = own_layer([s_all[0], s_all[1]])
-    grad_in = jnp.concatenate([gx.astype(F32), s_own.astype(F32)], 1)[None]
-
-    own, other = own_layer([b[2] for b in big])
-    other = swapped(other, "section")
-    pair = jnp.stack([jnp.where(low_layer, own, other), jnp.where(low_layer, other, own)])
-    spread = jnp.zeros((out_rows, width), BF16)
-    for s in range(layers):
-        start = (s * ranks + seq) * cw - dep * out_rows
-        inside = (start >= 0) & (start < out_rows)
-        block = jnp.where(inside, pair[s], jnp.zeros_like(pair[s]))
-        spread = spread + lax.dynamic_update_slice(jnp.zeros_like(spread), block, (jnp.clip(start, 0, out_rows - cw), 0))
-    grad_out = lax.psum(spread, "seq").astype(F32)[None]
-
-    tiny = lax.psum(jnp.stack(small), EVERY)
-    tiny = jnp.where(low_layer, tiny[0], tiny[1])
-    cuts = np.cumsum([0, width, taps * chans, chans, inner, heads_all, heads_all, heads_all])
-    parts = [tiny[cuts[i] : cuts[i + 1]] for i in range(7)]
+    grad_in = gall.astype(F32).T[None]
+    grad_out = oall.reshape(out_rows, width).astype(F32)[None]
+
+    sm = sm.astype(F32)
+    conv = jnp.transpose(sm[:, : taps + 1, :cw], (1, 0, 2)).reshape(taps + 1, inner)
+    conv = jnp.concatenate([conv, jnp.sum(sm[:, : taps + 1, cw:], 0)], 1)
+    g_norm = g_norm.reshape(-1)
+    g_norm = jnp.where(low_layer, g_norm[:lasting], g_norm[lasting : 2 * lasting])
+    by_head = g_norm[width:].reshape(3, STATE)[:, :heads_all]
+    g_norm = g_norm[:width]
 
     def share(v):
         count = v.shape[-1] // depth
@@ -1495,14 +1902,14 @@
 
     return (
         section_results,
-        share(parts[0]),
+        share(g_norm),
         grad_in,
-        share(parts[1].reshape(taps, chans)),
-        share(parts[2]),
-        share(parts[4]),
-        share(parts[5]),
-        share(parts[6]),
-        share(parts[3]),
+        share(conv[:taps]),
+        share(conv[taps]),
+        share(by_head[0]),
+        share(by_head[1]),
+        share(by_head[2]),
+        share(sm[:, 5, :cw].reshape(-1)),
         grad_out,
     )
 

time: 1070 us -> 723 us (0.68)
  waiting for transfers between devices: 253 us -> 0 us
  local copies, waits for them, and re-layouts: 77.4 us -> 29.6 us
  other arithmetic: 51.2 us -> 35.6 us
  between operations: 16.6 us -> 1.5 us
  matrix products: 11.3 us -> 24.4 us
    psum x3 -> x0, waiting for transfers between devices: 178 us -> none  [the longest x1 72.9 us: per_device(): tiny = lax.psum(jnp.stack(small), EVERY)]
    all_gather x1 -> x0, waiting for transfers between devices: 34.9 us -> none  [per_device(): gx = lax.all_gather(pair, 'seq')]
    convert_element_type x2 -> x0, local copies, waits for them, and re-layouts: 22.5 us -> none  [per_device(): grad_in = jnp.concatenate([gx.astype(F32), s_own.astype(F32)], 1)[None]]
    unnamed x8 -> x0, waiting for transfers between devices: 20.2 us -> none
    ppermute x3 -> x0, waiting for transfers between devices: 19.8 us -> none  [swapped(): return lax.ppermute(value, axis, [(i, count - 1 - i) for i in range(count)])]
    dot_general x2 -> x6, matrix products: 11.3 us -> 24.4 us  [dot(): lax.dot_general(a, b, (((ca,), (cb,)), ((), ())), preferred_element_type=...]
    pallas_call x2 -> x1, Pallas kernels: 181 us -> 175 us  [finish(): pl.pallas_call(functools.partial(finish_kernel, layers, ranks, parts, opa...]
  transfers between devices with their start and end apart: 9 -> 0, of which waited for: 7 -> 0; matrix products, arithmetic and copies ran while one was open for 5% -> 0% of each run, Pallas kernels for 17% -> 0%
where the time goes in v5:
time: 723 us; the launch traced here: 719 us
  Pallas kernels  628 us (87%)
  other arithmetic  35.6 us (5%)
  local copies, waits for them, and re-layouts  29.6 us (4%)
  matrix products  24.4 us (3%)
    pallas_call x2, Pallas kernels, layer_backward(): pl.pallas_call(functools.partial(backward_kernel, layers, heads, blocks,...  190 us
    pallas_call x2, Pallas kernels, layer_forward(): pl.pallas_call(functools.partial(forward_kernel, layers, heads, blocks, t...  180 us
    pallas_call x1, Pallas kernels, finish(): pl.pallas_call(functools.partial(finish_kernel, layers, ranks, parts, opa...  175 us
    pallas_call x1, Pallas kernels, start_up(): pl.pallas_call(functools.partial(start_kernel, layers, ranks, parts, opar...  82.7 us
    dot_general x6, matrix products, dot(): lax.dot_general(a, b, (((ca,), (cb,)), ((), ())), preferred_element_type=...  24.4 us

profile of v5, /device:TPU:19, one launch (start us, length us, event | category | flops | bytes accessed | tf_op | source)
XLA Modules:
  0.0 718.7 jit_solution(3229125427273866511)
XLA Ops:
  0.7 2.1 constant_dynamic-slice_fusion.9
  3.4 1.3 copy.33
  4.7 1.1 pad_maximum_fusion.1
  5.9 2.0 constant_dynamic-slice_fusion.6
  7.8 1.0 constant_dynamic-slice_fusion.5
  8.9 0.7 pad.38.strip_ref
  9.9 0.6 pad_bitcast_fusion.packed_ref
  10.5 82.7 %start_up.1 = (bf16[1536,768]{1,0:T(8,128)(2,1)}, bf16[4,96,1536]{2,1,0:T(8,128)(2,1)}, bf16[384,768]{1,0:T(8,128)(2,1)}, bf16[96,1536]{1,0:T(8,128)(2,1)}, bf16...) custom-call(bf16[384,768]{1,0:T(8,128)(2,1)} %get-tuple-element.146.mine, ...), custom_call_target="tpu_custom_call" | custom-call | tf_op jit(solution)/shard_map/start_up/pallas_call | solution.py:1707
  93.2 1.0 reshape.288
  95.6 1.2 concatenate.69.refs_4_.refs_12_
  98.0 1.2 concatenate.66.refs_4_.refs_12_
  99.3 1.9 fusion.69
  101.2 1.2 copy.35
  102.4 0.7 copy-done.4
  103.4 0.7 fusion.74
  104.2 1.1 fusion.18.refs_0_
  105.3 101.1 %layer_forward.2 = (f32[256,1536]{1,0:T(8,128)}, f32[2,8,256]{2,1,0:T(8,128)}, bf16[2048,768]{1,0:T(8,128)(2,1)}, bf16[2048,384]{1,0:T(8,128)(2,1)}, bf16[2048,3...) custom-call(bf16[256,1536]{1,0:T(8,128)(2,1)} %fusion.18.refs_0_, ...), custom_call_target="tpu_custom_call" | custom-call | flops 10764681216 | bytes 23592960 | tf_op jit(solution)/shard_map/layer_forward/pallas_call | solution.py:881
  206.4 0.7 add_rsqrt_fusion.1.refs_2_
  207.2 1.8 fusion.13
  209.0 1.1 fusion.8.refs_0_
  210.2 1.2 copy.37
  211.3 78.8 %layer_forward.3 = (f32[256,1536]{1,0:T(8,128)}, f32[2,8,256]{2,1,0:T(8,128)}, bf16[2048,768]{1,0:T(8,128)(2,1)}, bf16[2048,384]{1,0:T(8,128)(2,1)}, bf16[2048,3...) custom-call(bf16[256,1536]{1,0:T(8,128)(2,1)} %fusion.8.refs_0_, ...), custom_call_target="tpu_custom_call" | custom-call | flops 10764681216 | bytes 23592960 | tf_op jit(solution)/shard_map/layer_forward/pallas_call | solution.py:881
  290.2 0.8 add_rsqrt_fusion.refs_2_
  291.0 1.2 slice_select_fusion.1
  292.7 0.6 broadcast_in_dim.74.refs_1_
  293.3 90.8 %layer_backward.2 = (f32[256,1536]{1,0:T(8,128)}, bf16[2048,768]{1,0:T(8,128)(2,1)}, bf16[2048,384]{1,0:T(8,128)(2,1)}, bf16[2048,384]{1,0:T(8,128)(2,1)}, f32[1...) custom-call(bf16[256,1536]{1,0:T(8,128)(2,1)} %bitcast.121, f32[2,8,128]{2,1,0:T(8,128)} %broadcast_in_dim.74.refs_1_, ...), custom_call_target="tpu_custom_call" | custom-call | flops 12809404416 | bytes 23592960 | tf_op jit(solution)/shard_map/layer_backward/pallas_call | solution.py:946
  384.1 7.1 convolution_convert_fusion.1
  391.2 3.4 fusion.54
  394.6 3.4 fusion.51
  398.0 1.8 fusion.48
  399.8 1.8 fusion.45
  401.7 1.8 pad_maximum_fusion.refs_16_
  405.1 1.6 fusion.7
  407.3 98.9 %layer_backward.3 = (f32[256,1536]{1,0:T(8,128)}, bf16[2048,768]{1,0:T(8,128)(2,1)}, bf16[2048,384]{1,0:T(8,128)(2,1)}, bf16[2048,384]{1,0:T(8,128)(2,1)}, f32[1...) custom-call(bf16[256,1536]{1,0:T(8,128)(2,1)} %get-tuple-element.112.ref, ...), custom_call_target="tpu_custom_call" | custom-call | flops 12809404416 | bytes 23592960 | tf_op jit(solution)/shard_map/layer_backward/pallas_call | solution.py:946
  506.2 2.1 fusion.19
  508.3 3.8 select_convert_fusion
  513.5 0.6 pad_maximum_fusion.3.sm_ref
  514.1 6.9 convolution_convert_fusion.late_ref
  521.0 175.3 %finish.1 = (bf16[6448,384]{1,0:T(8,128)(2,1)}, bf16[2,384,1536]{2,1,0:T(8,128)(2,1)}, bf16[8,16,640]{2,1,0:T(8,128)(2,1)}, f32[8,512]{1,0:T(8,128)}, bf16[2,128,1536]{2,1,0:T(8,128)(2,1)}) custom-call(bf16[2048,1536]{1,0:T(8,128)(2,1)} %get-tuple-element.79.full_ref, bf16[2048,768]{1,0:T(8,128)(2,1)} %get-tuple-element.80.gp_ref, ...), custom_call_target="tpu_custom_call" | custom-call | flops 9663676416 | bytes 17301504 | tf_op jit(solution)/shard_map/finish/pallas_call | solution.py:1437
  696.4 0.9 convert_element_type.107
  697.3 0.8 slice.176
  698.1 0.7 fusion.62
  698.8 0.7 fusion.59
  699.5 6.9 convert_bitcast_fusion
  707.2 4.6 bitcast_convert_fusion
  711.9 1.2 copy-done.5
  713.1 2.1 fusion
  717.0 0.8 slice.185
  (150 shorter events, 11.4 us)
Async XLA Ops:
  3.4 2.4 copy-start.10
  5.8 3.8 copy-start.18
  5.8 3.9 copy-start.19
  5.8 3.9 copy-start.20
  5.8 3.9 copy-start.21
  5.9 3.9 copy-start.22
  5.9 3.9 copy-start.23
  5.9 3.9 copy-start.24
  94.2 7.0 copy-start.12
  101.2 1.8 copy-start.4
  207.1 199.6 %copy-start.16 = (f32[2,8,256]{2,1,0:T(8,128)}, f32[2,8,256]{2,1,0:T(8,128)S(1)}, u32[]{:S(2)}) copy-start(f32[2,8,256]{2,1,0:T(8,128)S(1)} %add_rsqrt_fusion.1.refs_2_) | copy-start | bytes 49156
  211.3 79.7 %copy-start.8 = (bf16[2,128,1536]{2,1,0:T(8,128)(2,1)S(1)}, bf16[2,128,1536]{2,1,0:T(8,128)(2,1)}, u32[]{:S(2)}) copy-start(bf16[2,128,1536]{2,1,0:T(8,128)(2,1)} %get-tuple-element.52) | copy-start | bytes 2359300
  290.2 2.1 copy-start.2
  291.0 1.5 copy-start.17
  292.3 1.0 copy-start
  384.1 7.1 copy-start.25
  391.2 6.8 slice-start
  394.6 3.4 slice-start.1
  401.6 1.8 copy-start.7
  403.4 1.1 copy-start.1
  403.4 1.7 copy-start.6
  506.2 2.1 copy-start.3
  506.2 2.1 copy-start.9
  508.3 3.8 copy-start.15
  508.3 4.1 copy-start.14
  699.5 7.0 copy-start.13
  707.2 4.6 copy-start.11
  711.7 1.4 copy-start.5
